TPU v7x, 512 devices: a whole 4x8x8 slice. The times are simulated.
512 devices in a mesh: row: 16 (over x, z_hi), col: 8 (over y), layer: 4 (over z_lo, core).
Axes of the slice: x: 4, y: 8, z: 8 (z_hi: 4, z_lo: 2; z = z_hi * 2 + z_lo), core: 2. Of those that a mesh axis runs over, the one named last changes fastest.
Arguments:
- a_values: float32 [16, 8, 4, 2, 8, 64, 64], P('row', 'col', 'layer'), may hold values from -6 to 6
- a_places: int32 [16, 8, 4, 2, 8, 2], P('row', 'col', 'layer'), may hold values from 0 to 7, as said below
- a_counts: int32 [16, 8, 4, 2], P('row', 'col', 'layer'), may hold values from 2 to 8, as said below
- b_values: float32 [16, 8, 4, 24, 64, 64], P('row', 'col', 'layer'), may hold values from -0.1875 to 0.1875
- b_places: int32 [16, 8, 4, 24, 2], P('row', 'col', 'layer'), may hold values from 0 to 15, as said below
- b_counts: int32 [16, 8, 4], P('row', 'col', 'layer'), may hold values from 6 to 24, as said below
Outputs:
- product: float32 [8192, 8192], P(('row', 'layer'), 'col')
Inputs may be any that keep to these rules, and one draw needn't show every extreme that they name: a_places[..., 0] lies below 8 and a_places[..., 1] below 2; within one tile the slots name distinct positions. b_places[..., 0] lies below 2 and b_places[..., 1] below 16; within one tile the slots name distinct positions. `a_counts`: some tile is full. `b_counts`: some tile is full.
All inputs are finite; a program needn't handle non-finite values.
Results may differ from a plain program's by a relative error of at most 0.00007.
Values sent between devices are 32-bit elements; how exact they have to be, the bound alone decides.
No kernel may reach another device: no remote copies, remote signals or barrier semaphores. Data moves between devices by JAX's collectives and lax.ppermute only.
A program may use at most 64 MiB of HBM per device.

v0:
```python
import jax
import jax.numpy as jnp
from jax import lax
from jax.sharding import PartitionSpec as P

TILE_ROWS = 8


def from_behind(block, axis, distance):
    devices = range(lax.axis_size(axis))
    route = [((i - distance) % len(devices), i) for i in devices]
    return lax.ppermute(block, axis, route)


def densify(values, places, count, rows, cols):
    slots = values.shape[0]
    width = values.shape[1]
    live = jnp.arange(slots, dtype=jnp.int32) < count
    spots = places[:, 0] * cols + places[:, 1]
    target = jnp.arange(rows * cols, dtype=jnp.int32)
    select = ((target[:, None] == spots[None, :]) & live[None, :]).astype(jnp.float32)
    flat = jnp.dot(
        select,
        values.reshape(slots, width * width),
        precision=lax.Precision.HIGHEST,
        preferred_element_type=jnp.float32,
    )
    return (
        flat.reshape(rows, cols, width, width)
        .transpose(0, 2, 1, 3)
        .reshape(rows * width, cols * width)
    )


def body(a_values, a_places, a_counts, b_values, b_places, b_counts):
    a_vals = a_values.reshape(a_values.shape[3:])
    a_pos = a_places.reshape(a_places.shape[3:])
    a_num = a_counts.reshape(a_counts.shape[3:])
    b_vals = b_values.reshape(b_values.shape[3:])
    b_pos = b_places.reshape(b_places.shape[3:])
    b_num = b_counts.reshape((1,))
    rows_grid = lax.axis_size("row")
    cols_grid = lax.axis_size("col")
    layers = lax.axis_size("layer")
    inner = TILE_ROWS // layers
    tile_cols = TILE_ROWS * rows_grid // cols_grid
    width = a_vals.shape[-1]
    my_col = lax.axis_index("col")

    def product(left_vals, left_pos, left_num, right_vals, right_pos, right_num):
        left = densify(left_vals, left_pos, left_num, TILE_ROWS, inner)
        right = densify(right_vals, right_pos, right_num, inner, tile_cols)
        return jnp.dot(
            left, right, precision=lax.Precision.HIGHEST, preferred_element_type=jnp.float32
        )

    start_sum = jnp.zeros((TILE_ROWS * width, tile_cols * width), jnp.float32)

    def advance(step, carry):
        partial_value, av, ap, an, bv, bp, bn = carry
        partial_value = partial_value + product(av[0], ap[0], an[0], bv, bp, bn[0])
        av, ap, an = from_behind((av, ap, an), "col", -1)
        last = my_col == cols_grid - 1
        av = jnp.where(last, jnp.roll(av, -1, 0), av)
        ap = jnp.where(last, jnp.roll(ap, -1, 0), ap)
        an = jnp.where(last, jnp.roll(an, -1, 0), an)
        bv, bp, bn = from_behind((bv, bp, bn), "row", -1)
        return (partial_value, av, ap, an, bv, bp, bn)

    carry = lax.fori_loop(
        0, rows_grid - 1, advance, (start_sum, a_vals, a_pos, a_num, b_vals, b_pos, b_num)
    )
    partial_value, av, ap, an, bv, bp, bn = carry
    partial_value = partial_value + product(av[0], ap[0], an[0], bv, bp, bn[0])
    return lax.psum_scatter(partial_value, "layer", scatter_dimension=0, tiled=True)


def solution(mesh):
    in_specs = (
        P("row", "col", "layer", None, None, None, None),
        P("row", "col", "layer", None, None, None),
        P("row", "col", "layer", None),
        P("row", "col", "layer", None, None, None),
        P("row", "col", "layer", None, None),
        P("row", "col", "layer"),
    )
    out_specs = P(("row", "layer"), "col")
    return jax.shard_map(body, mesh=mesh, in_specs=in_specs, out_specs=out_specs, check_vma=False)
```

profile of v0, /device:TPU:56, one launch (start us, length us, event | category | flops | bytes accessed | tf_op | source)
XLA Modules:
  0.0 828.4 jit_solution(2220266592300615370)
XLA Ops:
  12.9 760.0 %while.25 = (s32[]{:T(128)}, f32[512,1024]{1,0:T(8,128)}, f32[2,8,64,64]{3,2,1,0:T(8,128)}, s32[2,8,2]{1,2,0:T(2,128)S(1)}, s32[2]{0:T(128)}, /*index=5*/f32[24,...) while((s32[]{:T(128)}, f32[512,1024]{1,0:T(8,128)}, ...), condition=%wide.region_1.2_spmd.clone, body=%wide.region_0.1_spmd.clone.sunk | while | flops 850528256 | bytes 32247624 | solution.py:70
  23.8 13.1 %collective-permute-start.3 = (f32[24,64,64]{2,1,0:T(8,128)S(1)}, f32[24,64,64]{2,1,0:T(8,128)}, u32[]{:S(2)}, u32[]{:S(2)}) collective-permute-start(f32[24,64,64]{2,1,0:T(8,128)S(1)} %copy.52), channel_id=1, source_target_pairs={{32,0},{64,32},{96,64},{128,96},{160,128},{192,160},{224,192},{256... | collective-permute-start | bytes 1179656 | tf_op jit(solution)/shard_map/while/body/eval_jaxpr/ppermute | solution.py:12
  58.4 11.5 %collective-permute-start.5 = (s32[1]{0:T(128)}, s32[1]{0:T(128)}, u32[]{:S(2)}, u32[]{:S(2)}) collective-permute-start(s32[1]{0:T(128)} %copy.54), channel_id=1, source_target_pairs={{32,0},{64,32},{96,64},{128,96},{160,128},{192,160},{224,192},{256... | collective-permute-start | bytes 20 | tf_op jit(solution)/shard_map/while/body/eval_jaxpr/ppermute | solution.py:12
  75.2 3.4 collective-permute-start
  108.3 7.4 collective-permute-start.5
  124.4 5.4 collective-permute-start.1
  134.2 3.9 collective-permute-start.3
  159.8 5.5 collective-permute-start.5
  170.6 4.3 collective-permute-start
  181.6 4.3 collective-permute-start.3
  186.5 3.5 collective-permute-start.4
  208.3 5.0 collective-permute-start.5
  226.9 7.7 collective-permute-start.3
  255.5 10.5 %collective-permute-start.5 = (s32[1]{0:T(128)}, s32[1]{0:T(128)}, u32[]{:S(2)}, u32[]{:S(2)}) collective-permute-start(s32[1]{0:T(128)} %copy.54), channel_id=1, source_target_pairs={{32,0},{64,32},{96,64},{128,96},{160,128},{192,160},{224,192},{256... | collective-permute-start | bytes 20 | tf_op jit(solution)/shard_map/while/body/eval_jaxpr/ppermute | solution.py:12
  271.4 6.8 collective-permute-start
  280.3 4.0 collective-permute-start.2
  285.5 3.9 collective-permute-start.3
  310.3 7.0 collective-permute-start.5
  323.4 5.7 collective-permute-start
  360.3 5.2 collective-permute-start.5
  370.8 7.3 collective-permute-start
  386.1 3.4 collective-permute-start.4
  408.0 4.9 collective-permute-start.5
  421.1 3.9 collective-permute-start.1
  425.0 3.7 collective-permute-start.2
  429.9 5.2 collective-permute-start.3
  435.6 4.2 collective-permute-start.4
  458.2 5.6 collective-permute-start.5
  471.1 5.4 collective-permute-start.1
  479.8 4.3 collective-permute-start.3
  484.7 4.3 collective-permute-start.4
  507.4 5.8 collective-permute-start.5
  521.8 3.7 collective-permute-start.1
  532.8 5.1 collective-permute-start.4
  556.3 6.0 collective-permute-start.5
  567.6 4.1 collective-permute-start
  571.7 4.2 collective-permute-start.1
  579.0 9.0 %collective-permute-start.3 = (f32[24,64,64]{2,1,0:T(8,128)S(1)}, f32[24,64,64]{2,1,0:T(8,128)}, u32[]{:S(2)}, u32[]{:S(2)}) collective-permute-start(f32[24,64,64]{2,1,0:T(8,128)S(1)} %copy.52), channel_id=1, source_target_pairs={{32,0},{64,32},{96,64},{128,96},{160,128},{192,160},{224,192},{256... | collective-permute-start | bytes 1179656 | tf_op jit(solution)/shard_map/while/body/eval_jaxpr/ppermute | solution.py:12
  609.2 8.6 %collective-permute-start.5 = (s32[1]{0:T(128)}, s32[1]{0:T(128)}, u32[]{:S(2)}, u32[]{:S(2)}) collective-permute-start(s32[1]{0:T(128)} %copy.54), channel_id=1, source_target_pairs={{32,0},{64,32},{96,64},{128,96},{160,128},{192,160},{224,192},{256... | collective-permute-start | bytes 20 | tf_op jit(solution)/shard_map/while/body/eval_jaxpr/ppermute | solution.py:12
  634.0 4.3 collective-permute-start.3
  659.6 6.6 collective-permute-start.5
  680.1 4.9 collective-permute-start.3
  685.6 6.2 collective-permute-start.4
  710.2 7.5 collective-permute-start.5
  731.3 5.6 collective-permute-start.3
  737.4 6.9 collective-permute-start.4
  762.8 4.9 collective-permute-start.5
  784.2 37.4 %reduce-scatter.2.cloned.1.call-done = f32[128,1024]{1,0:T(8,128)} async-done(((f32[512,1024]{1,0:T(8,128)}), f32[128,1024]{1,0:T(8,128)}) %reduce-scatter.2.cloned.1.call-update) | async-done | bytes 524304 | tf_op jit(solution)/shard_map/reduce_scatter | solution.py:75
  (620 shorter events, 501.2 us)
Async XLA Ops:
  6.5 815.0 %reduce-scatter.2.cloned.1.call-start = ((), (), s32[]{:S(2)}) async-start(), calls=%async_computation.1 | async-start | bytes 2621440 | tf_op jit(solution)/shard_map/reduce_scatter | solution.py:75
  12.9 59.6 %collective-permute-start = (f32[2,8,64,64]{3,2,1,0:T(8,128)}, f32[2,8,64,64]{3,2,1,0:T(8,128)}, u32[]{:S(2)}, u32[]{:S(2)}) collective-permute-start(f32[2,8,64,64]{3,2,1,0:T(8,128)} %get-tuple-element.257), channel_id=1, source_target_pairs={{4,0},{8,4},{12,8},{16,12},{20,16},{24,20},{28,24},{0,28},{5,1},{9... | collective-permute-start | bytes 786440 | tf_op jit(solution)/shard_map/while/body/eval_jaxpr/ppermute | solution.py:12
  16.2 56.4 %collective-permute-start.1 = (s32[2,8,2]{1,2,0:T(2,128)S(1)}, s32[2,8,2]{1,2,0:T(2,128)S(1)}, u32[]{:S(2)}, u32[]{:S(2)}) collective-permute-start(s32[2,8,2]{1,2,0:T(2,128)S(1)} %get-tuple-element.258), channel_id=1, source_target_pairs={{4,0},{8,4},{12,8},{16,12},{20,16},{24,20},{28,24},{0,28},{5,1},{9... | collective-permute-start | bytes 392 | tf_op jit(solution)/shard_map/while/body/eval_jaxpr/ppermute | solution.py:12
  19.4 38.9 %collective-permute-start.2 = (s32[2]{0:T(128)}, s32[2]{0:T(128)S(1)}, u32[]{:S(2)}, u32[]{:S(2)}) collective-permute-start(s32[2]{0:T(128)} %get-tuple-element.259), channel_id=1, source_target_pairs={{4,0},{8,4},{12,8},{16,12},{20,16},{24,20},{28,24},{0,28},{5,1},{9... | collective-permute-start | bytes 32 | tf_op jit(solution)/shard_map/while/body/eval_jaxpr/ppermute | solution.py:12
  23.8 50.7 %collective-permute-start.3 = (f32[24,64,64]{2,1,0:T(8,128)S(1)}, f32[24,64,64]{2,1,0:T(8,128)}, u32[]{:S(2)}, u32[]{:S(2)}) collective-permute-start(f32[24,64,64]{2,1,0:T(8,128)S(1)} %copy.52), channel_id=1, source_target_pairs={{32,0},{64,32},{96,64},{128,96},{160,128},{192,160},{224,192},{256... | collective-permute-start | bytes 1179656 | tf_op jit(solution)/shard_map/while/body/eval_jaxpr/ppermute | solution.py:12
  37.5 37.0 %collective-permute-start.4 = (s32[24,2]{0,1:T(2,128)}, s32[24,2]{0,1:T(2,128)S(1)}, u32[]{:S(2)}, u32[]{:S(2)}) collective-permute-start(s32[24,2]{0,1:T(2,128)} %copy.53), channel_id=1, source_target_pairs={{32,0},{64,32},{96,64},{128,96},{160,128},{192,160},{224,192},{256... | collective-permute-start | bytes 584 | tf_op jit(solution)/shard_map/while/body/eval_jaxpr/ppermute | solution.py:12
  75.2 43.2 %collective-permute-start = (f32[2,8,64,64]{3,2,1,0:T(8,128)}, f32[2,8,64,64]{3,2,1,0:T(8,128)}, u32[]{:S(2)}, u32[]{:S(2)}) collective-permute-start(f32[2,8,64,64]{3,2,1,0:T(8,128)} %get-tuple-element.257), channel_id=1, source_target_pairs={{4,0},{8,4},{12,8},{16,12},{20,16},{24,20},{28,24},{0,28},{5,1},{9... | collective-permute-start | bytes 786440 | tf_op jit(solution)/shard_map/while/body/eval_jaxpr/ppermute | solution.py:12
  78.6 39.8 %collective-permute-start.1 = (s32[2,8,2]{1,2,0:T(2,128)S(1)}, s32[2,8,2]{1,2,0:T(2,128)S(1)}, u32[]{:S(2)}, u32[]{:S(2)}) collective-permute-start(s32[2,8,2]{1,2,0:T(2,128)S(1)} %get-tuple-element.258), channel_id=1, source_target_pairs={{4,0},{8,4},{12,8},{16,12},{20,16},{24,20},{28,24},{0,28},{5,1},{9... | collective-permute-start | bytes 392 | tf_op jit(solution)/shard_map/while/body/eval_jaxpr/ppermute | solution.py:12
  84.4 35.9 %collective-permute-start.3 = (f32[24,64,64]{2,1,0:T(8,128)S(1)}, f32[24,64,64]{2,1,0:T(8,128)}, u32[]{:S(2)}, u32[]{:S(2)}) collective-permute-start(f32[24,64,64]{2,1,0:T(8,128)S(1)} %copy.52), channel_id=1, source_target_pairs={{32,0},{64,32},{96,64},{128,96},{160,128},{192,160},{224,192},{256... | collective-permute-start | bytes 1179656 | tf_op jit(solution)/shard_map/while/body/eval_jaxpr/ppermute | solution.py:12
  121.0 46.9 %collective-permute-start = (f32[2,8,64,64]{3,2,1,0:T(8,128)}, f32[2,8,64,64]{3,2,1,0:T(8,128)}, u32[]{:S(2)}, u32[]{:S(2)}) collective-permute-start(f32[2,8,64,64]{3,2,1,0:T(8,128)} %get-tuple-element.257), channel_id=1, source_target_pairs={{4,0},{8,4},{12,8},{16,12},{20,16},{24,20},{28,24},{0,28},{5,1},{9... | collective-permute-start | bytes 786440 | tf_op jit(solution)/shard_map/while/body/eval_jaxpr/ppermute | solution.py:12
  124.4 43.5 %collective-permute-start.1 = (s32[2,8,2]{1,2,0:T(2,128)S(1)}, s32[2,8,2]{1,2,0:T(2,128)S(1)}, u32[]{:S(2)}, u32[]{:S(2)}) collective-permute-start(s32[2,8,2]{1,2,0:T(2,128)S(1)} %get-tuple-element.258), channel_id=1, source_target_pairs={{4,0},{8,4},{12,8},{16,12},{20,16},{24,20},{28,24},{0,28},{5,1},{9... | collective-permute-start | bytes 392 | tf_op jit(solution)/shard_map/while/body/eval_jaxpr/ppermute | solution.py:12
  134.2 35.7 %collective-permute-start.3 = (f32[24,64,64]{2,1,0:T(8,128)S(1)}, f32[24,64,64]{2,1,0:T(8,128)}, u32[]{:S(2)}, u32[]{:S(2)}) collective-permute-start(f32[24,64,64]{2,1,0:T(8,128)S(1)} %copy.52), channel_id=1, source_target_pairs={{32,0},{64,32},{96,64},{128,96},{160,128},{192,160},{224,192},{256... | collective-permute-start | bytes 1179656 | tf_op jit(solution)/shard_map/while/body/eval_jaxpr/ppermute | solution.py:12
  170.6 45.5 %collective-permute-start = (f32[2,8,64,64]{3,2,1,0:T(8,128)}, f32[2,8,64,64]{3,2,1,0:T(8,128)}, u32[]{:S(2)}, u32[]{:S(2)}) collective-permute-start(f32[2,8,64,64]{3,2,1,0:T(8,128)} %get-tuple-element.257), channel_id=1, source_target_pairs={{4,0},{8,4},{12,8},{16,12},{20,16},{24,20},{28,24},{0,28},{5,1},{9... | collective-permute-start | bytes 786440 | tf_op jit(solution)/shard_map/while/body/eval_jaxpr/ppermute | solution.py:12
  174.9 41.2 %collective-permute-start.1 = (s32[2,8,2]{1,2,0:T(2,128)S(1)}, s32[2,8,2]{1,2,0:T(2,128)S(1)}, u32[]{:S(2)}, u32[]{:S(2)}) collective-permute-start(s32[2,8,2]{1,2,0:T(2,128)S(1)} %get-tuple-element.258), channel_id=1, source_target_pairs={{4,0},{8,4},{12,8},{16,12},{20,16},{24,20},{28,24},{0,28},{5,1},{9... | collective-permute-start | bytes 392 | tf_op jit(solution)/shard_map/while/body/eval_jaxpr/ppermute | solution.py:12
  181.6 36.4 %collective-permute-start.3 = (f32[24,64,64]{2,1,0:T(8,128)S(1)}, f32[24,64,64]{2,1,0:T(8,128)}, u32[]{:S(2)}, u32[]{:S(2)}) collective-permute-start(f32[24,64,64]{2,1,0:T(8,128)S(1)} %copy.52), channel_id=1, source_target_pairs={{32,0},{64,32},{96,64},{128,96},{160,128},{192,160},{224,192},{256... | collective-permute-start | bytes 1179656 | tf_op jit(solution)/shard_map/while/body/eval_jaxpr/ppermute | solution.py:12
  218.7 50.1 %collective-permute-start = (f32[2,8,64,64]{3,2,1,0:T(8,128)}, f32[2,8,64,64]{3,2,1,0:T(8,128)}, u32[]{:S(2)}, u32[]{:S(2)}) collective-permute-start(f32[2,8,64,64]{3,2,1,0:T(8,128)} %get-tuple-element.257), channel_id=1, source_target_pairs={{4,0},{8,4},{12,8},{16,12},{20,16},{24,20},{28,24},{0,28},{5,1},{9... | collective-permute-start | bytes 786440 | tf_op jit(solution)/shard_map/while/body/eval_jaxpr/ppermute | solution.py:12
  221.2 47.5 %collective-permute-start.1 = (s32[2,8,2]{1,2,0:T(2,128)S(1)}, s32[2,8,2]{1,2,0:T(2,128)S(1)}, u32[]{:S(2)}, u32[]{:S(2)}) collective-permute-start(s32[2,8,2]{1,2,0:T(2,128)S(1)} %get-tuple-element.258), channel_id=1, source_target_pairs={{4,0},{8,4},{12,8},{16,12},{20,16},{24,20},{28,24},{0,28},{5,1},{9... | collective-permute-start | bytes 392 | tf_op jit(solution)/shard_map/while/body/eval_jaxpr/ppermute | solution.py:12
  226.9 43.8 %collective-permute-start.3 = (f32[24,64,64]{2,1,0:T(8,128)S(1)}, f32[24,64,64]{2,1,0:T(8,128)}, u32[]{:S(2)}, u32[]{:S(2)}) collective-permute-start(f32[24,64,64]{2,1,0:T(8,128)S(1)} %copy.52), channel_id=1, source_target_pairs={{32,0},{64,32},{96,64},{128,96},{160,128},{192,160},{224,192},{256... | collective-permute-start | bytes 1179656 | tf_op jit(solution)/shard_map/while/body/eval_jaxpr/ppermute | solution.py:12
  235.2 35.5 %collective-permute-start.4 = (s32[24,2]{0,1:T(2,128)}, s32[24,2]{0,1:T(2,128)S(1)}, u32[]{:S(2)}, u32[]{:S(2)}) collective-permute-start(s32[24,2]{0,1:T(2,128)} %copy.53), channel_id=1, source_target_pairs={{32,0},{64,32},{96,64},{128,96},{160,128},{192,160},{224,192},{256... | collective-permute-start | bytes 584 | tf_op jit(solution)/shard_map/while/body/eval_jaxpr/ppermute | solution.py:12
  271.4 48.6 %collective-permute-start = (f32[2,8,64,64]{3,2,1,0:T(8,128)}, f32[2,8,64,64]{3,2,1,0:T(8,128)}, u32[]{:S(2)}, u32[]{:S(2)}) collective-permute-start(f32[2,8,64,64]{3,2,1,0:T(8,128)} %get-tuple-element.257), channel_id=1, source_target_pairs={{4,0},{8,4},{12,8},{16,12},{20,16},{24,20},{28,24},{0,28},{5,1},{9... | collective-permute-start | bytes 786440 | tf_op jit(solution)/shard_map/while/body/eval_jaxpr/ppermute | solution.py:12
  278.1 41.8 %collective-permute-start.1 = (s32[2,8,2]{1,2,0:T(2,128)S(1)}, s32[2,8,2]{1,2,0:T(2,128)S(1)}, u32[]{:S(2)}, u32[]{:S(2)}) collective-permute-start(s32[2,8,2]{1,2,0:T(2,128)S(1)} %get-tuple-element.258), channel_id=1, source_target_pairs={{4,0},{8,4},{12,8},{16,12},{20,16},{24,20},{28,24},{0,28},{5,1},{9... | collective-permute-start | bytes 392 | tf_op jit(solution)/shard_map/while/body/eval_jaxpr/ppermute | solution.py:12
  285.5 37.2 %collective-permute-start.3 = (f32[24,64,64]{2,1,0:T(8,128)S(1)}, f32[24,64,64]{2,1,0:T(8,128)}, u32[]{:S(2)}, u32[]{:S(2)}) collective-permute-start(f32[24,64,64]{2,1,0:T(8,128)S(1)} %copy.52), channel_id=1, source_target_pairs={{32,0},{64,32},{96,64},{128,96},{160,128},{192,160},{224,192},{256... | collective-permute-start | bytes 1179656 | tf_op jit(solution)/shard_map/while/body/eval_jaxpr/ppermute | solution.py:12
  323.4 44.8 %collective-permute-start = (f32[2,8,64,64]{3,2,1,0:T(8,128)}, f32[2,8,64,64]{3,2,1,0:T(8,128)}, u32[]{:S(2)}, u32[]{:S(2)}) collective-permute-start(f32[2,8,64,64]{3,2,1,0:T(8,128)} %get-tuple-element.257), channel_id=1, source_target_pairs={{4,0},{8,4},{12,8},{16,12},{20,16},{24,20},{28,24},{0,28},{5,1},{9... | collective-permute-start | bytes 786440 | tf_op jit(solution)/shard_map/while/body/eval_jaxpr/ppermute | solution.py:12
  329.1 39.0 %collective-permute-start.1 = (s32[2,8,2]{1,2,0:T(2,128)S(1)}, s32[2,8,2]{1,2,0:T(2,128)S(1)}, u32[]{:S(2)}, u32[]{:S(2)}) collective-permute-start(s32[2,8,2]{1,2,0:T(2,128)S(1)} %get-tuple-element.258), channel_id=1, source_target_pairs={{4,0},{8,4},{12,8},{16,12},{20,16},{24,20},{28,24},{0,28},{5,1},{9... | collective-permute-start | bytes 392 | tf_op jit(solution)/shard_map/while/body/eval_jaxpr/ppermute | solution.py:12
  370.8 44.8 %collective-permute-start = (f32[2,8,64,64]{3,2,1,0:T(8,128)}, f32[2,8,64,64]{3,2,1,0:T(8,128)}, u32[]{:S(2)}, u32[]{:S(2)}) collective-permute-start(f32[2,8,64,64]{3,2,1,0:T(8,128)} %get-tuple-element.257), channel_id=1, source_target_pairs={{4,0},{8,4},{12,8},{16,12},{20,16},{24,20},{28,24},{0,28},{5,1},{9... | collective-permute-start | bytes 786440 | tf_op jit(solution)/shard_map/while/body/eval_jaxpr/ppermute | solution.py:12
  378.0 37.5 %collective-permute-start.1 = (s32[2,8,2]{1,2,0:T(2,128)S(1)}, s32[2,8,2]{1,2,0:T(2,128)S(1)}, u32[]{:S(2)}, u32[]{:S(2)}) collective-permute-start(s32[2,8,2]{1,2,0:T(2,128)S(1)} %get-tuple-element.258), channel_id=1, source_target_pairs={{4,0},{8,4},{12,8},{16,12},{20,16},{24,20},{28,24},{0,28},{5,1},{9... | collective-permute-start | bytes 392 | tf_op jit(solution)/shard_map/while/body/eval_jaxpr/ppermute | solution.py:12
  418.2 48.3 %collective-permute-start = (f32[2,8,64,64]{3,2,1,0:T(8,128)}, f32[2,8,64,64]{3,2,1,0:T(8,128)}, u32[]{:S(2)}, u32[]{:S(2)}) collective-permute-start(f32[2,8,64,64]{3,2,1,0:T(8,128)} %get-tuple-element.257), channel_id=1, source_target_pairs={{4,0},{8,4},{12,8},{16,12},{20,16},{24,20},{28,24},{0,28},{5,1},{9... | collective-permute-start | bytes 786440 | tf_op jit(solution)/shard_map/while/body/eval_jaxpr/ppermute | solution.py:12
  421.1 45.3 %collective-permute-start.1 = (s32[2,8,2]{1,2,0:T(2,128)S(1)}, s32[2,8,2]{1,2,0:T(2,128)S(1)}, u32[]{:S(2)}, u32[]{:S(2)}) collective-permute-start(s32[2,8,2]{1,2,0:T(2,128)S(1)} %get-tuple-element.258), channel_id=1, source_target_pairs={{4,0},{8,4},{12,8},{16,12},{20,16},{24,20},{28,24},{0,28},{5,1},{9... | collective-permute-start | bytes 392 | tf_op jit(solution)/shard_map/while/body/eval_jaxpr/ppermute | solution.py:12
  429.9 38.6 %collective-permute-start.3 = (f32[24,64,64]{2,1,0:T(8,128)S(1)}, f32[24,64,64]{2,1,0:T(8,128)}, u32[]{:S(2)}, u32[]{:S(2)}) collective-permute-start(f32[24,64,64]{2,1,0:T(8,128)S(1)} %copy.52), channel_id=1, source_target_pairs={{32,0},{64,32},{96,64},{128,96},{160,128},{192,160},{224,192},{256... | collective-permute-start | bytes 1179656 | tf_op jit(solution)/shard_map/while/body/eval_jaxpr/ppermute | solution.py:12
  469.1 46.8 %collective-permute-start = (f32[2,8,64,64]{3,2,1,0:T(8,128)}, f32[2,8,64,64]{3,2,1,0:T(8,128)}, u32[]{:S(2)}, u32[]{:S(2)}) collective-permute-start(f32[2,8,64,64]{3,2,1,0:T(8,128)} %get-tuple-element.257), channel_id=1, source_target_pairs={{4,0},{8,4},{12,8},{16,12},{20,16},{24,20},{28,24},{0,28},{5,1},{9... | collective-permute-start | bytes 786440 | tf_op jit(solution)/shard_map/while/body/eval_jaxpr/ppermute | solution.py:12
  471.1 44.8 %collective-permute-start.1 = (s32[2,8,2]{1,2,0:T(2,128)S(1)}, s32[2,8,2]{1,2,0:T(2,128)S(1)}, u32[]{:S(2)}, u32[]{:S(2)}) collective-permute-start(s32[2,8,2]{1,2,0:T(2,128)S(1)} %get-tuple-element.258), channel_id=1, source_target_pairs={{4,0},{8,4},{12,8},{16,12},{20,16},{24,20},{28,24},{0,28},{5,1},{9... | collective-permute-start | bytes 392 | tf_op jit(solution)/shard_map/while/body/eval_jaxpr/ppermute | solution.py:12
  479.8 39.1 %collective-permute-start.3 = (f32[24,64,64]{2,1,0:T(8,128)S(1)}, f32[24,64,64]{2,1,0:T(8,128)}, u32[]{:S(2)}, u32[]{:S(2)}) collective-permute-start(f32[24,64,64]{2,1,0:T(8,128)S(1)} %copy.52), channel_id=1, source_target_pairs={{32,0},{64,32},{96,64},{128,96},{160,128},{192,160},{224,192},{256... | collective-permute-start | bytes 1179656 | tf_op jit(solution)/shard_map/while/body/eval_jaxpr/ppermute | solution.py:12
  519.6 45.4 %collective-permute-start = (f32[2,8,64,64]{3,2,1,0:T(8,128)}, f32[2,8,64,64]{3,2,1,0:T(8,128)}, u32[]{:S(2)}, u32[]{:S(2)}) collective-permute-start(f32[2,8,64,64]{3,2,1,0:T(8,128)} %get-tuple-element.257), channel_id=1, source_target_pairs={{4,0},{8,4},{12,8},{16,12},{20,16},{24,20},{28,24},{0,28},{5,1},{9... | collective-permute-start | bytes 786440 | tf_op jit(solution)/shard_map/while/body/eval_jaxpr/ppermute | solution.py:12
  521.8 43.1 %collective-permute-start.1 = (s32[2,8,2]{1,2,0:T(2,128)S(1)}, s32[2,8,2]{1,2,0:T(2,128)S(1)}, u32[]{:S(2)}, u32[]{:S(2)}) collective-permute-start(s32[2,8,2]{1,2,0:T(2,128)S(1)} %get-tuple-element.258), channel_id=1, source_target_pairs={{4,0},{8,4},{12,8},{16,12},{20,16},{24,20},{28,24},{0,28},{5,1},{9... | collective-permute-start | bytes 392 | tf_op jit(solution)/shard_map/while/body/eval_jaxpr/ppermute | solution.py:12
  528.8 38.1 %collective-permute-start.3 = (f32[24,64,64]{2,1,0:T(8,128)S(1)}, f32[24,64,64]{2,1,0:T(8,128)}, u32[]{:S(2)}, u32[]{:S(2)}) collective-permute-start(f32[24,64,64]{2,1,0:T(8,128)S(1)} %copy.52), channel_id=1, source_target_pairs={{32,0},{64,32},{96,64},{128,96},{160,128},{192,160},{224,192},{256... | collective-permute-start | bytes 1179656 | tf_op jit(solution)/shard_map/while/body/eval_jaxpr/ppermute | solution.py:12
  567.6 53.0 %collective-permute-start = (f32[2,8,64,64]{3,2,1,0:T(8,128)}, f32[2,8,64,64]{3,2,1,0:T(8,128)}, u32[]{:S(2)}, u32[]{:S(2)}) collective-permute-start(f32[2,8,64,64]{3,2,1,0:T(8,128)} %get-tuple-element.257), channel_id=1, source_target_pairs={{4,0},{8,4},{12,8},{16,12},{20,16},{24,20},{28,24},{0,28},{5,1},{9... | collective-permute-start | bytes 786440 | tf_op jit(solution)/shard_map/while/body/eval_jaxpr/ppermute | solution.py:12
  571.7 48.8 %collective-permute-start.1 = (s32[2,8,2]{1,2,0:T(2,128)S(1)}, s32[2,8,2]{1,2,0:T(2,128)S(1)}, u32[]{:S(2)}, u32[]{:S(2)}) collective-permute-start(s32[2,8,2]{1,2,0:T(2,128)S(1)} %get-tuple-element.258), channel_id=1, source_target_pairs={{4,0},{8,4},{12,8},{16,12},{20,16},{24,20},{28,24},{0,28},{5,1},{9... | collective-permute-start | bytes 392 | tf_op jit(solution)/shard_map/while/body/eval_jaxpr/ppermute | solution.py:12
  579.0 43.5 %collective-permute-start.3 = (f32[24,64,64]{2,1,0:T(8,128)S(1)}, f32[24,64,64]{2,1,0:T(8,128)}, u32[]{:S(2)}, u32[]{:S(2)}) collective-permute-start(f32[24,64,64]{2,1,0:T(8,128)S(1)} %copy.52), channel_id=1, source_target_pairs={{32,0},{64,32},{96,64},{128,96},{160,128},{192,160},{224,192},{256... | collective-permute-start | bytes 1179656 | tf_op jit(solution)/shard_map/while/body/eval_jaxpr/ppermute | solution.py:12
  623.2 45.7 %collective-permute-start = (f32[2,8,64,64]{3,2,1,0:T(8,128)}, f32[2,8,64,64]{3,2,1,0:T(8,128)}, u32[]{:S(2)}, u32[]{:S(2)}) collective-permute-start(f32[2,8,64,64]{3,2,1,0:T(8,128)} %get-tuple-element.257), channel_id=1, source_target_pairs={{4,0},{8,4},{12,8},{16,12},{20,16},{24,20},{28,24},{0,28},{5,1},{9... | collective-permute-start | bytes 786440 | tf_op jit(solution)/shard_map/while/body/eval_jaxpr/ppermute | solution.py:12
  626.5 42.4 %collective-permute-start.1 = (s32[2,8,2]{1,2,0:T(2,128)S(1)}, s32[2,8,2]{1,2,0:T(2,128)S(1)}, u32[]{:S(2)}, u32[]{:S(2)}) collective-permute-start(s32[2,8,2]{1,2,0:T(2,128)S(1)} %get-tuple-element.258), channel_id=1, source_target_pairs={{4,0},{8,4},{12,8},{16,12},{20,16},{24,20},{28,24},{0,28},{5,1},{9... | collective-permute-start | bytes 392 | tf_op jit(solution)/shard_map/while/body/eval_jaxpr/ppermute | solution.py:12
  634.0 36.8 %collective-permute-start.3 = (f32[24,64,64]{2,1,0:T(8,128)S(1)}, f32[24,64,64]{2,1,0:T(8,128)}, u32[]{:S(2)}, u32[]{:S(2)}) collective-permute-start(f32[24,64,64]{2,1,0:T(8,128)S(1)} %copy.52), channel_id=1, source_target_pairs={{32,0},{64,32},{96,64},{128,96},{160,128},{192,160},{224,192},{256... | collective-permute-start | bytes 1179656 | tf_op jit(solution)/shard_map/while/body/eval_jaxpr/ppermute | solution.py:12
  671.5 48.9 %collective-permute-start = (f32[2,8,64,64]{3,2,1,0:T(8,128)}, f32[2,8,64,64]{3,2,1,0:T(8,128)}, u32[]{:S(2)}, u32[]{:S(2)}) collective-permute-start(f32[2,8,64,64]{3,2,1,0:T(8,128)} %get-tuple-element.257), channel_id=1, source_target_pairs={{4,0},{8,4},{12,8},{16,12},{20,16},{24,20},{28,24},{0,28},{5,1},{9... | collective-permute-start | bytes 786440 | tf_op jit(solution)/shard_map/while/body/eval_jaxpr/ppermute | solution.py:12
  674.7 45.7 %collective-permute-start.1 = (s32[2,8,2]{1,2,0:T(2,128)S(1)}, s32[2,8,2]{1,2,0:T(2,128)S(1)}, u32[]{:S(2)}, u32[]{:S(2)}) collective-permute-start(s32[2,8,2]{1,2,0:T(2,128)S(1)} %get-tuple-element.258), channel_id=1, source_target_pairs={{4,0},{8,4},{12,8},{16,12},{20,16},{24,20},{28,24},{0,28},{5,1},{9... | collective-permute-start | bytes 392 | tf_op jit(solution)/shard_map/while/body/eval_jaxpr/ppermute | solution.py:12
  680.1 42.3 %collective-permute-start.3 = (f32[24,64,64]{2,1,0:T(8,128)S(1)}, f32[24,64,64]{2,1,0:T(8,128)}, u32[]{:S(2)}, u32[]{:S(2)}) collective-permute-start(f32[24,64,64]{2,1,0:T(8,128)S(1)} %copy.52), channel_id=1, source_target_pairs={{32,0},{64,32},{96,64},{128,96},{160,128},{192,160},{224,192},{256... | collective-permute-start | bytes 1179656 | tf_op jit(solution)/shard_map/while/body/eval_jaxpr/ppermute | solution.py:12
  685.6 36.8 %collective-permute-start.4 = (s32[24,2]{0,1:T(2,128)}, s32[24,2]{0,1:T(2,128)S(1)}, u32[]{:S(2)}, u32[]{:S(2)}) collective-permute-start(s32[24,2]{0,1:T(2,128)} %copy.53), channel_id=1, source_target_pairs={{32,0},{64,32},{96,64},{128,96},{160,128},{192,160},{224,192},{256... | collective-permute-start | bytes 584 | tf_op jit(solution)/shard_map/while/body/eval_jaxpr/ppermute | solution.py:12
  723.0 47.3 %collective-permute-start = (f32[2,8,64,64]{3,2,1,0:T(8,128)}, f32[2,8,64,64]{3,2,1,0:T(8,128)}, u32[]{:S(2)}, u32[]{:S(2)}) collective-permute-start(f32[2,8,64,64]{3,2,1,0:T(8,128)} %get-tuple-element.257), channel_id=1, source_target_pairs={{4,0},{8,4},{12,8},{16,12},{20,16},{24,20},{28,24},{0,28},{5,1},{9... | collective-permute-start | bytes 786440 | tf_op jit(solution)/shard_map/while/body/eval_jaxpr/ppermute | solution.py:12
  726.3 44.0 %collective-permute-start.1 = (s32[2,8,2]{1,2,0:T(2,128)S(1)}, s32[2,8,2]{1,2,0:T(2,128)S(1)}, u32[]{:S(2)}, u32[]{:S(2)}) collective-permute-start(s32[2,8,2]{1,2,0:T(2,128)S(1)} %get-tuple-element.258), channel_id=1, source_target_pairs={{4,0},{8,4},{12,8},{16,12},{20,16},{24,20},{28,24},{0,28},{5,1},{9... | collective-permute-start | bytes 392 | tf_op jit(solution)/shard_map/while/body/eval_jaxpr/ppermute | solution.py:12
  731.3 41.0 %collective-permute-start.3 = (f32[24,64,64]{2,1,0:T(8,128)S(1)}, f32[24,64,64]{2,1,0:T(8,128)}, u32[]{:S(2)}, u32[]{:S(2)}) collective-permute-start(f32[24,64,64]{2,1,0:T(8,128)S(1)} %copy.52), channel_id=1, source_target_pairs={{32,0},{64,32},{96,64},{128,96},{160,128},{192,160},{224,192},{256... | collective-permute-start | bytes 1179656 | tf_op jit(solution)/shard_map/while/body/eval_jaxpr/ppermute | solution.py:12
  (79 other events, 1413.0 us)
Sparse Core Ops, SparseCore 0:
  784.3 37.2 reduce-scatter.1
where the time goes:
time: 839 us; the launch traced here: 828 us
  starting transfers between devices  377 us (45%)
  local copies, waits for them, and re-layouts  198 us (24%)
  matrix products  103 us (12%)
  other arithmetic  85.9 us (10%)
  waiting for transfers between devices  39.5 us (5%)
  between operations  14.2 us (2%)
  loops' own time  11.8 us (1%)
    ppermute x90, starting transfers between devices, from_behind(): return lax.ppermute(block, axis, route)  377 us
    dot_general x32, matrix products, densify(): jnp.dot(select, values.reshape(slots, width * width), precision=lax.Preci...  51.4 us
    dot_general x16, matrix products, product(): jnp.dot(left, right, precision=lax.Precision.HIGHEST, preferred_element_t...  51.2 us
    reduce_scatter x1, waiting for transfers between devices, body(): lax.psum_scatter(partial_value, 'layer', scatter_dimension=0, tiled=True)  37.4 us
    reshape x32, local copies, waits for them, and re-layouts, densify(): return flat.reshape(rows, cols, width, width).transpose(0, 2, 1, 3).resha...  34.7 us
    transpose x16, local copies, waits for them, and re-layouts, densify(): return flat.reshape(rows, cols, width, width).transpose(0, 2, 1, 3).resha...  31.5 us
    select_n x15, other arithmetic, advance(): an = jnp.where(last, jnp.roll(an, -1, 0), an)  30.3 us
    while x90, local copies, waits for them, and re-layouts  25.3 us
  transfers between devices with their start and end apart: 91, of which 3 were waited for; matrix products, arithmetic and copies ran while one was open for 45% of the time, Pallas kernels for 0%

commit v1 on v0

v1 whole, which is shorter than its diff:
```python
import jax
import jax.numpy as jnp
from jax import lax
from jax.experimental import pallas as pl
from jax.experimental.pallas import tpu as pltpu
from jax.sharding import Mesh, PartitionSpec as P

BLOCK = 64
LANES = 128
CAP_A = 8
CAP_B = 24
ROWS_A = 8
INNER = 2
COLS_B = 16
PIECES = 16
B_DATA = CAP_B // 2 * BLOCK
B_ROWS = B_DATA + 8
HALF = B_ROWS // 16 * 8
A_DATA = CAP_A * BLOCK
A_ROWS = A_DATA + 8
WHERE = pl.BlockSpec(memory_space=pl.ANY)
IN_VMEM = pl.BlockSpec(memory_space=pltpu.VMEM)
IN_HBM = pl.BlockSpec(memory_space=pltpu.HBM)
IN_SMEM = pl.BlockSpec(memory_space=pltpu.SMEM)


def around(array, axis, distance):
    n = lax.axis_size(axis)
    return lax.ppermute(array, axis, [(i, (i + distance) % n) for i in range(n)])


def slot_at(places, count, cols, base):
    slots = places.shape[1]
    spot = places[0:1, :] * cols + places[1:2, :] + base
    position = lax.broadcasted_iota(jnp.int32, (LANES, slots), 0)
    slot = lax.broadcasted_iota(jnp.int32, (LANES, slots), 1)
    hit = (position == spot) & (slot < count)
    return jnp.max(jnp.where(hit, slot + 1, 0), axis=1, keepdims=True)


def as_rows(column):
    return jnp.transpose(jnp.broadcast_to(column.astype(jnp.float32), (LANES, LANES)))[0:8, :]


def pack_kernel(*refs):
    ins, (a_ref, b_ref), held, sems = refs[:6], refs[6:8], refs[8:14], refs[14]
    an_ref, bn_ref, ap_ref, bp_ref, bv_ref, av_ref = held
    copies = [pltpu.make_async_copy(ins[k], held[k], sems.at[k]) for k in range(6)]
    for copy in copies:
        copy.start()
    for copy in copies[:4]:
        copy.wait()
    copy_b, copy_a = copies[4:]
    spots = slot_at(ap_ref[0], an_ref[0], INNER, 0) + slot_at(ap_ref[1], an_ref[1], INNER, 16) - 1
    a_ref[A_DATA:, :] = as_rows(spots)
    spots = slot_at(bp_ref[...], bn_ref[0], COLS_B, 0) - 1
    b_ref[B_DATA:, :] = as_rows(spots)
    copy_b.wait()
    for pair in range(CAP_B // 2):
        b_ref[pair * BLOCK : (pair + 1) * BLOCK, :] = jnp.concatenate(
            [bv_ref[2 * pair], bv_ref[2 * pair + 1]], axis=1
        )
    copy_a.wait()
    for pair in range(CAP_A):
        a_ref[pair * BLOCK : (pair + 1) * BLOCK, :] = jnp.concatenate(
            [av_ref[2 * pair], av_ref[2 * pair + 1]], axis=1
        )


def pack(an, bn, ap, bp, bv, av):
    return pl.pallas_call(
        pack_kernel,
        out_shape=(
            jax.ShapeDtypeStruct((A_ROWS, LANES), jnp.float32),
            jax.ShapeDtypeStruct((B_ROWS, LANES), jnp.float32),
        ),
        in_specs=[IN_HBM] * 6,
        out_specs=(IN_VMEM, IN_VMEM),
        scratch_shapes=[
            pltpu.SMEM(an.shape, jnp.int32),
            pltpu.SMEM(bn.shape, jnp.int32),
            pltpu.VMEM(ap.shape, jnp.int32),
            pltpu.VMEM(bp.shape, jnp.int32),
            pltpu.VMEM(bv.shape, jnp.float32),
            pltpu.VMEM(av.shape, jnp.float32),
            pltpu.SemaphoreType.DMA((6,)),
        ],
        compiler_params=pltpu.CompilerParams(vmem_limit_bytes=56 * 1024 * 1024),
    )(an, bn, ap, bp, bv, av)


LAST = B_ROWS - HALF
PIECE_LIST = (
    [(0, 0, B_ROWS, 0, 0), (1, 0, B_ROWS, 4, 0), (2, 0, B_ROWS, 8, 0), (3, 0, B_ROWS, 1, 0), (4, 0, B_ROWS, 2, 0)]
    + [(5, 0, HALF, 12, 0), (6, 0, LAST, 12, HALF)]
    + [(7, 0, B_ROWS, 5, 0), (7, B_ROWS, B_ROWS, 9, 0), (7, 2 * B_ROWS, HALF, 3, 0)]
    + [(8, 0, B_ROWS, 6, 0), (8, B_ROWS, B_ROWS, 10, 0), (8, 2 * B_ROWS, LAST, 3, HALF)]
    + [(9, 0, B_ROWS, 13, 0), (9, B_ROWS, B_ROWS, 7, 0)]
    + [(10, 0, B_ROWS, 14, 0), (10, B_ROWS, B_ROWS, 11, 0)]
    + [(11, 0, HALF, 15, 0), (12, 0, LAST, 15, HALF)]
)
CALLS = ((0, 1, 2, 4, 8, 3, 12, 5, 6, 9, 10), (13, 14, 7, 11), (15,))
ORDER = sum(CALLS, ())


def block_pair(load, left, right):
    lane = lax.broadcasted_iota(jnp.int32, (BLOCK, LANES), 1)
    low = jnp.maximum(left, 0)
    high = jnp.maximum(right, 0)
    one = pltpu.roll(load(low // 2), (low % 2) * BLOCK, 1)
    two = pltpu.roll(load(high // 2), (1 - high % 2) * BLOCK, 1)
    one = jnp.where((lane < BLOCK) & (left >= 0), one, 0.0)
    return jnp.where((lane >= BLOCK) & (right >= 0), two, one)


def halves(value):
    top = value.astype(jnp.bfloat16)
    return top, (value - top.astype(jnp.float32)).astype(jnp.bfloat16)


def place_left(me_ref, a_f, spots_s, a_hi, a_lo):
    x, zh, col, zl, core = (me_ref[k] for k in range(5))

    def left_tile(index, _):
        source = index // 2
        slot = index % 2
        owner = (4 * x + zh + source + 8 * slot - col) % PIECES
        off_x = (owner // 4 + 4 - x) % 4
        off_z = (owner % 4 + 4 - zh) % 4
        dx = jnp.where(off_x == 0, 0, jnp.where(off_x == 3, 1, off_x + 1))
        dz = jnp.where(off_z == 0, 0, jnp.where(off_z == 3, 1, off_z + 1))
        at = me_ref[5 + 4 * dz + dx]
        lanes = pl.ds(pl.multiple_of(at * LANES, LANES), LANES)
        for r in range(ROWS_A):
            quarter = r // 2
            place = jnp.where(quarter % 2 == core, 2, 0) + jnp.where(quarter // 2 == zl, 1, 0)
            rows = pl.ds(pl.multiple_of(place * 128 + (r % 2) * BLOCK, BLOCK), BLOCK)

            def load(pair):
                return a_f[source, pl.ds(pl.multiple_of((slot * 4 + pair) * BLOCK, BLOCK), BLOCK), :]

            left = spots_s[source, slot * 16 + 2 * r].astype(jnp.int32)
            right = spots_s[source, slot * 16 + 2 * r + 1].astype(jnp.int32)
            a_hi[rows, lanes], a_lo[rows, lanes] = halves(block_pair(load, left, right))
        return 0

    lax.fori_loop(0, 16, left_tile, 0)


def right_copies(call, b_in, b_f, spots_s, sem_b, sem_s):
    tiles = CALLS[call]
    copies, spots = [], []
    used = sorted({piece[0] for piece in PIECE_LIST if piece[3] in tiles})
    for operand, first, rows, tile, at in PIECE_LIST:
        if tile not in tiles:
            continue
        source, index = b_in[used.index(operand)], tiles.index(tile)
        copies.append(
            pltpu.make_async_copy(
                source.at[pl.ds(first, rows)], b_f.at[index, pl.ds(at, rows)], sem_b.at[len(copies)]
            )
        )
        if at <= B_DATA < at + rows:
            row = first + B_DATA - at
            spots.append(pltpu.make_async_copy(source.at[row], spots_s.at[index], sem_s.at[index]))
    return copies, spots


def place_right(tiles, b_f, spots_s, b_hi, b_lo):
    def right_tile(tile, _):
        for k in range(INNER):
            rows = pl.ds(pl.multiple_of(tile * LANES + k * BLOCK, BLOCK), BLOCK)
            for c in range(COLS_B // 2):

                def load(pair):
                    return b_f[tile, pl.ds(pl.multiple_of(pair * BLOCK, BLOCK), BLOCK), :]

                spot = k * COLS_B + 2 * c
                left = spots_s[tile, spot].astype(jnp.int32)
                right = spots_s[tile, spot + 1].astype(jnp.int32)
                lanes = slice(c * LANES, (c + 1) * LANES)
                b_hi[rows, lanes], b_lo[rows, lanes] = halves(block_pair(load, left, right))
        return 0

    lax.fori_loop(0, tiles, right_tile, 0)


def partial_product(call, a_hi, a_lo, b_hi, b_lo, store):
    first = sum(len(tiles) for tiles in CALLS[:call]) * LANES
    depth = len(CALLS[call]) * LANES
    left_hi, left_lo = a_hi[:, first : first + depth], a_lo[:, first : first + depth]
    for n in range(4):
        lanes = slice(n * 256, (n + 1) * 256)
        top = b_hi[:, lanes]
        total = jnp.dot(left_lo, top, preferred_element_type=jnp.float32)
        total += jnp.dot(left_hi, b_lo[:, lanes], preferred_element_type=jnp.float32)
        total += jnp.dot(left_hi, top, preferred_element_type=jnp.float32)
        store(lanes, total)


def first_kernel(n_right, *refs):
    me_ref, a_in = refs[0], refs[1]
    b_in = refs[2 : 2 + n_right]
    a_hi, a_lo, c_ref = refs[2 + n_right : 5 + n_right]
    a_f, spots_a, sem_a, sem_sa, b_f, b_hi, b_lo, spots_b, sem_b, sem_s = refs[5 + n_right :]
    copy_a = pltpu.make_async_copy(a_in, a_f, sem_a)
    copies, spots = right_copies(0, b_in, b_f, spots_b, sem_b, sem_s)
    copy_a.start()
    spots_of_a = [pltpu.make_async_copy(a_in.at[k, A_DATA], spots_a.at[k], sem_sa.at[k]) for k in range(8)]
    for copy in spots_of_a + spots + copies:
        copy.start()
    for copy in spots_of_a + [copy_a]:
        copy.wait()
    place_left(me_ref, a_f, spots_a, a_hi, a_lo)
    for copy in spots + copies:
        copy.wait()
    place_right(len(CALLS[0]), b_f, spots_b, b_hi, b_lo)

    def store(lanes, total):
        c_ref[:, lanes] = total

    partial_product(0, a_hi, a_lo, b_hi, b_lo, store)


def later_kernel(call, n_right, *refs):
    a_hi, a_lo, c_in = refs[:3]
    b_in = refs[3 : 3 + n_right]
    rest = refs[3 + n_right :]
    outs, (b_f, b_hi, b_lo, spots_b, sem_b, sem_s) = rest[:-6], rest[-6:]
    copies, spots = right_copies(call, b_in, b_f, spots_b, sem_b, sem_s)
    for copy in spots + copies:
        copy.start()
    for copy in spots + copies:
        copy.wait()
    place_right(len(CALLS[call]), b_f, spots_b, b_hi, b_lo)

    def store(lanes, total):
        total += c_in[:, lanes]
        if call == 1:
            outs[0][:, lanes] = total
        else:
            outs[0][:, lanes] = total[:256]
            outs[1][:, lanes] = total[256:384]
            outs[2][:, lanes] = total[384:]

    partial_product(call, a_hi, a_lo, b_hi, b_lo, store)


def right_scratch(call):
    tiles = len(CALLS[call])
    copies = sum(piece[3] in CALLS[call] for piece in PIECE_LIST)
    return [
        pltpu.VMEM((tiles, B_ROWS, LANES), jnp.float32),
        pltpu.VMEM((tiles * LANES, 1024), jnp.bfloat16),
        pltpu.VMEM((tiles * LANES, 1024), jnp.bfloat16),
        pltpu.SMEM((tiles, LANES), jnp.float32),
        pltpu.SemaphoreType.DMA((copies,)),
        pltpu.SemaphoreType.DMA((tiles,)),
    ]


def used_by(call, b_all):
    return [b_all[k] for k in sorted({piece[0] for piece in PIECE_LIST if piece[3] in CALLS[call]})]


def cost(call):
    flops = 3 * 2 * 512 * 1024 * LANES * len(CALLS[call])
    return pl.CostEstimate(flops=flops, bytes_accessed=16 * 1024 * 1024, transcendentals=0)


def first_product(me, a_all, b_all):
    operands = used_by(0, b_all)
    depth = PIECES * LANES
    return pl.pallas_call(
        lambda *refs: first_kernel(len(operands), *refs),
        out_shape=(
            jax.ShapeDtypeStruct((512, depth), jnp.bfloat16),
            jax.ShapeDtypeStruct((512, depth), jnp.bfloat16),
            jax.ShapeDtypeStruct((512, 1024), jnp.float32),
        ),
        in_specs=[IN_SMEM] + [WHERE] * (1 + len(operands)),
        out_specs=(IN_VMEM, IN_VMEM, IN_VMEM),
        scratch_shapes=[
            pltpu.VMEM((8, A_ROWS, LANES), jnp.float32),
            pltpu.SMEM((8, LANES), jnp.float32),
            pltpu.SemaphoreType.DMA,
            pltpu.SemaphoreType.DMA((8,)),
        ]
        + right_scratch(0),
        compiler_params=pltpu.CompilerParams(vmem_limit_bytes=28 * 1024 * 1024),
        cost_estimate=cost(0),
    )(me, a_all, *operands)


def later_product(call, a_hi, a_lo, so_far, b_all):
    operands = used_by(call, b_all)
    shapes = ((512, 1024),) if call == 1 else ((256, 1024), (128, 1024), (128, 1024))
    return pl.pallas_call(
        lambda *refs: later_kernel(call, len(operands), *refs),
        out_shape=tuple(jax.ShapeDtypeStruct(shape, jnp.float32) for shape in shapes),
        in_specs=[IN_VMEM] * 3 + [WHERE] * len(operands),
        out_specs=(IN_VMEM,) * len(shapes),
        scratch_shapes=right_scratch(call),
        compiler_params=pltpu.CompilerParams(vmem_limit_bytes=20 * 1024 * 1024),
        cost_estimate=cost(call),
    )(a_hi, a_lo, so_far, *operands)


def body(a_values, a_places, a_counts, b_values, b_places, b_counts):
    hold = lax.optimization_barrier
    me = [lax.axis_index(name) for name in ("x", "zh", "col", "zl", "core")]
    me = jnp.stack(me + [ORDER.index(tile) for tile in range(PIECES)]).astype(jnp.int32)
    own_a, own = pack(
        a_counts.reshape(2),
        b_counts.reshape(1),
        a_places.reshape(2, CAP_A, 2).swapaxes(1, 2),
        b_places.reshape(CAP_B, 2).swapaxes(0, 1),
        b_values.reshape(CAP_B, BLOCK, BLOCK),
        a_values.reshape(2 * CAP_A, BLOCK, BLOCK),
    )
    a_all = lax.all_gather(own_a, "col")

    z_behind = around(own, "zh", 1)
    z_ahead = around(own, "zh", -1)
    x_behind = around(own, "x", 1)
    x_ahead = around(own, "x", -1)
    z_behind, z_ahead, x_behind, x_ahead = hold((z_behind, z_ahead, x_behind, x_ahead))

    z_far0 = around(z_behind[:HALF], "zh", 1)
    z_far1 = around(z_ahead[HALF:], "zh", -1)
    two_behind = around(jnp.concatenate([z_behind, z_ahead, x_behind[:HALF]], axis=0), "x", 1)
    two_ahead = around(jnp.concatenate([z_behind, z_ahead, x_ahead[HALF:]], axis=0), "x", -1)
    z_far0, z_far1, two_behind, two_ahead = hold((z_far0, z_far1, two_behind, two_ahead))

    three_behind = around(jnp.concatenate([z_far0, z_far1, two_behind[:B_ROWS]], axis=0), "x", 1)
    three_ahead = around(jnp.concatenate([z_far0, z_far1, two_ahead[B_ROWS : 2 * B_ROWS]], axis=0), "x", -1)
    b_all = [own, z_behind, z_ahead, x_behind, x_ahead, z_far0, z_far1, two_behind, two_ahead]
    a_hi, a_lo, total = first_product(me, a_all, b_all)
    three_behind, three_ahead, a_hi, a_lo, total = hold((three_behind, three_ahead, a_hi, a_lo, total))

    four_behind = around(three_behind[:HALF], "x", 1)
    four_ahead = around(three_ahead[HALF:B_ROWS], "x", -1)
    b_all += [three_behind, three_ahead, four_behind, four_ahead]
    (total,) = later_product(1, a_hi, a_lo, total, b_all)
    other, send, keep = later_product(2, a_hi, a_lo, total, b_all)

    got = around(other, "core", 1)
    ahead = around(send + got[:128], "zl", 1)
    return (keep + got[128:]) + ahead


def solution(mesh):
    split = Mesh(mesh.devices.reshape(4, 4, 8, 2, 2), ("x", "zh", "col", "zl", "core"))
    row, layer = ("x", "zh"), ("zl", "core")
    in_specs = (
        P(row, "col", layer, None, None, None, None),
        P(row, "col", layer, None, None, None),
        P(row, "col", layer, None),
        P(row, "col", layer, None, None, None),
        P(row, "col", layer, None, None),
        P(row, "col", layer),
    )
    out_specs = P(("x", "zh", "zl", "core"), "col")
    return jax.shard_map(body, mesh=split, in_specs=in_specs, out_specs=out_specs, check_vma=False)
```

time: 839 us -> 145 us (0.17); the launches traced: 828 us -> 143 us
  starting transfers between devices: 377 us -> 52 us
  local copies, waits for them, and re-layouts: 198 us -> 6.61 us
  matrix products: 103 us -> 0 us
  other arithmetic: 85.9 us -> 2.53 us
  Pallas kernels: 0 us -> 25.3 us
  loops' own time: 11.8 us -> 0 us
    ppermute x90 -> x14, starting transfers between devices: 377 us -> 52 us  [around(): lax.ppermute(array, axis, [(i, (i + distance) % n) for i in range(n)])]
    dot_general x48 -> x0, matrix products: 103 us -> none  [the longest x32 51.4 us: densify(): jnp.dot(select, values.reshape(slots, width * width), precision=lax.Preci...]
    slice x61 -> x8, local copies, waits for them, and re-layouts: 51.8 us -> 0.14 us  [the longest x1 0.03 us: body(): two_ahead[B_ROWS:2 * B_ROWS]]
    select_n x45 -> x0, other arithmetic: 43.6 us -> none  [the longest x15 30.3 us: advance(): an = jnp.where(last, jnp.roll(an, -1, 0), an)]
    ppermute x90 -> x14, waiting for transfers between devices: 2.06 us -> 42.6 us  [around(): lax.ppermute(array, axis, [(i, (i + distance) % n) for i in range(n)])]
    reshape x48 -> x0, local copies, waits for them, and re-layouts: 40.5 us -> none  [the longest x32 34.7 us: densify(): return flat.reshape(rows, cols, width, width).transpose(0, 2, 1, 3).resha...]
    reduce_scatter x1 -> x0, waiting for transfers between devices: 37.4 us -> none  [body(): lax.psum_scatter(partial_value, 'layer', scatter_dimension=0, tiled=True)]
    transpose x16 -> x0, local copies, waits for them, and re-layouts: 31.5 us -> none  [densify(): return flat.reshape(rows, cols, width, width).transpose(0, 2, 1, 3).resha...]
  transfers between devices with their start and end apart: 91 -> 15, of which waited for: 3 -> 7; matrix products, arithmetic and copies ran while one was open for 45% -> 1% of each run, Pallas kernels for 0% -> 15%
where the time goes in v1:
time: 145 us; the launch traced here: 143 us
  starting transfers between devices  52 us (36%)
  waiting for transfers between devices  42.6 us (29%)
  Pallas kernels  25.3 us (17%)
  between operations  14.3 us (10%)
  local copies, waits for them, and re-layouts  6.61 us (5%)
  other arithmetic  2.53 us (2%)
    ppermute x14, starting transfers between devices, around(): lax.ppermute(array, axis, [(i, (i + distance) % n) for i in range(n)])  52 us
    ppermute x14, waiting for transfers between devices, around(): lax.ppermute(array, axis, [(i, (i + distance) % n) for i in range(n)])  42.6 us
    pallas_call x1, Pallas kernels, first_product(): pl.pallas_call(lambda *refs: first_kernel(len(operands), *refs), out_shap...  17.1 us
    unnamed x16, local copies, waits for them, and re-layouts  6.36 us
    pallas_call x2, Pallas kernels, later_product(): pl.pallas_call(lambda *refs: later_kernel(call, len(operands), *refs), ou...  5.88 us
  transfers between devices with their start and end apart: 15, of which 7 were waited for; matrix products, arithmetic and copies ran while one was open for 1% of the time, Pallas kernels for 15%

profile of v1, /device:TPU:56, one launch (start us, length us, event | category | flops | bytes accessed | tf_op | source)
XLA Modules:
  0.0 143.3 jit_solution(14005670258808070718)
XLA Ops:
  6.5 0.0 all-gather.3.cloned.1.call-start
  7.2 2.2 %shard_map.64 = (f32[520,128]{1,0:T(8,128)}, f32[776,128]{1,0:T(8,128)}) custom-call(s32[2]{0:T(128)} %bitcast.22, s32[1]{0:T(128)} %bitcast.16.refs_1_, s32[2,2,8]{2,1,0:T(2,128)} %bitcast.20, s32[2,24]{1,0:T(2,128)} %bitcast.21, f32[24,64,64]{2,1,0:T(8,128)} %bitcast.18, f32[16,64,64]{2,1,0:T(8,128)} %bitcast.19), custom_call_target="tpu_custom_call" | custom-call | tf_op jit(solution)/shard_map/pallas_call | solution.py:71
  9.4 0.0 all-gather.3.cloned.1.call-update
  9.5 6.1 %collective-permute-start = (f32[776,128]{1,0:T(8,128)}, f32[776,128]{1,0:T(8,128)S(1)}, u32[]{:S(2)}, u32[]{:S(2)}) collective-permute-start(f32[776,128]{1,0:T(8,128)} %get-tuple-element.26.refs_2_), channel_id=1, source_target_pairs={{0,32},{32,64},{64,96},{96,0},{1,33},{33,65},{65,97},{97,1},{2,34}... | collective-permute-start | bytes 1191944 | tf_op jit(solution)/shard_map/ppermute | solution.py:29
  15.6 6.8 %collective-permute-start.1 = (f32[776,128]{1,0:T(8,128)}, f32[776,128]{1,0:T(8,128)S(1)}, u32[]{:S(2)}, u32[]{:S(2)}) collective-permute-start(f32[776,128]{1,0:T(8,128)} %get-tuple-element.26.refs_2_), channel_id=1, source_target_pairs={{0,96},{32,0},{64,32},{96,64},{1,97},{33,1},{65,33},{97,65},{2,98}... | collective-permute-start | bytes 1191944 | tf_op jit(solution)/shard_map/ppermute | solution.py:29
  22.3 3.4 %collective-permute-start.2 = (f32[776,128]{1,0:T(8,128)}, f32[776,128]{1,0:T(8,128)S(1)}, u32[]{:S(2)}, u32[]{:S(2)}) collective-permute-start(f32[776,128]{1,0:T(8,128)} %get-tuple-element.26.refs_2_), channel_id=1, source_target_pairs={{0,128},{128,256},{256,384},{384,0},{1,129},{129,257},{257,385},{3... | collective-permute-start | bytes 1191944 | tf_op jit(solution)/shard_map/ppermute | solution.py:29
  25.8 3.7 %collective-permute-start.3 = (f32[776,128]{1,0:T(8,128)}, f32[776,128]{1,0:T(8,128)S(1)}, u32[]{:S(2)}, u32[]{:S(2)}) collective-permute-start(f32[776,128]{1,0:T(8,128)} %get-tuple-element.26.refs_2_), channel_id=1, source_target_pairs={{0,384},{128,0},{256,128},{384,256},{1,385},{129,1},{257,129},{385... | collective-permute-start | bytes 1191944 | tf_op jit(solution)/shard_map/ppermute | solution.py:29
  29.4 0.6 collective-permute-done.refs_3_
  30.0 9.6 %collective-permute-done.1.refs_4_ = f32[776,128]{1,0:T(8,128)S(1)} collective-permute-done((f32[776,128]{1,0:T(8,128)}, f32[776,128]{1,0:T(8,128)S(1)}, u32[]{:S(2)}, u32[]{:S(2)}) %collective-permute-start.1) | collective-permute-done | bytes 397344 | tf_op jit(solution)/shard_map/ppermute | solution.py:29
  39.6 0.0 collective-permute-done.2.refs_5_
  39.6 0.0 collective-permute-done.3.refs_6_
  39.6 0.1 pad_maximum_fusion
  39.7 4.7 %collective-permute-start.7 = (f32[1944,128]{1,0:T(8,128)S(1)}, f32[1944,128]{1,0:T(8,128)S(1)}, u32[]{:S(2)}, u32[]{:S(2)}) collective-permute-start(f32[1944,128]{1,0:T(8,128)S(1)} %pad_maximum_fusion), channel_id=1, source_target_pairs={{0,384},{128,0},{256,128},{384,256},{1,385},{129,1},{257,129},{385... | collective-permute-start | bytes 2985992 | tf_op jit(solution)/shard_map/ppermute | solution.py:29
  44.4 0.0 copy-done.4
  44.4 0.1 pad_maximum_fusion.1
  44.5 1.9 %collective-permute-start.6 = (f32[1936,128]{1,0:T(8,128)S(1)}, f32[1936,128]{1,0:T(8,128)S(1)}, u32[]{:S(2)}, u32[]{:S(2)}) collective-permute-start(f32[1936,128]{1,0:T(8,128)S(1)} %pad_maximum_fusion.1), channel_id=1, source_target_pairs={{0,128},{128,256},{256,384},{384,0},{1,129},{129,257},{257,385},{3... | collective-permute-start | bytes 2973704 | tf_op jit(solution)/shard_map/ppermute | solution.py:29
  46.4 5.5 %collective-permute-start.5 = (f32[392,128]{1,0:T(8,128)S(1)}, f32[392,128]{1,0:T(8,128)S(1)}, u32[]{:S(2)}, u32[]{:S(2)}) collective-permute-start(f32[392,128]{1,0:T(8,128)S(1)} %slice.31), channel_id=1, source_target_pairs={{0,96},{32,0},{64,32},{96,64},{1,97},{33,1},{65,33},{97,65},{2,98}... | collective-permute-start | bytes 602120 | tf_op jit(solution)/shard_map/ppermute | solution.py:29
  51.9 2.2 %collective-permute-start.4 = (f32[384,128]{1,0:T(8,128)S(1)}, f32[384,128]{1,0:T(8,128)S(1)}, u32[]{:S(2)}, u32[]{:S(2)}) collective-permute-start(f32[384,128]{1,0:T(8,128)S(1)} %slice.30), channel_id=1, source_target_pairs={{0,32},{32,64},{64,96},{96,0},{1,33},{33,65},{65,97},{97,1},{2,34}... | collective-permute-start | bytes 589832 | tf_op jit(solution)/shard_map/ppermute | solution.py:29
  54.2 11.2 %collective-permute-done.4.refs_7_ = f32[384,128]{1,0:T(8,128)S(1)} collective-permute-done((f32[384,128]{1,0:T(8,128)S(1)}, f32[384,128]{1,0:T(8,128)S(1)}, u32[]{:S(2)}, u32[]{:S(2)}) %collective-permute-start.4) | collective-permute-done | bytes 196640 | tf_op jit(solution)/shard_map/ppermute | solution.py:29
  65.4 0.0 collective-permute-done.5.refs_8_
  65.4 4.9 %collective-permute-done.6.refs_9_ = f32[1936,128]{1,0:T(8,128)S(1)} collective-permute-done((f32[1936,128]{1,0:T(8,128)S(1)}, f32[1936,128]{1,0:T(8,128)S(1)}, u32[]{:S(2)}, u32[]{:S(2)}) %collective-permute-start.6) | collective-permute-done | bytes 991264 | tf_op jit(solution)/shard_map/ppermute | solution.py:29
  70.3 0.0 collective-permute-done.7.refs_10_
  70.4 1.4 fusion
  71.8 0.4 copy-done.2
  72.2 1.9 %collective-permute-start.8 = (f32[1552,128]{1,0:T(8,128)}, f32[1552,128]{1,0:T(8,128)S(1)}, u32[]{:S(2)}, u32[]{:S(2)}) collective-permute-start(f32[1552,128]{1,0:T(8,128)} %get-tuple-element.48), channel_id=1, source_target_pairs={{0,128},{128,256},{256,384},{384,0},{1,129},{129,257},{257,385},{3... | collective-permute-start | bytes 2383880 | tf_op jit(solution)/shard_map/ppermute | solution.py:29
  74.1 5.1 %collective-permute-start.9 = (f32[1552,128]{1,0:T(8,128)}, f32[1552,128]{1,0:T(8,128)S(1)}, u32[]{:S(2)}, u32[]{:S(2)}) collective-permute-start(f32[1552,128]{1,0:T(8,128)} %get-tuple-element.47), channel_id=1, source_target_pairs={{0,384},{128,0},{256,128},{384,256},{1,385},{129,1},{257,129},{385... | collective-permute-start | bytes 2383880 | tf_op jit(solution)/shard_map/ppermute | solution.py:29
  79.2 0.1 stack.23.refs_0_
  79.3 0.0 all-gather.3.cloned.1.call-done
  79.4 1.2 copy-done.1
  80.6 1.2 copy-done.3
  81.8 1.0 copy-done.5
  82.8 1.6 %copy-done.6 = f32[4160,128]{1,0:T(8,128)S(1)} copy-done((f32[4160,128]{1,0:T(8,128)S(1)}, f32[4160,128]{1,0:T(8,128)}, u32[]{:S(2)}) %copy-start.6) | copy-done | bytes 2129944
  84.4 1.0 copy-done.7
  85.4 17.1 %shard_map.65 = (bf16[512,2048]{1,0:T(8,128)(2,1)S(1)}, bf16[512,2048]{1,0:T(8,128)(2,1)S(1)}, f32[512,1024]{1,0:T(8,128)S(1)}) custom-call(s32[21]{0:T(128)S(1)} %stack.23.refs_0_, f32[8,520,128]{2,1,0:T(8,128)S(1)} %bitcast.17, f32[776,128]{1,0:T(8,128)S(1)} %copy-done.7, f32[776,128]{1,0:T(8,128)S(1)} %collective-permute-done.refs_3_, ...), custom_call_target="tpu_custom_call" | custom-call | flops 4429185024 | bytes 16777216 | tf_op jit(solution)/shard_map/pallas_call | solution.py:274
  102.5 0.0 collective-permute-done.8.refs_3_
  102.5 0.0 collective-permute-done.9.refs_4_
  102.6 1.9 %collective-permute-start.11 = (f32[392,128]{1,0:T(8,128)S(1)}, f32[392,128]{1,0:T(8,128)S(1)}, u32[]{:S(2)}, u32[]{:S(2)}) collective-permute-start(f32[392,128]{1,0:T(8,128)S(1)} %slice.37), channel_id=1, source_target_pairs={{0,384},{128,0},{256,128},{384,256},{1,385},{129,1},{257,129},{385... | collective-permute-start | bytes 602120 | tf_op jit(solution)/shard_map/ppermute | solution.py:29
  104.5 3.9 %collective-permute-start.10 = (f32[384,128]{1,0:T(8,128)S(1)}, f32[384,128]{1,0:T(8,128)S(1)}, u32[]{:S(2)}, u32[]{:S(2)}) collective-permute-start(f32[384,128]{1,0:T(8,128)S(1)} %slice.36), channel_id=1, source_target_pairs={{0,128},{128,256},{256,384},{384,0},{1,129},{129,257},{257,385},{3... | collective-permute-start | bytes 589832 | tf_op jit(solution)/shard_map/ppermute | solution.py:29
  108.4 4.1 %shard_map.66.refs_2_ = f32[512,1024]{1,0:T(8,128)S(1)} custom-call(bf16[512,2048]{1,0:T(8,128)(2,1)S(1)} %get-tuple-element.39.refs_0_, bf16[512,2048]{1,0:T(8,128)(2,1)S(1)} %get-tuple-element.40.refs_1_, f32[512,1024]{1,0:T(8,128)S(1)} %get-tuple-element.41.refs_2_, f32[1552,128]{1,0:T(8,128)S(1)} %collective-permute-done.8.refs_3_, ...), custom_call_target="tpu_custom_call" | custom-call | flops 1610612736 | bytes 16777216 | tf_op jit(solution)/shard_map/pallas_call | solution.py:298
  112.5 0.8 collective-permute-done.10.refs_3_
  113.3 0.0 collective-permute-done.11.refs_4_
  113.3 1.8 %shard_map.67 = (f32[256,1024]{1,0:T(8,128)S(1)}, f32[128,1024]{1,0:T(8,128)S(1)}, f32[128,1024]{1,0:T(8,128)S(1)}) custom-call(bf16[512,2048]{1,0:T(8,128)(2,1)S(1)} %get-tuple-element.39.refs_0_, bf16[512,2048]{1,0:T(8,128)(2,1)S(1)} %get-tuple-element.40.refs_1_, f32[512,1024]{1,0:T(8,128)S(1)} %shard_map.66.refs_2_, ...), custom_call_target="tpu_custom_call" | custom-call | flops 402653184 | bytes 16777216 | tf_op jit(solution)/shard_map/pallas_call | solution.py:298
  115.1 1.9 %collective-permute-start.12 = (f32[256,1024]{1,0:T(8,128)S(1)}, f32[256,1024]{1,0:T(8,128)S(1)}, u32[]{:S(2)}, u32[]{:S(2)}) collective-permute-start(f32[256,1024]{1,0:T(8,128)S(1)} %get-tuple-element.45), channel_id=1, source_target_pairs={{0,1},{1,0},{2,3},{3,2},{4,5},{5,4},{6,7},{7,6},{8,9},{9,8},{10,11... | collective-permute-start | bytes 3145736 | tf_op jit(solution)/shard_map/ppermute | solution.py:29
  117.0 2.6 %collective-permute-done.12 = f32[256,1024]{1,0:T(8,128)S(1)} collective-permute-done((f32[256,1024]{1,0:T(8,128)S(1)}, f32[256,1024]{1,0:T(8,128)S(1)}, u32[]{:S(2)}, u32[]{:S(2)}) %collective-permute-start.12) | collective-permute-done | bytes 1048608 | tf_op jit(solution)/shard_map/ppermute | solution.py:29
  119.7 0.1 slice_add_fusion
  119.7 3.0 %collective-permute-start.13 = (f32[128,1024]{1,0:T(8,128)S(1)}, f32[128,1024]{1,0:T(8,128)S(1)}, u32[]{:S(2)}, u32[]{:S(2)}) collective-permute-start(f32[128,1024]{1,0:T(8,128)S(1)} %slice_add_fusion), channel_id=1, source_target_pairs={{0,2},{2,0},{1,3},{3,1},{4,6},{6,4},{5,7},{7,5},{8,10},{10,8},{9,1... | collective-permute-start | bytes 1572872 | tf_op jit(solution)/shard_map/ppermute | solution.py:29
  122.7 12.9 %collective-permute-done.13 = f32[128,1024]{1,0:T(8,128)S(1)} collective-permute-done((f32[128,1024]{1,0:T(8,128)S(1)}, f32[128,1024]{1,0:T(8,128)S(1)}, u32[]{:S(2)}, u32[]{:S(2)}) %collective-permute-start.13) | collective-permute-done | bytes 524320 | tf_op jit(solution)/shard_map/ppermute | solution.py:29
  135.6 0.9 fusion.1
  (17 shorter events, 0.2 us)
Async XLA Ops:
  6.5 72.8 %all-gather.3.cloned.1.call-start = ((), (), s32[]{:S(2)}) async-start(), calls=%async_computation | async-start | bytes 2396160 | tf_op jit(solution)/shard_map/all_gather | solution.py:321
  9.5 20.5 %collective-permute-start = (f32[776,128]{1,0:T(8,128)}, f32[776,128]{1,0:T(8,128)S(1)}, u32[]{:S(2)}, u32[]{:S(2)}) collective-permute-start(f32[776,128]{1,0:T(8,128)} %get-tuple-element.26.refs_2_), channel_id=1, source_target_pairs={{0,32},{32,64},{64,96},{96,0},{1,33},{33,65},{65,97},{97,1},{2,34}... | collective-permute-start | bytes 1191944 | tf_op jit(solution)/shard_map/ppermute | solution.py:29
  15.6 24.0 %collective-permute-start.1 = (f32[776,128]{1,0:T(8,128)}, f32[776,128]{1,0:T(8,128)S(1)}, u32[]{:S(2)}, u32[]{:S(2)}) collective-permute-start(f32[776,128]{1,0:T(8,128)} %get-tuple-element.26.refs_2_), channel_id=1, source_target_pairs={{0,96},{32,0},{64,32},{96,64},{1,97},{33,1},{65,33},{97,65},{2,98}... | collective-permute-start | bytes 1191944 | tf_op jit(solution)/shard_map/ppermute | solution.py:29
  22.3 17.2 %collective-permute-start.2 = (f32[776,128]{1,0:T(8,128)}, f32[776,128]{1,0:T(8,128)S(1)}, u32[]{:S(2)}, u32[]{:S(2)}) collective-permute-start(f32[776,128]{1,0:T(8,128)} %get-tuple-element.26.refs_2_), channel_id=1, source_target_pairs={{0,128},{128,256},{256,384},{384,0},{1,129},{129,257},{257,385},{3... | collective-permute-start | bytes 1191944 | tf_op jit(solution)/shard_map/ppermute | solution.py:29
  25.8 13.8 %collective-permute-start.3 = (f32[776,128]{1,0:T(8,128)}, f32[776,128]{1,0:T(8,128)S(1)}, u32[]{:S(2)}, u32[]{:S(2)}) collective-permute-start(f32[776,128]{1,0:T(8,128)} %get-tuple-element.26.refs_2_), channel_id=1, source_target_pairs={{0,384},{128,0},{256,128},{384,256},{1,385},{129,1},{257,129},{385... | collective-permute-start | bytes 1191944 | tf_op jit(solution)/shard_map/ppermute | solution.py:29
  39.6 4.8 %copy-start.4 = (f32[776,128]{1,0:T(8,128)}, f32[776,128]{1,0:T(8,128)S(1)}, u32[]{:S(2)}) copy-start(f32[776,128]{1,0:T(8,128)S(1)} %collective-permute-done.2.refs_5_) | copy-start | bytes 1191940
  39.7 30.6 %collective-permute-start.7 = (f32[1944,128]{1,0:T(8,128)S(1)}, f32[1944,128]{1,0:T(8,128)S(1)}, u32[]{:S(2)}, u32[]{:S(2)}) collective-permute-start(f32[1944,128]{1,0:T(8,128)S(1)} %pad_maximum_fusion), channel_id=1, source_target_pairs={{0,384},{128,0},{256,128},{384,256},{1,385},{129,1},{257,129},{385... | collective-permute-start | bytes 2985992 | tf_op jit(solution)/shard_map/ppermute | solution.py:29
  44.5 25.9 %collective-permute-start.6 = (f32[1936,128]{1,0:T(8,128)S(1)}, f32[1936,128]{1,0:T(8,128)S(1)}, u32[]{:S(2)}, u32[]{:S(2)}) collective-permute-start(f32[1936,128]{1,0:T(8,128)S(1)} %pad_maximum_fusion.1), channel_id=1, source_target_pairs={{0,128},{128,256},{256,384},{384,0},{1,129},{129,257},{257,385},{3... | collective-permute-start | bytes 2973704 | tf_op jit(solution)/shard_map/ppermute | solution.py:29
  46.4 19.0 %collective-permute-start.5 = (f32[392,128]{1,0:T(8,128)S(1)}, f32[392,128]{1,0:T(8,128)S(1)}, u32[]{:S(2)}, u32[]{:S(2)}) collective-permute-start(f32[392,128]{1,0:T(8,128)S(1)} %slice.31), channel_id=1, source_target_pairs={{0,96},{32,0},{64,32},{96,64},{1,97},{33,1},{65,33},{97,65},{2,98}... | collective-permute-start | bytes 602120 | tf_op jit(solution)/shard_map/ppermute | solution.py:29
  51.9 13.4 %collective-permute-start.4 = (f32[384,128]{1,0:T(8,128)S(1)}, f32[384,128]{1,0:T(8,128)S(1)}, u32[]{:S(2)}, u32[]{:S(2)}) collective-permute-start(f32[384,128]{1,0:T(8,128)S(1)} %slice.30), channel_id=1, source_target_pairs={{0,32},{32,64},{64,96},{96,0},{1,33},{33,65},{65,97},{97,1},{2,34}... | collective-permute-start | bytes 589832 | tf_op jit(solution)/shard_map/ppermute | solution.py:29
  70.3 1.5 %copy-start = (f32[1936,128]{1,0:T(8,128)}, f32[1936,128]{1,0:T(8,128)S(1)}, u32[]{:S(2)}) copy-start(f32[1936,128]{1,0:T(8,128)S(1)} %collective-permute-done.6.refs_9_) | copy-start | bytes 2973700
  70.3 1.9 %copy-start.2 = (f32[1944,128]{1,0:T(8,128)}, f32[1944,128]{1,0:T(8,128)S(1)}, u32[]{:S(2)}) copy-start(f32[1944,128]{1,0:T(8,128)S(1)} %collective-permute-done.7.refs_10_) | copy-start | bytes 2985988
  72.2 30.3 %collective-permute-start.8 = (f32[1552,128]{1,0:T(8,128)}, f32[1552,128]{1,0:T(8,128)S(1)}, u32[]{:S(2)}, u32[]{:S(2)}) collective-permute-start(f32[1552,128]{1,0:T(8,128)} %get-tuple-element.48), channel_id=1, source_target_pairs={{0,128},{128,256},{256,384},{384,0},{1,129},{129,257},{257,385},{3... | collective-permute-start | bytes 2383880 | tf_op jit(solution)/shard_map/ppermute | solution.py:29
  74.1 28.4 %collective-permute-start.9 = (f32[1552,128]{1,0:T(8,128)}, f32[1552,128]{1,0:T(8,128)S(1)}, u32[]{:S(2)}, u32[]{:S(2)}) collective-permute-start(f32[1552,128]{1,0:T(8,128)} %get-tuple-element.47), channel_id=1, source_target_pairs={{0,384},{128,0},{256,128},{384,256},{1,385},{129,1},{257,129},{385... | collective-permute-start | bytes 2383880 | tf_op jit(solution)/shard_map/ppermute | solution.py:29
  79.4 1.2 copy-start.1
  80.6 1.2 copy-start.3
  81.8 1.0 copy-start.5
  82.8 1.6 %copy-start.6 = (f32[4160,128]{1,0:T(8,128)S(1)}, f32[4160,128]{1,0:T(8,128)}, u32[]{:S(2)}) copy-start(f32[4160,128]{1,0:T(8,128)} %all-gather.3.cloned.1.call-done) | copy-start | bytes 6389764
  84.4 1.0 copy-start.7
  102.6 10.7 %collective-permute-start.11 = (f32[392,128]{1,0:T(8,128)S(1)}, f32[392,128]{1,0:T(8,128)S(1)}, u32[]{:S(2)}, u32[]{:S(2)}) collective-permute-start(f32[392,128]{1,0:T(8,128)S(1)} %slice.37), channel_id=1, source_target_pairs={{0,384},{128,0},{256,128},{384,256},{1,385},{129,1},{257,129},{385... | collective-permute-start | bytes 602120 | tf_op jit(solution)/shard_map/ppermute | solution.py:29
  104.5 8.8 %collective-permute-start.10 = (f32[384,128]{1,0:T(8,128)S(1)}, f32[384,128]{1,0:T(8,128)S(1)}, u32[]{:S(2)}, u32[]{:S(2)}) collective-permute-start(f32[384,128]{1,0:T(8,128)S(1)} %slice.36), channel_id=1, source_target_pairs={{0,128},{128,256},{256,384},{384,0},{1,129},{129,257},{257,385},{3... | collective-permute-start | bytes 589832 | tf_op jit(solution)/shard_map/ppermute | solution.py:29
  115.1 4.6 %collective-permute-start.12 = (f32[256,1024]{1,0:T(8,128)S(1)}, f32[256,1024]{1,0:T(8,128)S(1)}, u32[]{:S(2)}, u32[]{:S(2)}) collective-permute-start(f32[256,1024]{1,0:T(8,128)S(1)} %get-tuple-element.45), channel_id=1, source_target_pairs={{0,1},{1,0},{2,3},{3,2},{4,5},{5,4},{6,7},{7,6},{8,9},{9,8},{10,11... | collective-permute-start | bytes 3145736 | tf_op jit(solution)/shard_map/ppermute | solution.py:29
  119.7 15.9 %collective-permute-start.13 = (f32[128,1024]{1,0:T(8,128)S(1)}, f32[128,1024]{1,0:T(8,128)S(1)}, u32[]{:S(2)}, u32[]{:S(2)}) collective-permute-start(f32[128,1024]{1,0:T(8,128)S(1)} %slice_add_fusion), channel_id=1, source_target_pairs={{0,2},{2,0},{1,3},{3,1},{4,6},{6,4},{5,7},{7,5},{8,10},{10,8},{9,1... | collective-permute-start | bytes 1572872 | tf_op jit(solution)/shard_map/ppermute | solution.py:29
Sparse Core Ops, SparseCore 0:
  9.6 46.8 all-gather.2

commit v2 on v1

v2 whole, which is shorter than its diff:
```python
import jax
import jax.numpy as jnp
from jax import lax
from jax.experimental import pallas as pl
from jax.experimental.pallas import tpu as pltpu
from jax.sharding import Mesh, PartitionSpec as P

BLOCK = 64
LANES = 128
CAP_A = 8
CAP_B = 24
ROWS_A = 8
INNER = 2
COLS_B = 16
PIECES = 16
B_DATA = CAP_B // 2 * BLOCK
B_ROWS = B_DATA + 8
A_DATA = CAP_A * BLOCK
A_ROWS = A_DATA + 8
WHERE = pl.BlockSpec(memory_space=pl.ANY)
IN_VMEM = pl.BlockSpec(memory_space=pltpu.VMEM)
BIG = 56 * 1024 * 1024
EARLY = 20 * 1024 * 1024
FIRST = 20 * 1024 * 1024
IN_HBM = pl.BlockSpec(memory_space=pltpu.HBM)
IN_SMEM = pl.BlockSpec(memory_space=pltpu.SMEM)


def exchange(array, axis, step):
    mask = {0: (1, 3)[step], 1: (3, 1)[step]}
    route = [(2 * i + core, 2 * (i ^ mask[core]) + core) for i in range(4) for core in range(2)]
    return lax.ppermute(array, (axis, "core"), route)


def col_partner(place, core, distance):
    if distance == 4:
        return place ^ 4
    if distance == 2:
        forward = place // 2 % 2 == (core + place) % 2
        return (place + (2 if forward else -2)) % 8
    return (place + (1 if place % 2 == core else -1)) % 8


def exchange_col(array, distance):
    route = [(2 * i + core, 2 * col_partner(i, core, distance) + core) for i in range(8) for core in range(2)]
    return lax.ppermute(array, ("col", "core"), route)


def holders(place, core):
    held = [place]
    for distance in (4, 2, 1):
        partner = holders_before(col_partner(place, core, distance), core, distance)
        held = held + partner
    return held


def holders_before(place, core, distance):
    held = [place]
    for earlier in (4, 2):
        if earlier <= distance:
            break
        held = held + holders_before(col_partner(place, core, earlier), core, earlier)
    return held


def swap(array, axis):
    return lax.ppermute(array, axis, [(0, 1), (1, 0)])


def slot_at(places, count, cols, base):
    slots = places.shape[1]
    spot = places[0:1, :] * cols + places[1:2, :] + base
    position = lax.broadcasted_iota(jnp.int32, (LANES, slots), 0)
    slot = lax.broadcasted_iota(jnp.int32, (LANES, slots), 1)
    hit = (position == spot) & (slot < count)
    return jnp.max(jnp.where(hit, slot + 1, 0), axis=1, keepdims=True)


def as_rows(column):
    return jnp.transpose(jnp.broadcast_to(column.astype(jnp.float32), (LANES, LANES)))[0:8, :]


def pack_kernel(*refs):
    ins, (a_ref, b_ref), held, sems = refs[:6], refs[6:8], refs[8:14], refs[14]
    an_ref, bn_ref, ap_ref, bp_ref, bv_ref, av_ref = held
    copies = [pltpu.make_async_copy(ins[k], held[k], sems.at[k]) for k in range(6)]
    for copy in copies:
        copy.start()
    for copy in copies[:4]:
        copy.wait()
    copy_b, copy_a = copies[4:]
    spots = slot_at(ap_ref[0], an_ref[0], INNER, 0) + slot_at(ap_ref[1], an_ref[1], INNER, 16) - 1
    a_ref[A_DATA:, :] = as_rows(spots)
    spots = slot_at(bp_ref[...], bn_ref[0, 0, 0], COLS_B, 0) - 1
    b_ref[B_DATA:, :] = as_rows(spots)
    copy_b.wait()
    for pair in range(CAP_B // 2):
        b_ref[pair * BLOCK : (pair + 1) * BLOCK, :] = jnp.concatenate(
            [bv_ref[2 * pair], bv_ref[2 * pair + 1]], axis=1
        )
    copy_a.wait()
    for pair in range(CAP_A):
        a_ref[pair * BLOCK : (pair + 1) * BLOCK, :] = jnp.concatenate(
            [av_ref[2 * pair], av_ref[2 * pair + 1]], axis=1
        )


def pack(an, bn, ap, bp, bv, av):
    return pl.pallas_call(
        pack_kernel,
        out_shape=(
            jax.ShapeDtypeStruct((A_ROWS, LANES), jnp.float32),
            jax.ShapeDtypeStruct((B_ROWS, LANES), jnp.float32),
        ),
        in_specs=[IN_HBM] * 6,
        out_specs=(IN_VMEM, IN_VMEM),
        scratch_shapes=[
            pltpu.SMEM(an.shape, jnp.int32),
            pltpu.SMEM(bn.shape, jnp.int32),
            pltpu.VMEM(ap.shape, jnp.int32),
            pltpu.VMEM(bp.shape, jnp.int32),
            pltpu.VMEM(bv.shape, jnp.float32),
            pltpu.VMEM(av.shape, jnp.float32),
            pltpu.SemaphoreType.DMA((6,)),
        ],
        compiler_params=pltpu.CompilerParams(vmem_limit_bytes=BIG),
    )(an, bn, ap, bp, bv, av)


HELD = ((0,), (4,), (1,), (8, 12), (2, 3), (5, 9, 13), (6, 10, 14), (7, 11, 15))
CALLS = ((0, 4, 1, 8, 12, 2, 3), (5, 9, 13, 6, 10, 14), (7, 11, 15))
ORDER = sum(CALLS, ())


def block_pair(load, left, right):
    lane = lax.broadcasted_iota(jnp.int32, (BLOCK, LANES), 1)
    low = jnp.maximum(left, 0)
    high = jnp.maximum(right, 0)
    one = pltpu.roll(load(low // 2), (low % 2) * BLOCK, 1)
    two = pltpu.roll(load(high // 2), (1 - high % 2) * BLOCK, 1)
    one = jnp.where((lane < BLOCK) & (left >= 0), one, 0.0)
    return jnp.where((lane >= BLOCK) & (right >= 0), two, one)


def halves(value):
    top = value.astype(jnp.bfloat16)
    return top, (value - top.astype(jnp.float32)).astype(jnp.bfloat16)


def ring_place(mask, core):
    near = jnp.where(mask == 1 + 2 * core, 1, 2)
    return jnp.where(mask == 0, 0, jnp.where(mask == 2, 3, near))


def place_left(me_ref, a_f, spots_s, a_hi, a_lo):
    x, zh, col, zl, core = (me_ref[k] for k in range(5))

    def left_tile(index, _):
        source = index // 2
        slot = index % 2
        holder = me_ref[5 + PIECES + (2 * col + core) * 8 + source]
        owner = (4 * x + zh + holder + 8 * slot + PIECES - col) % PIECES
        dx = ring_place((owner // 4) ^ x, core)
        dz = ring_place((owner % 4) ^ zh, core)
        at = me_ref[5 + 4 * dz + dx]
        lanes = pl.ds(pl.multiple_of(at * LANES, LANES), LANES)
        for r in range(ROWS_A):
            quarter = r // 2
            place = jnp.where(quarter % 2 == core, 2, 0) + jnp.where(quarter // 2 == zl, 1, 0)
            rows = pl.ds(pl.multiple_of(place * 128 + (r % 2) * BLOCK, BLOCK), BLOCK)

            def load(pair):
                return a_f[source, pl.ds(pl.multiple_of((slot * 4 + pair) * BLOCK, BLOCK), BLOCK), :]

            left = spots_s[source, slot * 16 + 2 * r].astype(jnp.int32)
            right = spots_s[source, slot * 16 + 2 * r + 1].astype(jnp.int32)
            a_hi[rows, lanes], a_lo[rows, lanes] = halves(block_pair(load, left, right))
        return 0

    lax.fori_loop(0, 16, left_tile, 0)


def right_copies(call, b_in, b_f, spots_s, sem_b, sem_s):
    tiles = CALLS[call]
    copies, spots = [], []
    for source, held in zip(b_in, [held for held in HELD if held[0] in tiles], strict=True):
        for k, tile in enumerate(held):
            at = tiles.index(tile)
            rows = pl.ds(k * B_ROWS, B_ROWS)
            copies.append(pltpu.make_async_copy(source.at[rows], b_f.at[at], sem_b.at[at]))
            spots.append(pltpu.make_async_copy(source.at[k * B_ROWS + B_DATA], spots_s.at[at], sem_s.at[at]))
    return copies, spots


def place_right(tiles, b_f, spots_s, b_hi, b_lo):
    def right_tile(tile, _):
        for k in range(INNER):
            rows = pl.ds(pl.multiple_of(tile * LANES + k * BLOCK, BLOCK), BLOCK)
            for c in range(COLS_B // 2):

                def load(pair):
                    return b_f[tile, pl.ds(pl.multiple_of(pair * BLOCK, BLOCK), BLOCK), :]

                spot = k * COLS_B + 2 * c
                left = spots_s[tile, spot].astype(jnp.int32)
                right = spots_s[tile, spot + 1].astype(jnp.int32)
                lanes = slice(c * LANES, (c + 1) * LANES)
                b_hi[rows, lanes], b_lo[rows, lanes] = halves(block_pair(load, left, right))
        return 0

    lax.fori_loop(0, tiles, right_tile, 0)


def first_lane(call):
    return sum(len(tiles) for tiles in CALLS[:call]) * LANES


def partial_product(left_hi, left_lo, b_hi, b_lo, store):
    for n in range(4):
        lanes = slice(n * 256, (n + 1) * 256)
        top = b_hi[:, lanes]
        total = jnp.dot(left_lo, top, preferred_element_type=jnp.float32)
        total += jnp.dot(left_hi, b_lo[:, lanes], preferred_element_type=jnp.float32)
        total += jnp.dot(left_hi, top, preferred_element_type=jnp.float32)
        store(lanes, total)


def early_kernel(n_right, *refs):
    b_in = refs[:n_right]
    b_hi, b_lo, b_f, spots_b, sem_b, sem_s = refs[n_right:]
    copies, spots = right_copies(0, b_in, b_f, spots_b, sem_b, sem_s)
    for copy in spots + copies:
        copy.start()
    for copy in spots + copies:
        copy.wait()
    place_right(len(CALLS[0]), b_f, spots_b, b_hi, b_lo)


def first_kernel(*refs):
    me_ref, a_in, b_in = refs[0], refs[1:5], refs[5:7]
    a_hi, a_lo, c_ref = refs[7:10]
    a_f, spots_a, sem_a, sem_sa, b_hi, b_lo, sem_b = refs[10:]
    parts = [(part, k) for part in a_in for k in range(part.shape[0] // A_ROWS)]
    copies_a, spots_of_a = [], []
    for n, (part, k) in enumerate(parts):
        rows = pl.ds(k * A_ROWS, A_ROWS)
        copies_a.append(pltpu.make_async_copy(part.at[rows], a_f.at[n], sem_a.at[n]))
        spots_of_a.append(pltpu.make_async_copy(part.at[k * A_ROWS + A_DATA], spots_a.at[n], sem_sa.at[n]))
    copies = [pltpu.make_async_copy(b_in[k], (b_hi, b_lo)[k], sem_b.at[k]) for k in range(2)]
    for copy in spots_of_a + copies_a + copies:
        copy.start()
    for copy in spots_of_a + copies_a:
        copy.wait()
    place_left(me_ref, a_f, spots_a, a_hi, a_lo)
    for copy in copies:
        copy.wait()

    def store(lanes, total):
        c_ref[:, lanes] = total

    depth = len(CALLS[0]) * LANES
    partial_product(a_hi[:, :depth], a_lo[:, :depth], b_hi, b_lo, store)


def middle_kernel(call, n_right, *refs):
    a_in, c_in = refs[:2], refs[2]
    b_in = refs[3 : 3 + n_right]
    c_out, a_hi, a_lo, c_held, sem_a, b_f, b_hi, b_lo, spots_b, sem_b, sem_s = refs[3 + n_right :]
    copies, spots = right_copies(call, b_in, b_f, spots_b, sem_b, sem_s)
    lanes = pl.ds(first_lane(call), len(CALLS[call]) * LANES)
    held = [pltpu.make_async_copy(a_in[k].at[:, lanes], (a_hi, a_lo)[k], sem_a.at[k]) for k in range(2)]
    held.append(pltpu.make_async_copy(c_in, c_held, sem_a.at[2]))
    for copy in spots + copies + held:
        copy.start()
    for copy in spots + copies:
        copy.wait()
    place_right(len(CALLS[call]), b_f, spots_b, b_hi, b_lo)
    for copy in held:
        copy.wait()

    def store(lanes, total):
        c_out[:, lanes] = total + c_held[:, lanes]

    partial_product(a_hi[...], a_lo[...], b_hi, b_lo, store)


def last_kernel(call, n_right, *refs):
    a_hi, a_lo, c_in = refs[:3]
    b_in = refs[3 : 3 + n_right]
    other, send, keep, b_f, b_hi, b_lo, spots_b, sem_b, sem_s = refs[3 + n_right :]
    copies, spots = right_copies(call, b_in, b_f, spots_b, sem_b, sem_s)
    for copy in spots + copies:
        copy.start()
    for copy in spots + copies:
        copy.wait()
    place_right(len(CALLS[call]), b_f, spots_b, b_hi, b_lo)

    def store(lanes, total):
        total += c_in[:, lanes]
        other[:, lanes] = total[:256]
        send[:, lanes] = total[256:384]
        keep[:, lanes] = total[384:]

    first = first_lane(call)
    depth = len(CALLS[call]) * LANES
    partial_product(a_hi[:, first : first + depth], a_lo[:, first : first + depth], b_hi, b_lo, store)


def right_scratch(call):
    tiles = len(CALLS[call])
    return [
        pltpu.VMEM((tiles, B_ROWS, LANES), jnp.float32),
        pltpu.VMEM((tiles * LANES, 1024), jnp.bfloat16),
        pltpu.VMEM((tiles * LANES, 1024), jnp.bfloat16),
        pltpu.SMEM((tiles, LANES), jnp.float32),
        pltpu.SemaphoreType.DMA((tiles,)),
        pltpu.SemaphoreType.DMA((tiles,)),
    ]


def used_by(call, b_all):
    return [b_all[k] for k in range(len(HELD)) if HELD[k][0] in CALLS[call]]


def cost(call):
    flops = 3 * 2 * 512 * 1024 * LANES * len(CALLS[call])
    return pl.CostEstimate(flops=flops, bytes_accessed=16 * 1024 * 1024, transcendentals=0)


def early_right(b_all):
    operands = used_by(0, b_all)
    depth = len(CALLS[0]) * LANES
    scratch = right_scratch(0)
    return pl.pallas_call(
        lambda *refs: early_kernel(len(operands), *refs),
        out_shape=(jax.ShapeDtypeStruct((depth, 1024), jnp.bfloat16),) * 2,
        in_specs=[WHERE] * len(operands),
        out_specs=(IN_VMEM,) * 2,
        scratch_shapes=scratch[:1] + scratch[3:],
        compiler_params=pltpu.CompilerParams(vmem_limit_bytes=EARLY),
        cost_estimate=pl.CostEstimate(flops=10**9, bytes_accessed=16 * 1024 * 1024, transcendentals=0),
    )(*operands)


def first_product(me, a_all, right):
    depth = PIECES * LANES
    return pl.pallas_call(
        first_kernel,
        out_shape=(
            jax.ShapeDtypeStruct((512, depth), jnp.bfloat16),
            jax.ShapeDtypeStruct((512, depth), jnp.bfloat16),
            jax.ShapeDtypeStruct((512, 1024), jnp.float32),
        ),
        in_specs=[IN_SMEM] + [WHERE] * 6,
        out_specs=(IN_VMEM,) * 3,
        scratch_shapes=[
            pltpu.VMEM((8, A_ROWS, LANES), jnp.float32),
            pltpu.SMEM((8, LANES), jnp.float32),
            pltpu.SemaphoreType.DMA((8,)),
            pltpu.SemaphoreType.DMA((8,)),
        ]
        + right_scratch(0)[1:3]
        + [pltpu.SemaphoreType.DMA((2,))],
        compiler_params=pltpu.CompilerParams(vmem_limit_bytes=FIRST),
        cost_estimate=cost(0),
    )(me, *a_all, *right)


def middle_product(call, a_hi, a_lo, so_far, b_all, limit):
    operands = used_by(call, b_all)
    depth = len(CALLS[call]) * LANES
    return pl.pallas_call(
        lambda *refs: middle_kernel(call, len(operands), *refs),
        out_shape=jax.ShapeDtypeStruct((512, 1024), jnp.float32),
        in_specs=[WHERE] * (3 + len(operands)),
        out_specs=IN_VMEM,
        scratch_shapes=[
            pltpu.VMEM((512, depth), jnp.bfloat16),
            pltpu.VMEM((512, depth), jnp.bfloat16),
            pltpu.VMEM((512, 1024), jnp.float32),
            pltpu.SemaphoreType.DMA((3,)),
        ]
        + right_scratch(call),
        compiler_params=pltpu.CompilerParams(vmem_limit_bytes=limit),
        cost_estimate=cost(call),
    )(a_hi, a_lo, so_far, *operands)


def last_product(call, a_hi, a_lo, so_far, b_all):
    operands = used_by(call, b_all)
    return pl.pallas_call(
        lambda *refs: last_kernel(call, len(operands), *refs),
        out_shape=tuple(jax.ShapeDtypeStruct((rows, 1024), jnp.float32) for rows in (256, 128, 128)),
        in_specs=[IN_VMEM] * 3 + [WHERE] * len(operands),
        out_specs=(IN_VMEM,) * 3,
        scratch_shapes=right_scratch(call),
        compiler_params=pltpu.CompilerParams(vmem_limit_bytes=16 * 1024 * 1024),
        cost_estimate=cost(call),
    )(a_hi, a_lo, so_far, *operands)


def body(a_values, a_places, a_counts, b_values, b_places, b_counts):
    hold = lax.optimization_barrier
    by_place = [holder for place in range(8) for core in range(2) for holder in holders(place, core)]
    me = [lax.axis_index(name) for name in ("x", "zh", "col", "zl", "core")]
    table = jnp.array([ORDER.index(tile) for tile in range(PIECES)] + by_place, jnp.int32)
    me = jnp.concatenate([jnp.stack(me).astype(jnp.int32), table])
    own_a, own = pack(
        a_counts.reshape(2),
        b_counts,
        a_places.reshape(2, CAP_A, 2).swapaxes(1, 2),
        b_places.reshape(CAP_B, 2).swapaxes(0, 1),
        b_values.reshape(CAP_B, BLOCK, BLOCK),
        a_values.reshape(2 * CAP_A, BLOCK, BLOCK),
    )
    z_one = exchange(own, "zh", 0)
    x_one = exchange(own, "x", 0)
    a_one = exchange_col(own_a, 4)
    z_one, x_one, a_one = hold((z_one, x_one, a_one))

    z_two = exchange(jnp.concatenate([own, z_one], axis=0), "zh", 1)
    x_two = exchange(jnp.concatenate([own, x_one], axis=0), "x", 1)
    a_two = exchange_col(jnp.concatenate([own_a, a_one], axis=0), 2)
    z_two, x_two = hold((z_two, x_two))

    column = jnp.concatenate([z_one, z_two], axis=0)
    x_three = exchange(column, "x", 0)
    x_four = exchange(column, "x", 1)
    b_all = [own, z_one, x_one, z_two, x_two]
    x_two, a_two = hold((x_two, a_two))
    b_all = [own, z_one, x_one, z_two, x_two]
    right_hi, right_lo = early_right(b_all)
    a_two, right_hi, right_lo = hold((a_two, right_hi, right_lo))
    a_four = exchange_col(jnp.concatenate([own_a, a_one, a_two], axis=0), 1)
    a_hi, a_lo, total = first_product(me, (own_a, a_one, a_two, a_four), (right_hi, right_lo))

    b_all += [x_three, x_four, exchange(x_three, "x", 1)]
    total = middle_product(1, a_hi, a_lo, total, b_all, 20 * 1024 * 1024)
    other, send, keep = last_product(2, a_hi, a_lo, total, b_all)

    got = swap(other, "core")
    ahead = swap(send + got[:128], "zl")
    return (keep + got[128:]) + ahead


def solution(mesh):
    split = Mesh(mesh.devices.reshape(4, 4, 8, 2, 2), ("x", "zh", "col", "zl", "core"))
    row, layer = ("x", "zh"), ("zl", "core")
    in_specs = (
        P(row, "col", layer, None, None, None, None),
        P(row, "col", layer, None, None, None),
        P(row, "col", layer, None),
        P(row, "col", layer, None, None, None),
        P(row, "col", layer, None, None),
        P(row, "col", layer),
    )
    out_specs = P(("x", "zh", "zl", "core"), "col")
    return jax.shard_map(body, mesh=split, in_specs=in_specs, out_specs=out_specs, check_vma=False)
```

time: 145 us -> 134 us (0.924)
  the two profiles are of different devices: /device:TPU:56 before, /device:TPU:38 now
where the time goes in v2:
time: 134 us; the launch traced here: 133 us
  starting transfers between devices  51.2 us (38%)
  waiting for transfers between devices  46 us (34%)
  Pallas kernels  26.1 us (19%)
  local copies, waits for them, and re-layouts  6.1 us (5%)
  other arithmetic  3.25 us (2%)
    ppermute x7, starting transfers between devices, exchange(): return lax.ppermute(array, (axis, 'core'), route)  40.2 us
    ppermute x7, waiting for transfers between devices, exchange(): return lax.ppermute(array, (axis, 'core'), route)  18.8 us
    ppermute x2, waiting for transfers between devices, swap(): return lax.ppermute(array, axis, [(0, 1), (1, 0)])  16.6 us
    ppermute x3, waiting for transfers between devices, exchange_col(): return lax.ppermute(array, ('col', 'core'), route)  10.6 us
    pallas_call x1, Pallas kernels, first_product(): pl.pallas_call(first_kernel, out_shape=(jax.ShapeDtypeStruct((512, depth)...  9.7 us
    ppermute x3, starting transfers between devices, exchange_col(): return lax.ppermute(array, ('col', 'core'), route)  7.09 us
    pallas_call x1, Pallas kernels, middle_product(): pl.pallas_call(lambda *refs: middle_kernel(call, len(operands), *refs), o...  6.65 us
    unnamed x15, local copies, waits for them, and re-layouts  5.08 us
  transfers between devices with their start and end apart: 12, of which 5 were waited for; matrix products, arithmetic and copies ran while one was open for 2% of the time, Pallas kernels for 15%

profile of v2, /device:TPU:38, one launch (start us, length us, event | category | flops | bytes accessed | tf_op | source)
XLA Modules:
  0.0 133.5 jit_solution(2266552218815684885)
XLA Ops:
  0.7 2.2 %shard_map.73 = (f32[520,128]{1,0:T(8,128)}, f32[776,128]{1,0:T(8,128)}) custom-call(s32[2]{0:T(128)} %bitcast.18, s32[1,1,1]{2,1,0:T(1,128)S(6)} %copy.9.refs_1_, s32[2,2,8]{2,1,0:T(2,128)} %bitcast.16, s32[2,24]{1,0:T(2,128)} %bitcast.17, f32[24,64,64]{2,1,0:T(8,128)} %bitcast.14, f32[16,64,64]{2,1,0:T(8,128)} %bitcast.15), custom_call_target="tpu_custom_call" | custom-call | tf_op jit(solution)/shard_map/pallas_call | solution.py:109
  2.9 6.1 %collective-permute-start = (f32[776,128]{1,0:T(8,128)}, f32[776,128]{1,0:T(8,128)S(1)}, u32[]{:S(2)}, u32[]{:S(2)}) collective-permute-start(f32[776,128]{1,0:T(8,128)} %get-tuple-element.26.refs_0_), channel_id=1, source_target_pairs={{0,32},{1,97},{32,0},{33,65},{64,96},{65,33},{96,64},{97,1},{2,34}... | collective-permute-start | bytes 1191944 | tf_op jit(solution)/shard_map/ppermute | solution.py:32
  9.0 2.7 %collective-permute-start.1 = (f32[776,128]{1,0:T(8,128)}, f32[776,128]{1,0:T(8,128)S(1)}, u32[]{:S(2)}, u32[]{:S(2)}) collective-permute-start(f32[776,128]{1,0:T(8,128)} %get-tuple-element.26.refs_0_), channel_id=1, source_target_pairs={{0,128},{1,385},{128,0},{129,257},{256,384},{257,129},{384,256},{3... | collective-permute-start | bytes 1191944 | tf_op jit(solution)/shard_map/ppermute | solution.py:32
  11.7 0.0 copy-start
  11.7 2.1 %collective-permute-start.2 = (f32[520,128]{1,0:T(8,128)}, f32[520,128]{1,0:T(8,128)S(1)}, u32[]{:S(2)}, u32[]{:S(2)}) collective-permute-start(f32[520,128]{1,0:T(8,128)} %get-tuple-element.25.refs_1_), channel_id=1, source_target_pairs={{0,16},{1,17},{4,20},{5,21},{8,24},{9,25},{12,28},{13,29},{16,0},{... | collective-permute-start | bytes 798728 | tf_op jit(solution)/shard_map/ppermute | solution.py:46
  13.9 10.6 %collective-permute-done.2.refs_2_ = f32[520,128]{1,0:T(8,128)S(1)} collective-permute-done((f32[520,128]{1,0:T(8,128)}, f32[520,128]{1,0:T(8,128)S(1)}, u32[]{:S(2)}, u32[]{:S(2)}) %collective-permute-start.2) | collective-permute-done | bytes 266272 | tf_op jit(solution)/shard_map/ppermute | solution.py:46
  24.5 0.0 collective-permute-done.refs_1_
  24.5 0.0 collective-permute-done.1.refs_2_
  24.5 1.1 pad_maximum_fusion.1
  25.6 13.4 %collective-permute-start.3 = (f32[1552,128]{1,0:T(8,128)S(1)}, f32[1552,128]{1,0:T(8,128)S(1)}, u32[]{:S(2)}, u32[]{:S(2)}) collective-permute-start(f32[1552,128]{1,0:T(8,128)S(1)} %get-tuple-element.46), channel_id=1, source_target_pairs={{0,96},{1,33},{32,64},{33,1},{64,32},{65,97},{96,0},{97,65},{2,98}... | collective-permute-start | bytes 2383880 | tf_op jit(solution)/shard_map/ppermute | solution.py:32
  39.0 4.7 %collective-permute-start.4 = (f32[1552,128]{1,0:T(8,128)S(1)}, f32[1552,128]{1,0:T(8,128)S(1)}, u32[]{:S(2)}, u32[]{:S(2)}) collective-permute-start(f32[1552,128]{1,0:T(8,128)S(1)} %get-tuple-element.45), channel_id=1, source_target_pairs={{0,384},{1,129},{128,256},{129,1},{256,128},{257,385},{384,0},{385... | collective-permute-start | bytes 2383880 | tf_op jit(solution)/shard_map/ppermute | solution.py:32
  43.7 0.0 copy-done
  43.7 0.0 copy-start.1
  43.7 2.7 %collective-permute-start.5 = (f32[1040,128]{1,0:T(8,128)S(1)}, f32[1040,128]{1,0:T(8,128)S(1)}, u32[]{:S(2)}, u32[]{:S(2)}) collective-permute-start(f32[1040,128]{1,0:T(8,128)S(1)} %pad_maximum_fusion.3), channel_id=1, source_target_pairs={{0,8},{1,25},{4,28},{5,13},{8,0},{9,17},{12,20},{13,5},{16,24},{17... | collective-permute-start | bytes 1597448 | tf_op jit(solution)/shard_map/ppermute | solution.py:46
  46.4 0.8 constant_dynamic-update-slice_fusion.1
  47.2 10.4 %collective-permute-done.3.refs_3_ = f32[1552,128]{1,0:T(8,128)S(1)} collective-permute-done((f32[1552,128]{1,0:T(8,128)S(1)}, f32[1552,128]{1,0:T(8,128)S(1)}, u32[]{:S(2)}, u32[]{:S(2)}) %collective-permute-start.3) | collective-permute-done | bytes 794656 | tf_op jit(solution)/shard_map/ppermute | solution.py:32
  57.6 0.0 collective-permute-done.4.refs_4_
  57.6 0.9 constant_dynamic-update-slice_fusion
  58.5 2.8 %collective-permute-start.7 = (f32[2328,128]{1,0:T(8,128)}, f32[2328,128]{1,0:T(8,128)S(1)}, u32[]{:S(2)}, u32[]{:S(2)}) collective-permute-start(f32[2328,128]{1,0:T(8,128)} %constant_dynamic-update-slice_fusion), channel_id=1, source_target_pairs={{0,128},{1,385},{128,0},{129,257},{256,384},{257,129},{384,256},{3... | collective-permute-start | bytes 3575816 | tf_op jit(solution)/shard_map/ppermute | solution.py:32
  61.3 0.0 collective-permute-done.5.refs_3_
  61.3 0.0 copy-done.1
  61.4 4.0 %shard_map.74 = (bf16[896,1024]{1,0:T(8,128)(2,1)S(1)}, bf16[896,1024]{1,0:T(8,128)(2,1)S(1)}) custom-call(f32[776,128]{1,0:T(8,128)S(1)} %copy-done.1, f32[776,128]{1,0:T(8,128)S(1)} %collective-permute-done.refs_1_, f32[776,128]{1,0:T(8,128)S(1)} %collective-permute-done.1.refs_2_, f32[1552,128]{1,0:T(8,128)S(1)} %collective-permute-done.3.refs_3_, ...), custom_call_target="tpu_custom_call" | custom-call | flops 1000000000 | bytes 16777216 | tf_op jit(solution)/shard_map/pallas_call | solution.py:334
  65.4 0.0 copy-start.4
  65.4 1.3 copy-done.4
  66.6 0.0 copy-start.2
  66.7 1.1 pad_maximum_fusion
  67.8 2.3 %collective-permute-start.6 = (f32[2080,128]{1,0:T(8,128)}, f32[2080,128]{1,0:T(8,128)}, u32[]{:S(2)}, u32[]{:S(2)}) collective-permute-start(f32[2080,128]{1,0:T(8,128)} %pad_maximum_fusion), channel_id=1, source_target_pairs={{0,4},{1,29},{4,0},{5,9},{8,12},{9,5},{12,8},{13,17},{16,20},{17,1... | collective-permute-start | bytes 3194888 | tf_op jit(solution)/shard_map/ppermute | solution.py:46
  70.1 3.6 %collective-permute-start.8 = (f32[2328,128]{1,0:T(8,128)}, f32[2328,128]{1,0:T(8,128)}, u32[]{:S(2)}, u32[]{:S(2)}) collective-permute-start(f32[2328,128]{1,0:T(8,128)} %constant_dynamic-update-slice_fusion), channel_id=1, source_target_pairs={{0,384},{1,129},{128,256},{129,1},{256,128},{257,385},{384,0},{385... | collective-permute-start | bytes 3575816 | tf_op jit(solution)/shard_map/ppermute | solution.py:32
  73.7 8.4 %collective-permute-done.7.refs_3_ = f32[2328,128]{1,0:T(8,128)S(1)} collective-permute-done((f32[2328,128]{1,0:T(8,128)}, f32[2328,128]{1,0:T(8,128)S(1)}, u32[]{:S(2)}, u32[]{:S(2)}) %collective-permute-start.7) | collective-permute-done | bytes 1191968 | tf_op jit(solution)/shard_map/ppermute | solution.py:32
  82.1 0.0 copy-done.2
  82.1 7.0 %collective-permute-start.9 = (f32[2328,128]{1,0:T(8,128)S(1)}, f32[2328,128]{1,0:T(8,128)S(1)}, u32[]{:S(2)}, u32[]{:S(2)}) collective-permute-start(f32[2328,128]{1,0:T(8,128)S(1)} %collective-permute-done.7.refs_3_), channel_id=1, source_target_pairs={{0,384},{1,129},{128,256},{129,1},{256,128},{257,385},{384,0},{385... | collective-permute-start | bytes 3575816 | tf_op jit(solution)/shard_map/ppermute | solution.py:32
  89.1 0.0 copy-done.6
  89.1 0.1 concatenate.18.refs_0_
  89.2 0.0 collective-permute-done.6.refs_4_
  89.2 0.0 copy-start.3
  89.2 1.5 %copy-done.3 = bf16[896,1024]{1,0:T(8,128)(2,1)S(1)} copy-done((bf16[896,1024]{1,0:T(8,128)(2,1)S(1)}, bf16[896,1024]{1,0:T(8,128)(2,1)}, u32[]{:S(2)}) %copy-start.3) | copy-done | bytes 1835032
  90.7 1.5 %copy-done.5 = bf16[896,1024]{1,0:T(8,128)(2,1)S(1)} copy-done((bf16[896,1024]{1,0:T(8,128)(2,1)S(1)}, bf16[896,1024]{1,0:T(8,128)(2,1)}, u32[]{:S(2)}) %copy-start.5) | copy-done | bytes 1835032
  92.2 9.7 %shard_map.75 = (bf16[512,2048]{1,0:T(8,128)(2,1)S(1)}, bf16[512,2048]{1,0:T(8,128)(2,1)S(1)}, f32[512,1024]{1,0:T(8,128)S(1)}) custom-call(s32[149]{0:T(256)S(1)} %concatenate.18.refs_0_, f32[520,128]{1,0:T(8,128)S(1)} %copy-done, f32[520,128]{1,0:T(8,128)S(1)} %collective-permute-done.2.refs_2_, f32[1040,128]{1,0:T(8,128)S(1)} %collective-permute-done.5.refs_3_, ...), custom_call_target="tpu_custom_call" | custom-call | flops 2818572288 | bytes 16777216 | tf_op jit(solution)/shard_map/pallas_call | solution.py:347
  101.9 0.0 collective-permute-done.8.refs_4_
  101.9 6.7 %shard_map.76.refs_2_ = f32[512,1024]{1,0:T(8,128)S(1)} custom-call(bf16[512,2048]{1,0:T(8,128)(2,1)S(1)} %get-tuple-element.39.refs_0_, bf16[512,2048]{1,0:T(8,128)(2,1)S(1)} %get-tuple-element.40.refs_1_, f32[512,1024]{1,0:T(8,128)S(1)} %get-tuple-element.41.refs_2_, f32[2328,128]{1,0:T(8,128)S(1)} %collective-permute-done.7.refs_3_, ...), custom_call_target="tpu_custom_call" | custom-call | flops 2415919104 | bytes 16777216 | tf_op jit(solution)/shard_map/pallas_call | solution.py:372
  108.6 0.0 collective-permute-done.9.refs_3_
  108.6 3.5 %shard_map.77 = (f32[256,1024]{1,0:T(8,128)S(1)}, f32[128,1024]{1,0:T(8,128)S(1)}, f32[128,1024]{1,0:T(8,128)S(1)}) custom-call(bf16[512,2048]{1,0:T(8,128)(2,1)S(1)} %get-tuple-element.39.refs_0_, bf16[512,2048]{1,0:T(8,128)(2,1)S(1)} %get-tuple-element.40.refs_1_, f32[512,1024]{1,0:T(8,128)S(1)} %shard_map.76.refs_2_, ...), custom_call_target="tpu_custom_call" | custom-call | flops 1207959552 | bytes 16777216 | tf_op jit(solution)/shard_map/pallas_call | solution.py:391
  112.1 1.9 %collective-permute-start.10 = (f32[256,1024]{1,0:T(8,128)S(1)}, f32[256,1024]{1,0:T(8,128)S(1)}, u32[]{:S(2)}, u32[]{:S(2)}) collective-permute-start(f32[256,1024]{1,0:T(8,128)S(1)} %get-tuple-element.43), channel_id=1, source_target_pairs={{0,1},{1,0},{2,3},{3,2},{4,5},{5,4},{6,7},{7,6},{8,9},{9,8},{10,11... | collective-permute-start | bytes 3145736 | tf_op jit(solution)/shard_map/ppermute | solution.py:67
  114.0 2.6 %collective-permute-done.10 = f32[256,1024]{1,0:T(8,128)S(1)} collective-permute-done((f32[256,1024]{1,0:T(8,128)S(1)}, f32[256,1024]{1,0:T(8,128)S(1)}, u32[]{:S(2)}, u32[]{:S(2)}) %collective-permute-start.10) | collective-permute-done | bytes 1048608 | tf_op jit(solution)/shard_map/ppermute | solution.py:67
  116.7 0.1 slice_add_fusion
  116.7 1.9 %collective-permute-start.11 = (f32[128,1024]{1,0:T(8,128)S(1)}, f32[128,1024]{1,0:T(8,128)S(1)}, u32[]{:S(2)}, u32[]{:S(2)}) collective-permute-start(f32[128,1024]{1,0:T(8,128)S(1)} %slice_add_fusion), channel_id=1, source_target_pairs={{0,2},{2,0},{1,3},{3,1},{4,6},{6,4},{5,7},{7,5},{8,10},{10,8},{9,1... | collective-permute-start | bytes 1572872 | tf_op jit(solution)/shard_map/ppermute | solution.py:67
  118.7 13.9 %collective-permute-done.11 = f32[128,1024]{1,0:T(8,128)S(1)} collective-permute-done((f32[128,1024]{1,0:T(8,128)S(1)}, f32[128,1024]{1,0:T(8,128)S(1)}, u32[]{:S(2)}, u32[]{:S(2)}) %collective-permute-start.11) | collective-permute-done | bytes 524320 | tf_op jit(solution)/shard_map/ppermute | solution.py:67
  132.6 0.9 fusion
  (3 shorter events, 0.0 us)
Async XLA Ops:
  2.9 21.6 %collective-permute-start = (f32[776,128]{1,0:T(8,128)}, f32[776,128]{1,0:T(8,128)S(1)}, u32[]{:S(2)}, u32[]{:S(2)}) collective-permute-start(f32[776,128]{1,0:T(8,128)} %get-tuple-element.26.refs_0_), channel_id=1, source_target_pairs={{0,32},{1,97},{32,0},{33,65},{64,96},{65,33},{96,64},{97,1},{2,34}... | collective-permute-start | bytes 1191944 | tf_op jit(solution)/shard_map/ppermute | solution.py:32
  9.0 15.5 %collective-permute-start.1 = (f32[776,128]{1,0:T(8,128)}, f32[776,128]{1,0:T(8,128)S(1)}, u32[]{:S(2)}, u32[]{:S(2)}) collective-permute-start(f32[776,128]{1,0:T(8,128)} %get-tuple-element.26.refs_0_), channel_id=1, source_target_pairs={{0,128},{1,385},{128,0},{129,257},{256,384},{257,129},{384,256},{3... | collective-permute-start | bytes 1191944 | tf_op jit(solution)/shard_map/ppermute | solution.py:32
  11.7 32.0 %copy-start = (f32[520,128]{1,0:T(8,128)S(1)}, f32[520,128]{1,0:T(8,128)}, u32[]{:S(2)}) copy-start(f32[520,128]{1,0:T(8,128)} %get-tuple-element.25.refs_1_) | copy-start | bytes 798724
  11.7 12.8 %collective-permute-start.2 = (f32[520,128]{1,0:T(8,128)}, f32[520,128]{1,0:T(8,128)S(1)}, u32[]{:S(2)}, u32[]{:S(2)}) collective-permute-start(f32[520,128]{1,0:T(8,128)} %get-tuple-element.25.refs_1_), channel_id=1, source_target_pairs={{0,16},{1,17},{4,20},{5,21},{8,24},{9,25},{12,28},{13,29},{16,0},{... | collective-permute-start | bytes 798728 | tf_op jit(solution)/shard_map/ppermute | solution.py:46
  25.6 32.0 %collective-permute-start.3 = (f32[1552,128]{1,0:T(8,128)S(1)}, f32[1552,128]{1,0:T(8,128)S(1)}, u32[]{:S(2)}, u32[]{:S(2)}) collective-permute-start(f32[1552,128]{1,0:T(8,128)S(1)} %get-tuple-element.46), channel_id=1, source_target_pairs={{0,96},{1,33},{32,64},{33,1},{64,32},{65,97},{96,0},{97,65},{2,98}... | collective-permute-start | bytes 2383880 | tf_op jit(solution)/shard_map/ppermute | solution.py:32
  39.0 18.6 %collective-permute-start.4 = (f32[1552,128]{1,0:T(8,128)S(1)}, f32[1552,128]{1,0:T(8,128)S(1)}, u32[]{:S(2)}, u32[]{:S(2)}) collective-permute-start(f32[1552,128]{1,0:T(8,128)S(1)} %get-tuple-element.45), channel_id=1, source_target_pairs={{0,384},{1,129},{128,256},{129,1},{256,128},{257,385},{384,0},{385... | collective-permute-start | bytes 2383880 | tf_op jit(solution)/shard_map/ppermute | solution.py:32
  43.7 17.6 %copy-start.1 = (f32[776,128]{1,0:T(8,128)S(1)}, f32[776,128]{1,0:T(8,128)}, u32[]{:S(2)}) copy-start(f32[776,128]{1,0:T(8,128)} %get-tuple-element.26.refs_0_) | copy-start | bytes 1191940
  43.7 17.6 %collective-permute-start.5 = (f32[1040,128]{1,0:T(8,128)S(1)}, f32[1040,128]{1,0:T(8,128)S(1)}, u32[]{:S(2)}, u32[]{:S(2)}) collective-permute-start(f32[1040,128]{1,0:T(8,128)S(1)} %pad_maximum_fusion.3), channel_id=1, source_target_pairs={{0,8},{1,25},{4,28},{5,13},{8,0},{9,17},{12,20},{13,5},{16,24},{17... | collective-permute-start | bytes 1597448 | tf_op jit(solution)/shard_map/ppermute | solution.py:46
  58.5 23.5 %collective-permute-start.7 = (f32[2328,128]{1,0:T(8,128)}, f32[2328,128]{1,0:T(8,128)S(1)}, u32[]{:S(2)}, u32[]{:S(2)}) collective-permute-start(f32[2328,128]{1,0:T(8,128)} %constant_dynamic-update-slice_fusion), channel_id=1, source_target_pairs={{0,128},{1,385},{128,0},{129,257},{256,384},{257,129},{384,256},{3... | collective-permute-start | bytes 3575816 | tf_op jit(solution)/shard_map/ppermute | solution.py:32
  65.4 1.3 copy-start.4
  66.6 15.4 %copy-start.2 = (bf16[896,1024]{1,0:T(8,128)(2,1)}, bf16[896,1024]{1,0:T(8,128)(2,1)S(1)}, u32[]{:S(2)}) copy-start(bf16[896,1024]{1,0:T(8,128)(2,1)S(1)} %get-tuple-element.37.refs_5_) | copy-start | bytes 5505028
  66.7 22.4 %copy-start.6 = (s32[144]{0:T(256)S(1)}, s32[144]{0:T(256)}, u32[]{:S(2)}) copy-start(s32[144]{0:T(256)} %constant.22.clone) | copy-start | bytes 1732
  67.8 21.4 %collective-permute-start.6 = (f32[2080,128]{1,0:T(8,128)}, f32[2080,128]{1,0:T(8,128)}, u32[]{:S(2)}, u32[]{:S(2)}) collective-permute-start(f32[2080,128]{1,0:T(8,128)} %pad_maximum_fusion), channel_id=1, source_target_pairs={{0,4},{1,29},{4,0},{5,9},{8,12},{9,5},{12,8},{13,17},{16,20},{17,1... | collective-permute-start | bytes 3194888 | tf_op jit(solution)/shard_map/ppermute | solution.py:46
  70.1 31.8 %collective-permute-start.8 = (f32[2328,128]{1,0:T(8,128)}, f32[2328,128]{1,0:T(8,128)}, u32[]{:S(2)}, u32[]{:S(2)}) collective-permute-start(f32[2328,128]{1,0:T(8,128)} %constant_dynamic-update-slice_fusion), channel_id=1, source_target_pairs={{0,384},{1,129},{128,256},{129,1},{256,128},{257,385},{384,0},{385... | collective-permute-start | bytes 3575816 | tf_op jit(solution)/shard_map/ppermute | solution.py:32
  82.1 26.5 %collective-permute-start.9 = (f32[2328,128]{1,0:T(8,128)S(1)}, f32[2328,128]{1,0:T(8,128)S(1)}, u32[]{:S(2)}, u32[]{:S(2)}) collective-permute-start(f32[2328,128]{1,0:T(8,128)S(1)} %collective-permute-done.7.refs_3_), channel_id=1, source_target_pairs={{0,384},{1,129},{128,256},{129,1},{256,128},{257,385},{384,0},{385... | collective-permute-start | bytes 3575816 | tf_op jit(solution)/shard_map/ppermute | solution.py:32
  89.2 1.5 %copy-start.3 = (bf16[896,1024]{1,0:T(8,128)(2,1)S(1)}, bf16[896,1024]{1,0:T(8,128)(2,1)}, u32[]{:S(2)}) copy-start(bf16[896,1024]{1,0:T(8,128)(2,1)} %copy-done.2) | copy-start | bytes 5505028
  90.7 1.5 %copy-start.5 = (bf16[896,1024]{1,0:T(8,128)(2,1)S(1)}, bf16[896,1024]{1,0:T(8,128)(2,1)}, u32[]{:S(2)}) copy-start(bf16[896,1024]{1,0:T(8,128)(2,1)} %copy-done.4) | copy-start | bytes 5505028
  112.1 4.6 %collective-permute-start.10 = (f32[256,1024]{1,0:T(8,128)S(1)}, f32[256,1024]{1,0:T(8,128)S(1)}, u32[]{:S(2)}, u32[]{:S(2)}) collective-permute-start(f32[256,1024]{1,0:T(8,128)S(1)} %get-tuple-element.43), channel_id=1, source_target_pairs={{0,1},{1,0},{2,3},{3,2},{4,5},{5,4},{6,7},{7,6},{8,9},{9,8},{10,11... | collective-permute-start | bytes 3145736 | tf_op jit(solution)/shard_map/ppermute | solution.py:67
  116.7 15.9 %collective-permute-start.11 = (f32[128,1024]{1,0:T(8,128)S(1)}, f32[128,1024]{1,0:T(8,128)S(1)}, u32[]{:S(2)}, u32[]{:S(2)}) collective-permute-start(f32[128,1024]{1,0:T(8,128)S(1)} %slice_add_fusion), channel_id=1, source_target_pairs={{0,2},{2,0},{1,3},{3,1},{4,6},{6,4},{5,7},{7,5},{8,10},{10,8},{9,1... | collective-permute-start | bytes 1572872 | tf_op jit(solution)/shard_map/ppermute | solution.py:67

commit v3 on v2

--- a/solution.py
+++ b/solution.py
@@ -20,8 +20,9 @@
 WHERE = pl.BlockSpec(memory_space=pl.ANY)
 IN_VMEM = pl.BlockSpec(memory_space=pltpu.VMEM)
 BIG = 56 * 1024 * 1024
-EARLY = 20 * 1024 * 1024
 FIRST = 20 * 1024 * 1024
+MIDDLE = 24 * 1024 * 1024
+LAST = 16 * 1024 * 1024
 IN_HBM = pl.BlockSpec(memory_space=pltpu.HBM)
 IN_SMEM = pl.BlockSpec(memory_space=pltpu.SMEM)
 
@@ -128,8 +129,10 @@
 
 
 HELD = ((0,), (4,), (1,), (8, 12), (2, 3), (5, 9, 13), (6, 10, 14), (7, 11, 15))
-CALLS = ((0, 4, 1, 8, 12, 2, 3), (5, 9, 13, 6, 10, 14), (7, 11, 15))
-ORDER = sum(CALLS, ())
+CALLS = ((0, 1, 12, 2, 3), (13, 14, 4, 8, 5, 9, 6, 10), (15, 7, 11))
+NEAR = (0, 1, 12, 2, 3, 13, 14, 15)
+LATE = CALLS[1] + CALLS[2]
+FIRST_DEPTH, MIDDLE_DEPTH, LAST_DEPTH = (len(tiles) * LANES for tiles in CALLS)
 
 
 def block_pair(load, left, right):
@@ -152,13 +155,13 @@
     return jnp.where(mask == 0, 0, jnp.where(mask == 2, 3, near))
 
 
-def place_left(me_ref, a_f, spots_s, a_hi, a_lo):
+def place_left(me_ref, first, a_f, spots_s, a_hi, a_lo):
     x, zh, col, zl, core = (me_ref[k] for k in range(5))
 
     def left_tile(index, _):
         source = index // 2
         slot = index % 2
-        holder = me_ref[5 + PIECES + (2 * col + core) * 8 + source]
+        holder = me_ref[5 + PIECES + (2 * col + core) * 8 + first + source]
         owner = (4 * x + zh + holder + 8 * slot + PIECES - col) % PIECES
         dx = ring_place((owner // 4) ^ x, core)
         dz = ring_place((owner % 4) ^ zh, core)
@@ -177,14 +180,16 @@
             a_hi[rows, lanes], a_lo[rows, lanes] = halves(block_pair(load, left, right))
         return 0
 
-    lax.fori_loop(0, 16, left_tile, 0)
+    lax.fori_loop(0, 8, left_tile, 0)
 
 
 def right_copies(call, b_in, b_f, spots_s, sem_b, sem_s):
     tiles = CALLS[call]
     copies, spots = [], []
-    for source, held in zip(b_in, [held for held in HELD if held[0] in tiles], strict=True):
+    for source, held in zip(b_in, [held for held in HELD if set(held) & set(tiles)], strict=True):
         for k, tile in enumerate(held):
+            if tile not in tiles:
+                continue
             at = tiles.index(tile)
             rows = pl.ds(k * B_ROWS, B_ROWS)
             copies.append(pltpu.make_async_copy(source.at[rows], b_f.at[at], sem_b.at[at]))
@@ -211,8 +216,12 @@
     lax.fori_loop(0, tiles, right_tile, 0)
 
 
-def first_lane(call):
-    return sum(len(tiles) for tiles in CALLS[:call]) * LANES
+def left_copies(parts, a_f, spots_s, sem_a, sem_s):
+    copies, spots = [], []
+    for n, (part, k) in enumerate([(part, k) for part in parts for k in range(part.shape[0] // A_ROWS)]):
+        copies.append(pltpu.make_async_copy(part.at[pl.ds(k * A_ROWS, A_ROWS)], a_f.at[n], sem_a.at[n]))
+        spots.append(pltpu.make_async_copy(part.at[k * A_ROWS + A_DATA], spots_s.at[n], sem_s.at[n]))
+    return copies, spots
 
 
 def partial_product(left_hi, left_lo, b_hi, b_lo, store):
@@ -237,63 +246,63 @@
 
 
 def first_kernel(*refs):
-    me_ref, a_in, b_in = refs[0], refs[1:5], refs[5:7]
-    a_hi, a_lo, c_ref = refs[7:10]
-    a_f, spots_a, sem_a, sem_sa, b_hi, b_lo, sem_b = refs[10:]
-    parts = [(part, k) for part in a_in for k in range(part.shape[0] // A_ROWS)]
-    copies_a, spots_of_a = [], []
-    for n, (part, k) in enumerate(parts):
-        rows = pl.ds(k * A_ROWS, A_ROWS)
-        copies_a.append(pltpu.make_async_copy(part.at[rows], a_f.at[n], sem_a.at[n]))
-        spots_of_a.append(pltpu.make_async_copy(part.at[k * A_ROWS + A_DATA], spots_a.at[n], sem_sa.at[n]))
+    me_ref, a_in, b_in = refs[0], refs[1:4], refs[4:6]
+    near_hi, near_lo, c_out = refs[6:9]
+    a_f, spots_a, sem_a, sem_sa, b_hi, b_lo, sem_b = refs[9:]
+    copies_a, spots_of_a = left_copies(a_in, a_f, spots_a, sem_a, sem_sa)
     copies = [pltpu.make_async_copy(b_in[k], (b_hi, b_lo)[k], sem_b.at[k]) for k in range(2)]
     for copy in spots_of_a + copies_a + copies:
         copy.start()
     for copy in spots_of_a + copies_a:
         copy.wait()
-    place_left(me_ref, a_f, spots_a, a_hi, a_lo)
+    place_left(me_ref, 0, a_f, spots_a, near_hi, near_lo)
     for copy in copies:
         copy.wait()
 
     def store(lanes, total):
-        c_ref[:, lanes] = total
-
-    depth = len(CALLS[0]) * LANES
-    partial_product(a_hi[:, :depth], a_lo[:, :depth], b_hi, b_lo, store)
-
-
-def middle_kernel(call, n_right, *refs):
-    a_in, c_in = refs[:2], refs[2]
-    b_in = refs[3 : 3 + n_right]
-    c_out, a_hi, a_lo, c_held, sem_a, b_f, b_hi, b_lo, spots_b, sem_b, sem_s = refs[3 + n_right :]
-    copies, spots = right_copies(call, b_in, b_f, spots_b, sem_b, sem_s)
-    lanes = pl.ds(first_lane(call), len(CALLS[call]) * LANES)
-    held = [pltpu.make_async_copy(a_in[k].at[:, lanes], (a_hi, a_lo)[k], sem_a.at[k]) for k in range(2)]
-    held.append(pltpu.make_async_copy(c_in, c_held, sem_a.at[2]))
-    for copy in spots + copies + held:
+        c_out[:, lanes] = total
+
+    partial_product(near_hi[:, :FIRST_DEPTH], near_lo[:, :FIRST_DEPTH], b_hi, b_lo, store)
+
+
+def middle_kernel(n_right, *refs):
+    me_ref, a_in, near, c_in, b_in = refs[0], refs[1], refs[2:4], refs[4], refs[5 : 5 + n_right]
+    late_hi, late_lo, c_out = refs[5 + n_right : 8 + n_right]
+    a_f, spots_a, sem_a, sem_sa, c_held, sem_c, b_f, b_hi, b_lo, spots_b, sem_b, sem_s = refs[8 + n_right :]
+    copies_a, spots_of_a = left_copies((a_in,), a_f, spots_a, sem_a, sem_sa)
+    copies, spots = right_copies(1, b_in, b_f, spots_b, sem_b, sem_s)
+    held = [pltpu.make_async_copy(c_in, c_held, sem_c.at[0])]
+    for k, late in enumerate((late_hi, late_lo)):
+        for n, (first, at, lanes) in enumerate(((FIRST_DEPTH, 0, 256), (FIRST_DEPTH + 256, MIDDLE_DEPTH, 128))):
+            source = near[k].at[:, pl.ds(first, lanes)]
+            held.append(pltpu.make_async_copy(source, late.at[:, pl.ds(at, lanes)], sem_c.at[1 + 2 * k + n]))
+    for copy in spots_of_a + copies_a + spots + copies + held:
         copy.start()
+    for copy in spots_of_a + copies_a:
+        copy.wait()
+    place_left(me_ref, 4, a_f, spots_a, late_hi, late_lo)
     for copy in spots + copies:
         copy.wait()
-    place_right(len(CALLS[call]), b_f, spots_b, b_hi, b_lo)
+    place_right(len(CALLS[1]), b_f, spots_b, b_hi, b_lo)
     for copy in held:
         copy.wait()
 
     def store(lanes, total):
         c_out[:, lanes] = total + c_held[:, lanes]
 
-    partial_product(a_hi[...], a_lo[...], b_hi, b_lo, store)
-
-
-def last_kernel(call, n_right, *refs):
-    a_hi, a_lo, c_in = refs[:3]
+    partial_product(late_hi[:, :MIDDLE_DEPTH], late_lo[:, :MIDDLE_DEPTH], b_hi, b_lo, store)
+
+
+def last_kernel(n_right, *refs):
+    late_hi, late_lo, c_in = refs[:3]
     b_in = refs[3 : 3 + n_right]
     other, send, keep, b_f, b_hi, b_lo, spots_b, sem_b, sem_s = refs[3 + n_right :]
-    copies, spots = right_copies(call, b_in, b_f, spots_b, sem_b, sem_s)
+    copies, spots = right_copies(2, b_in, b_f, spots_b, sem_b, sem_s)
     for copy in spots + copies:
         copy.start()
     for copy in spots + copies:
         copy.wait()
-    place_right(len(CALLS[call]), b_f, spots_b, b_hi, b_lo)
+    place_right(len(CALLS[2]), b_f, spots_b, b_hi, b_lo)
 
     def store(lanes, total):
         total += c_in[:, lanes]
@@ -301,9 +310,7 @@
         send[:, lanes] = total[256:384]
         keep[:, lanes] = total[384:]
 
-    first = first_lane(call)
-    depth = len(CALLS[call]) * LANES
-    partial_product(a_hi[:, first : first + depth], a_lo[:, first : first + depth], b_hi, b_lo, store)
+    partial_product(late_hi[:, MIDDLE_DEPTH:], late_lo[:, MIDDLE_DEPTH:], b_hi, b_lo, store)
 
 
 def right_scratch(call):
@@ -319,7 +326,7 @@
 
 
 def used_by(call, b_all):
-    return [b_all[k] for k in range(len(HELD)) if HELD[k][0] in CALLS[call]]
+    return [b_all[k] for k in range(len(HELD)) if set(HELD[k]) & set(CALLS[call])]
 
 
 def cost(call):
@@ -327,83 +334,79 @@
     return pl.CostEstimate(flops=flops, bytes_accessed=16 * 1024 * 1024, transcendentals=0)
 
 
+LEFT_SCRATCH = (
+    pltpu.VMEM((4, A_ROWS, LANES), jnp.float32),
+    pltpu.SMEM((4, LANES), jnp.float32),
+    pltpu.SemaphoreType.DMA((4,)),
+    pltpu.SemaphoreType.DMA((4,)),
+)
+
+
 def early_right(b_all):
     operands = used_by(0, b_all)
-    depth = len(CALLS[0]) * LANES
+    dense = jax.ShapeDtypeStruct((FIRST_DEPTH, 1024), jnp.bfloat16)
     scratch = right_scratch(0)
     return pl.pallas_call(
         lambda *refs: early_kernel(len(operands), *refs),
-        out_shape=(jax.ShapeDtypeStruct((depth, 1024), jnp.bfloat16),) * 2,
+        out_shape=(dense, dense),
         in_specs=[WHERE] * len(operands),
         out_specs=(IN_VMEM,) * 2,
         scratch_shapes=scratch[:1] + scratch[3:],
-        compiler_params=pltpu.CompilerParams(vmem_limit_bytes=EARLY),
+        compiler_params=pltpu.CompilerParams(vmem_limit_bytes=FIRST),
         cost_estimate=pl.CostEstimate(flops=10**9, bytes_accessed=16 * 1024 * 1024, transcendentals=0),
     )(*operands)
 
 
-def first_product(me, a_all, right):
-    depth = PIECES * LANES
+def first_product(me, a_near, right):
+    near = jax.ShapeDtypeStruct((512, len(NEAR) * LANES), jnp.bfloat16)
     return pl.pallas_call(
         first_kernel,
-        out_shape=(
-            jax.ShapeDtypeStruct((512, depth), jnp.bfloat16),
-            jax.ShapeDtypeStruct((512, depth), jnp.bfloat16),
-            jax.ShapeDtypeStruct((512, 1024), jnp.float32),
-        ),
-        in_specs=[IN_SMEM] + [WHERE] * 6,
+        out_shape=(near, near, jax.ShapeDtypeStruct((512, 1024), jnp.float32)),
+        in_specs=[IN_SMEM] + [WHERE] * 5,
+        out_specs=(IN_VMEM,) * 3,
+        scratch_shapes=[*LEFT_SCRATCH, *right_scratch(0)[1:3], pltpu.SemaphoreType.DMA((2,))],
+        compiler_params=pltpu.CompilerParams(vmem_limit_bytes=FIRST),
+        cost_estimate=cost(0),
+    )(me, *a_near, *right)
+
+
+def middle_product(me, a_far, near_hi, near_lo, so_far, b_all):
+    operands = used_by(1, b_all)
+    late = jax.ShapeDtypeStruct((512, len(LATE) * LANES), jnp.bfloat16)
+    return pl.pallas_call(
+        lambda *refs: middle_kernel(len(operands), *refs),
+        out_shape=(late, late, jax.ShapeDtypeStruct((512, 1024), jnp.float32)),
+        in_specs=[IN_SMEM] + [WHERE] * (4 + len(operands)),
         out_specs=(IN_VMEM,) * 3,
         scratch_shapes=[
-            pltpu.VMEM((8, A_ROWS, LANES), jnp.float32),
-            pltpu.SMEM((8, LANES), jnp.float32),
-            pltpu.SemaphoreType.DMA((8,)),
-            pltpu.SemaphoreType.DMA((8,)),
-        ]
-        + right_scratch(0)[1:3]
-        + [pltpu.SemaphoreType.DMA((2,))],
-        compiler_params=pltpu.CompilerParams(vmem_limit_bytes=FIRST),
-        cost_estimate=cost(0),
-    )(me, *a_all, *right)
-
-
-def middle_product(call, a_hi, a_lo, so_far, b_all, limit):
-    operands = used_by(call, b_all)
-    depth = len(CALLS[call]) * LANES
+            *LEFT_SCRATCH,
+            pltpu.VMEM((512, 1024), jnp.float32),
+            pltpu.SemaphoreType.DMA((5,)),
+            *right_scratch(1),
+        ],
+        compiler_params=pltpu.CompilerParams(vmem_limit_bytes=MIDDLE),
+        cost_estimate=cost(1),
+    )(me, a_far, near_hi, near_lo, so_far, *operands)
+
+
+def last_product(late_hi, late_lo, so_far, b_all):
+    operands = used_by(2, b_all)
     return pl.pallas_call(
-        lambda *refs: middle_kernel(call, len(operands), *refs),
-        out_shape=jax.ShapeDtypeStruct((512, 1024), jnp.float32),
-        in_specs=[WHERE] * (3 + len(operands)),
-        out_specs=IN_VMEM,
-        scratch_shapes=[
-            pltpu.VMEM((512, depth), jnp.bfloat16),
-            pltpu.VMEM((512, depth), jnp.bfloat16),
-            pltpu.VMEM((512, 1024), jnp.float32),
-            pltpu.SemaphoreType.DMA((3,)),
-        ]
-        + right_scratch(call),
-        compiler_params=pltpu.CompilerParams(vmem_limit_bytes=limit),
-        cost_estimate=cost(call),
-    )(a_hi, a_lo, so_far, *operands)
-
-
-def last_product(call, a_hi, a_lo, so_far, b_all):
-    operands = used_by(call, b_all)
-    return pl.pallas_call(
-        lambda *refs: last_kernel(call, len(operands), *refs),
+        lambda *refs: last_kernel(len(operands), *refs),
         out_shape=tuple(jax.ShapeDtypeStruct((rows, 1024), jnp.float32) for rows in (256, 128, 128)),
         in_specs=[IN_VMEM] * 3 + [WHERE] * len(operands),
         out_specs=(IN_VMEM,) * 3,
-        scratch_shapes=right_scratch(call),
-        compiler_params=pltpu.CompilerParams(vmem_limit_bytes=16 * 1024 * 1024),
-        cost_estimate=cost(call),
-    )(a_hi, a_lo, so_far, *operands)
+        scratch_shapes=right_scratch(2),
+        compiler_params=pltpu.CompilerParams(vmem_limit_bytes=LAST),
+        cost_estimate=cost(2),
+    )(late_hi, late_lo, so_far, *operands)
 
 
 def body(a_values, a_places, a_counts, b_values, b_places, b_counts):
     hold = lax.optimization_barrier
     by_place = [holder for place in range(8) for core in range(2) for holder in holders(place, core)]
     me = [lax.axis_index(name) for name in ("x", "zh", "col", "zl", "core")]
-    table = jnp.array([ORDER.index(tile) for tile in range(PIECES)] + by_place, jnp.int32)
+    table = jnp.array([(NEAR if tile in NEAR else LATE).index(tile) for tile in range(PIECES)] + by_place, jnp.int32)
     me = jnp.concatenate([jnp.stack(me).astype(jnp.int32), table])
     own_a, own = pack(
         a_counts.reshape(2),
@@ -415,28 +418,27 @@
     )
     z_one = exchange(own, "zh", 0)
     x_one = exchange(own, "x", 0)
+    x_one, z_one, own_a = hold((x_one, z_one, own_a))
     a_one = exchange_col(own_a, 4)
-    z_one, x_one, a_one = hold((z_one, x_one, a_one))
 
     z_two = exchange(jnp.concatenate([own, z_one], axis=0), "zh", 1)
     x_two = exchange(jnp.concatenate([own, x_one], axis=0), "x", 1)
+    x_two, z_two = hold((x_two, z_two))
+    a_one, _ = hold((a_one, z_two))
     a_two = exchange_col(jnp.concatenate([own_a, a_one], axis=0), 2)
-    z_two, x_two = hold((z_two, x_two))
 
     column = jnp.concatenate([z_one, z_two], axis=0)
     x_three = exchange(column, "x", 0)
     x_four = exchange(column, "x", 1)
     b_all = [own, z_one, x_one, z_two, x_two]
-    x_two, a_two = hold((x_two, a_two))
-    b_all = [own, z_one, x_one, z_two, x_two]
-    right_hi, right_lo = early_right(b_all)
-    a_two, right_hi, right_lo = hold((a_two, right_hi, right_lo))
+    right = early_right(b_all)
+    a_two, *right = hold((a_two, *right))
     a_four = exchange_col(jnp.concatenate([own_a, a_one, a_two], axis=0), 1)
-    a_hi, a_lo, total = first_product(me, (own_a, a_one, a_two, a_four), (right_hi, right_lo))
-
+    x_three, a_two = hold((x_three, a_two))
+    near_hi, near_lo, total = first_product(me, (own_a, a_one, a_two), right)
     b_all += [x_three, x_four, exchange(x_three, "x", 1)]
-    total = middle_product(1, a_hi, a_lo, total, b_all, 20 * 1024 * 1024)
-    other, send, keep = last_product(2, a_hi, a_lo, total, b_all)
+    late_hi, late_lo, total = middle_product(me, a_four, near_hi, near_lo, total, b_all)
+    other, send, keep = last_product(late_hi, late_lo, total, b_all)
 
     got = swap(other, "core")
     ahead = swap(send + got[:128], "zl")

time: 134 us -> 128 us (0.955)
  the two profiles are of different devices: /device:TPU:38 before, /device:TPU:56 now
where the time goes in v3:
time: 128 us; the launch traced here: 127 us
  starting transfers between devices  52.1 us (41%)
  waiting for transfers between devices  39.9 us (31%)
  Pallas kernels  24.9 us (19%)
  local copies, waits for them, and re-layouts  5.56 us (4%)
  other arithmetic  3.28 us (3%)
    ppermute x7, starting transfers between devices, exchange(): return lax.ppermute(array, (axis, 'core'), route)  35.4 us
    ppermute x7, waiting for transfers between devices, exchange(): return lax.ppermute(array, (axis, 'core'), route)  16.2 us
    ppermute x2, waiting for transfers between devices, swap(): return lax.ppermute(array, axis, [(0, 1), (1, 0)])  14.8 us
    pallas_call x1, Pallas kernels, middle_product(): pl.pallas_call(lambda *refs: middle_kernel(len(operands), *refs), out_sha...  10.4 us
    ppermute x3, starting transfers between devices, exchange_col(): return lax.ppermute(array, ('col', 'core'), route)  9.1 us
    ppermute x3, waiting for transfers between devices, exchange_col(): return lax.ppermute(array, ('col', 'core'), route)  8.84 us
    ppermute x2, starting transfers between devices, swap(): return lax.ppermute(array, axis, [(0, 1), (1, 0)])  7.61 us
    pallas_call x1, Pallas kernels, first_product(): pl.pallas_call(first_kernel, out_shape=(near, near, jax.ShapeDtypeStruct(...  5.92 us
  transfers between devices with their start and end apart: 12, of which 7 were waited for; matrix products, arithmetic and copies ran while one was open for 2% of the time, Pallas kernels for 15%

profile of v3, /device:TPU:56, one launch (start us, length us, event | category | flops | bytes accessed | tf_op | source)
XLA Modules:
  0.0 126.6 jit_solution(12099466710547400231)
XLA Ops:
  0.7 2.2 %shard_map.73 = (f32[520,128]{1,0:T(8,128)}, f32[776,128]{1,0:T(8,128)}) custom-call(s32[2]{0:T(128)} %bitcast.18, s32[1,1,1]{2,1,0:T(1,128)S(6)} %copy.9.refs_1_, s32[2,2,8]{2,1,0:T(2,128)} %bitcast.16, s32[2,24]{1,0:T(2,128)} %bitcast.17, f32[24,64,64]{2,1,0:T(8,128)} %bitcast.14, f32[16,64,64]{2,1,0:T(8,128)} %bitcast.15), custom_call_target="tpu_custom_call" | custom-call | tf_op jit(solution)/shard_map/pallas_call | solution.py:110
  2.9 6.1 %collective-permute-start.1 = (f32[776,128]{1,0:T(8,128)}, f32[776,128]{1,0:T(8,128)S(1)}, u32[]{:S(2)}, u32[]{:S(2)}) collective-permute-start(f32[776,128]{1,0:T(8,128)} %get-tuple-element.29.refs_0_), channel_id=1, source_target_pairs={{0,32},{1,97},{32,0},{33,65},{64,96},{65,33},{96,64},{97,1},{2,34}... | collective-permute-start | bytes 1191944 | tf_op jit(solution)/shard_map/ppermute | solution.py:33
  9.0 3.4 %collective-permute-start = (f32[776,128]{1,0:T(8,128)}, f32[776,128]{1,0:T(8,128)S(1)}, u32[]{:S(2)}, u32[]{:S(2)}) collective-permute-start(f32[776,128]{1,0:T(8,128)} %get-tuple-element.29.refs_0_), channel_id=1, source_target_pairs={{0,128},{1,385},{128,0},{129,257},{256,384},{257,129},{384,256},{3... | collective-permute-start | bytes 1191944 | tf_op jit(solution)/shard_map/ppermute | solution.py:33
  12.4 6.9 %collective-permute-done.1.refs_5_ = f32[776,128]{1,0:T(8,128)S(1)} collective-permute-done((f32[776,128]{1,0:T(8,128)}, f32[776,128]{1,0:T(8,128)S(1)}, u32[]{:S(2)}, u32[]{:S(2)}) %collective-permute-start.1) | collective-permute-done | bytes 397344 | tf_op jit(solution)/shard_map/ppermute | solution.py:33
  19.3 0.0 collective-permute-done.refs_1_
  19.4 0.0 copy-start
  19.4 1.1 pad_maximum_fusion.1
  20.5 9.6 %collective-permute-start.4 = (f32[1552,128]{1,0:T(8,128)S(1)}, f32[1552,128]{1,0:T(8,128)S(1)}, u32[]{:S(2)}, u32[]{:S(2)}) collective-permute-start(f32[1552,128]{1,0:T(8,128)S(1)} %get-tuple-element.53), channel_id=1, source_target_pairs={{0,96},{1,33},{32,64},{33,1},{64,32},{65,97},{96,0},{97,65},{2,98}... | collective-permute-start | bytes 2383880 | tf_op jit(solution)/shard_map/ppermute | solution.py:33
  30.1 4.7 %collective-permute-start.3 = (f32[1552,128]{1,0:T(8,128)S(1)}, f32[1552,128]{1,0:T(8,128)S(1)}, u32[]{:S(2)}, u32[]{:S(2)}) collective-permute-start(f32[1552,128]{1,0:T(8,128)S(1)} %get-tuple-element.54), channel_id=1, source_target_pairs={{0,384},{1,129},{128,256},{129,1},{256,128},{257,385},{384,0},{385... | collective-permute-start | bytes 2383880 | tf_op jit(solution)/shard_map/ppermute | solution.py:33
  34.8 0.0 copy-done
  34.8 4.7 %collective-permute-start.2 = (f32[520,128]{1,0:T(8,128)S(1)}, f32[520,128]{1,0:T(8,128)S(1)}, u32[]{:S(2)}, u32[]{:S(2)}) collective-permute-start(f32[520,128]{1,0:T(8,128)S(1)} %copy-done), channel_id=1, source_target_pairs={{0,16},{1,17},{4,20},{5,21},{8,24},{9,25},{12,28},{13,29},{16,0},{... | collective-permute-start | bytes 798728 | tf_op jit(solution)/shard_map/ppermute | solution.py:47
  39.5 0.8 constant_dynamic-update-slice_fusion.1
  40.3 0.0 copy-start.1
  40.3 7.3 %collective-permute-done.4.refs_2_.refs_6_ = f32[1552,128]{1,0:T(8,128)S(1)} collective-permute-done((f32[1552,128]{1,0:T(8,128)S(1)}, f32[1552,128]{1,0:T(8,128)S(1)}, u32[]{:S(2)}, u32[]{:S(2)}) %collective-permute-start.4) | collective-permute-done | bytes 794656 | tf_op jit(solution)/shard_map/ppermute | solution.py:33
  47.6 0.0 collective-permute-done.3.refs_3_
  47.6 1.0 constant_dynamic-update-slice_fusion
  48.5 1.3 %collective-permute-done.2.refs_2_ = f32[520,128]{1,0:T(8,128)S(1)} collective-permute-done((f32[520,128]{1,0:T(8,128)S(1)}, f32[520,128]{1,0:T(8,128)S(1)}, u32[]{:S(2)}, u32[]{:S(2)}) %collective-permute-start.2) | collective-permute-done | bytes 266272 | tf_op jit(solution)/shard_map/ppermute | solution.py:47
  49.8 2.3 %collective-permute-start.7 = (f32[2328,128]{1,0:T(8,128)}, f32[2328,128]{1,0:T(8,128)}, u32[]{:S(2)}, u32[]{:S(2)}) collective-permute-start(f32[2328,128]{1,0:T(8,128)} %constant_dynamic-update-slice_fusion), channel_id=1, source_target_pairs={{0,128},{1,385},{128,0},{129,257},{256,384},{257,129},{384,256},{3... | collective-permute-start | bytes 3575816 | tf_op jit(solution)/shard_map/ppermute | solution.py:33
  52.2 2.5 %collective-permute-start.5 = (f32[1040,128]{1,0:T(8,128)S(1)}, f32[1040,128]{1,0:T(8,128)S(1)}, u32[]{:S(2)}, u32[]{:S(2)}) collective-permute-start(f32[1040,128]{1,0:T(8,128)S(1)} %pad_maximum_fusion.3), channel_id=1, source_target_pairs={{0,8},{1,25},{4,28},{5,13},{8,0},{9,17},{12,20},{13,5},{16,24},{17... | collective-permute-start | bytes 1597448 | tf_op jit(solution)/shard_map/ppermute | solution.py:47
  54.7 4.4 %collective-permute-start.8 = (f32[2328,128]{1,0:T(8,128)}, f32[2328,128]{1,0:T(8,128)}, u32[]{:S(2)}, u32[]{:S(2)}) collective-permute-start(f32[2328,128]{1,0:T(8,128)} %constant_dynamic-update-slice_fusion), channel_id=1, source_target_pairs={{0,384},{1,129},{128,256},{129,1},{256,128},{257,385},{384,0},{385... | collective-permute-start | bytes 3575816 | tf_op jit(solution)/shard_map/ppermute | solution.py:33
  59.1 0.0 copy-done.1
  59.1 2.9 %shard_map.74 = (bf16[640,1024]{1,0:T(8,128)(2,1)S(1)}, bf16[640,1024]{1,0:T(8,128)(2,1)S(1)}) custom-call(f32[776,128]{1,0:T(8,128)S(1)} %copy-done.1, f32[776,128]{1,0:T(8,128)S(1)} %collective-permute-done.refs_1_, f32[1552,128]{1,0:T(8,128)S(1)} %collective-permute-done.4.refs_2_.refs_6_, f32[1552,128]{1,0:T(8,128)S(1)} %collective-permute-done.3.refs_3_), custom_call_target="tpu_custom_call" | custom-call | flops 1000000000 | bytes 16777216 | tf_op jit(solution)/shard_map/pallas_call | solution.py:349
  62.0 0.0 copy-start.4
  62.0 1.1 copy-done.4
  63.0 0.0 copy-start.6
  63.0 7.5 %collective-permute-done.5.refs_3_ = f32[1040,128]{1,0:T(8,128)S(1)} collective-permute-done((f32[1040,128]{1,0:T(8,128)S(1)}, f32[1040,128]{1,0:T(8,128)S(1)}, u32[]{:S(2)}, u32[]{:S(2)}) %collective-permute-start.5) | collective-permute-done | bytes 532512 | tf_op jit(solution)/shard_map/ppermute | solution.py:47
  70.6 1.1 pad_maximum_fusion
  71.7 1.9 %collective-permute-start.6 = (f32[2080,128]{1,0:T(8,128)}, f32[2080,128]{1,0:T(8,128)}, u32[]{:S(2)}, u32[]{:S(2)}) collective-permute-start(f32[2080,128]{1,0:T(8,128)} %pad_maximum_fusion), channel_id=1, source_target_pairs={{0,4},{1,29},{4,0},{5,9},{8,12},{9,5},{12,8},{13,17},{16,20},{17,1... | collective-permute-start | bytes 3194888 | tf_op jit(solution)/shard_map/ppermute | solution.py:47
  73.6 0.0 copy-done.2
  73.6 2.0 %collective-permute-done.7.refs_7_ = f32[2328,128]{1,0:T(8,128)} collective-permute-done((f32[2328,128]{1,0:T(8,128)}, f32[2328,128]{1,0:T(8,128)}, u32[]{:S(2)}, u32[]{:S(2)}) %collective-permute-start.7) | collective-permute-done | bytes 1191968 | tf_op jit(solution)/shard_map/ppermute | solution.py:33
  75.6 5.0 %collective-permute-start.9 = (f32[2328,128]{1,0:T(8,128)}, f32[2328,128]{1,0:T(8,128)S(1)}, u32[]{:S(2)}, u32[]{:S(2)}) collective-permute-start(f32[2328,128]{1,0:T(8,128)} %collective-permute-done.7.refs_7_), channel_id=1, source_target_pairs={{0,384},{1,129},{128,256},{129,1},{256,128},{257,385},{384,0},{385... | collective-permute-start | bytes 3575816 | tf_op jit(solution)/shard_map/ppermute | solution.py:33
  80.6 0.0 copy-done.6
  80.6 0.1 concatenate.18.refs_0_
  80.7 1.3 %copy-done.3 = bf16[640,1024]{1,0:T(8,128)(2,1)S(1)} copy-done((bf16[640,1024]{1,0:T(8,128)(2,1)S(1)}, bf16[640,1024]{1,0:T(8,128)(2,1)}, u32[]{:S(2)}) %copy-start.3) | copy-done | bytes 1310744
  82.0 0.0 copy-start.5
  82.0 1.3 %copy-done.5 = bf16[640,1024]{1,0:T(8,128)(2,1)S(1)} copy-done((bf16[640,1024]{1,0:T(8,128)(2,1)S(1)}, bf16[640,1024]{1,0:T(8,128)(2,1)}, u32[]{:S(2)}) %copy-start.5) | copy-done | bytes 1310744
  83.3 5.9 %shard_map.75 = (bf16[512,1024]{1,0:T(8,128)(2,1)S(1)}, bf16[512,1024]{1,0:T(8,128)(2,1)S(1)}, f32[512,1024]{1,0:T(8,128)S(1)}) custom-call(s32[149]{0:T(256)S(1)} %concatenate.18.refs_0_, f32[520,128]{1,0:T(8,128)S(1)} %copy-done, f32[520,128]{1,0:T(8,128)S(1)} %collective-permute-done.2.refs_2_, f32[1040,128]{1,0:T(8,128)S(1)} %collective-permute-done.5.refs_3_, ...), custom_call_target="tpu_custom_call" | custom-call | flops 2013265920 | bytes 16777216 | tf_op jit(solution)/shard_map/pallas_call | solution.py:362
  89.2 0.0 collective-permute-done.8.refs_8_
  89.2 0.0 collective-permute-done.6.refs_1_
  89.3 10.4 %shard_map.76 = (bf16[512,1408]{1,0:T(8,128)(2,1)S(1)}, bf16[512,1408]{1,0:T(8,128)(2,1)S(1)}, f32[512,1024]{1,0:T(8,128)S(1)}) custom-call(s32[149]{0:T(256)S(1)} %concatenate.18.refs_0_, f32[2080,128]{1,0:T(8,128)} %collective-permute-done.6.refs_1_, bf16[512,1024]{1,0:T(8,128)(2,1)S(1)} %get-tuple-element.43.refs_2_, ...), custom_call_target="tpu_custom_call" | custom-call | flops 3221225472 | bytes 16777216 | tf_op jit(solution)/shard_map/pallas_call | solution.py:376
  99.7 0.0 collective-permute-done.9.refs_3_
  99.7 3.5 %shard_map.77 = (f32[256,1024]{1,0:T(8,128)S(1)}, f32[128,1024]{1,0:T(8,128)S(1)}, f32[128,1024]{1,0:T(8,128)S(1)}) custom-call(bf16[512,1408]{1,0:T(8,128)(2,1)S(1)} %get-tuple-element.47.refs_0_, bf16[512,1408]{1,0:T(8,128)(2,1)S(1)} %get-tuple-element.48.refs_1_, f32[512,1024]{1,0:T(8,128)S(1)} %get-tuple-element.49.refs_2_, ...), custom_call_target="tpu_custom_call" | custom-call | flops 1207959552 | bytes 16777216 | tf_op jit(solution)/shard_map/pallas_call | solution.py:394
  103.2 1.9 %collective-permute-start.10 = (f32[256,1024]{1,0:T(8,128)S(1)}, f32[256,1024]{1,0:T(8,128)S(1)}, u32[]{:S(2)}, u32[]{:S(2)}) collective-permute-start(f32[256,1024]{1,0:T(8,128)S(1)} %get-tuple-element.51), channel_id=1, source_target_pairs={{0,1},{1,0},{2,3},{3,2},{4,5},{5,4},{6,7},{7,6},{8,9},{9,8},{10,11... | collective-permute-start | bytes 3145736 | tf_op jit(solution)/shard_map/ppermute | solution.py:68
  105.1 2.6 %collective-permute-done.10 = f32[256,1024]{1,0:T(8,128)S(1)} collective-permute-done((f32[256,1024]{1,0:T(8,128)S(1)}, f32[256,1024]{1,0:T(8,128)S(1)}, u32[]{:S(2)}, u32[]{:S(2)}) %collective-permute-start.10) | collective-permute-done | bytes 1048608 | tf_op jit(solution)/shard_map/ppermute | solution.py:68
  107.8 0.1 slice_add_fusion
  107.8 5.7 %collective-permute-start.11 = (f32[128,1024]{1,0:T(8,128)S(1)}, f32[128,1024]{1,0:T(8,128)S(1)}, u32[]{:S(2)}, u32[]{:S(2)}) collective-permute-start(f32[128,1024]{1,0:T(8,128)S(1)} %slice_add_fusion), channel_id=1, source_target_pairs={{0,2},{2,0},{1,3},{3,1},{4,6},{6,4},{5,7},{7,5},{8,10},{10,8},{9,1... | collective-permute-start | bytes 1572872 | tf_op jit(solution)/shard_map/ppermute | solution.py:68
  113.5 12.2 %collective-permute-done.11 = f32[128,1024]{1,0:T(8,128)S(1)} collective-permute-done((f32[128,1024]{1,0:T(8,128)S(1)}, f32[128,1024]{1,0:T(8,128)S(1)}, u32[]{:S(2)}, u32[]{:S(2)}) %collective-permute-start.11) | collective-permute-done | bytes 524320 | tf_op jit(solution)/shard_map/ppermute | solution.py:68
  125.7 0.9 fusion
  (3 shorter events, 0.0 us)
Async XLA Ops:
  2.9 16.4 %collective-permute-start.1 = (f32[776,128]{1,0:T(8,128)}, f32[776,128]{1,0:T(8,128)S(1)}, u32[]{:S(2)}, u32[]{:S(2)}) collective-permute-start(f32[776,128]{1,0:T(8,128)} %get-tuple-element.29.refs_0_), channel_id=1, source_target_pairs={{0,32},{1,97},{32,0},{33,65},{64,96},{65,33},{96,64},{97,1},{2,34}... | collective-permute-start | bytes 1191944 | tf_op jit(solution)/shard_map/ppermute | solution.py:33
  9.0 10.4 %collective-permute-start = (f32[776,128]{1,0:T(8,128)}, f32[776,128]{1,0:T(8,128)S(1)}, u32[]{:S(2)}, u32[]{:S(2)}) collective-permute-start(f32[776,128]{1,0:T(8,128)} %get-tuple-element.29.refs_0_), channel_id=1, source_target_pairs={{0,128},{1,385},{128,0},{129,257},{256,384},{257,129},{384,256},{3... | collective-permute-start | bytes 1191944 | tf_op jit(solution)/shard_map/ppermute | solution.py:33
  19.4 15.4 %copy-start = (f32[520,128]{1,0:T(8,128)S(1)}, f32[520,128]{1,0:T(8,128)}, u32[]{:S(2)}) copy-start(f32[520,128]{1,0:T(8,128)} %get-tuple-element.31.refs_1_) | copy-start | bytes 798724
  20.5 27.1 %collective-permute-start.4 = (f32[1552,128]{1,0:T(8,128)S(1)}, f32[1552,128]{1,0:T(8,128)S(1)}, u32[]{:S(2)}, u32[]{:S(2)}) collective-permute-start(f32[1552,128]{1,0:T(8,128)S(1)} %get-tuple-element.53), channel_id=1, source_target_pairs={{0,96},{1,33},{32,64},{33,1},{64,32},{65,97},{96,0},{97,65},{2,98}... | collective-permute-start | bytes 2383880 | tf_op jit(solution)/shard_map/ppermute | solution.py:33
  30.1 17.5 %collective-permute-start.3 = (f32[1552,128]{1,0:T(8,128)S(1)}, f32[1552,128]{1,0:T(8,128)S(1)}, u32[]{:S(2)}, u32[]{:S(2)}) collective-permute-start(f32[1552,128]{1,0:T(8,128)S(1)} %get-tuple-element.54), channel_id=1, source_target_pairs={{0,384},{1,129},{128,256},{129,1},{256,128},{257,385},{384,0},{385... | collective-permute-start | bytes 2383880 | tf_op jit(solution)/shard_map/ppermute | solution.py:33
  34.8 15.1 %collective-permute-start.2 = (f32[520,128]{1,0:T(8,128)S(1)}, f32[520,128]{1,0:T(8,128)S(1)}, u32[]{:S(2)}, u32[]{:S(2)}) collective-permute-start(f32[520,128]{1,0:T(8,128)S(1)} %copy-done), channel_id=1, source_target_pairs={{0,16},{1,17},{4,20},{5,21},{8,24},{9,25},{12,28},{13,29},{16,0},{... | collective-permute-start | bytes 798728 | tf_op jit(solution)/shard_map/ppermute | solution.py:47
  40.3 18.8 %copy-start.1 = (f32[776,128]{1,0:T(8,128)S(1)}, f32[776,128]{1,0:T(8,128)}, u32[]{:S(2)}) copy-start(f32[776,128]{1,0:T(8,128)} %get-tuple-element.29.refs_0_) | copy-start | bytes 1191940
  49.8 25.8 %collective-permute-start.7 = (f32[2328,128]{1,0:T(8,128)}, f32[2328,128]{1,0:T(8,128)}, u32[]{:S(2)}, u32[]{:S(2)}) collective-permute-start(f32[2328,128]{1,0:T(8,128)} %constant_dynamic-update-slice_fusion), channel_id=1, source_target_pairs={{0,128},{1,385},{128,0},{129,257},{256,384},{257,129},{384,256},{3... | collective-permute-start | bytes 3575816 | tf_op jit(solution)/shard_map/ppermute | solution.py:33
  52.2 18.4 %collective-permute-start.5 = (f32[1040,128]{1,0:T(8,128)S(1)}, f32[1040,128]{1,0:T(8,128)S(1)}, u32[]{:S(2)}, u32[]{:S(2)}) collective-permute-start(f32[1040,128]{1,0:T(8,128)S(1)} %pad_maximum_fusion.3), channel_id=1, source_target_pairs={{0,8},{1,25},{4,28},{5,13},{8,0},{9,17},{12,20},{13,5},{16,24},{17... | collective-permute-start | bytes 1597448 | tf_op jit(solution)/shard_map/ppermute | solution.py:47
  54.7 34.6 %collective-permute-start.8 = (f32[2328,128]{1,0:T(8,128)}, f32[2328,128]{1,0:T(8,128)}, u32[]{:S(2)}, u32[]{:S(2)}) collective-permute-start(f32[2328,128]{1,0:T(8,128)} %constant_dynamic-update-slice_fusion), channel_id=1, source_target_pairs={{0,384},{1,129},{128,256},{129,1},{256,128},{257,385},{384,0},{385... | collective-permute-start | bytes 3575816 | tf_op jit(solution)/shard_map/ppermute | solution.py:33
  62.0 1.1 copy-start.4
  63.0 10.6 %copy-start.2 = (bf16[640,1024]{1,0:T(8,128)(2,1)}, bf16[640,1024]{1,0:T(8,128)(2,1)S(1)}, u32[]{:S(2)}) copy-start(bf16[640,1024]{1,0:T(8,128)(2,1)S(1)} %get-tuple-element.41.refs_4_) | copy-start | bytes 3932164
  63.0 17.5 %copy-start.6 = (s32[144]{0:T(256)S(1)}, s32[144]{0:T(256)}, u32[]{:S(2)}) copy-start(s32[144]{0:T(256)} %constant.22.clone) | copy-start | bytes 1732
  71.7 17.6 %collective-permute-start.6 = (f32[2080,128]{1,0:T(8,128)}, f32[2080,128]{1,0:T(8,128)}, u32[]{:S(2)}, u32[]{:S(2)}) collective-permute-start(f32[2080,128]{1,0:T(8,128)} %pad_maximum_fusion), channel_id=1, source_target_pairs={{0,4},{1,29},{4,0},{5,9},{8,12},{9,5},{12,8},{13,17},{16,20},{17,1... | collective-permute-start | bytes 3194888 | tf_op jit(solution)/shard_map/ppermute | solution.py:47
  75.6 24.1 %collective-permute-start.9 = (f32[2328,128]{1,0:T(8,128)}, f32[2328,128]{1,0:T(8,128)S(1)}, u32[]{:S(2)}, u32[]{:S(2)}) collective-permute-start(f32[2328,128]{1,0:T(8,128)} %collective-permute-done.7.refs_7_), channel_id=1, source_target_pairs={{0,384},{1,129},{128,256},{129,1},{256,128},{257,385},{384,0},{385... | collective-permute-start | bytes 3575816 | tf_op jit(solution)/shard_map/ppermute | solution.py:33
  80.7 1.3 %copy-start.3 = (bf16[640,1024]{1,0:T(8,128)(2,1)S(1)}, bf16[640,1024]{1,0:T(8,128)(2,1)}, u32[]{:S(2)}) copy-start(bf16[640,1024]{1,0:T(8,128)(2,1)} %copy-done.2) | copy-start | bytes 3932164
  82.0 1.3 %copy-start.5 = (bf16[640,1024]{1,0:T(8,128)(2,1)S(1)}, bf16[640,1024]{1,0:T(8,128)(2,1)}, u32[]{:S(2)}) copy-start(bf16[640,1024]{1,0:T(8,128)(2,1)} %copy-done.4) | copy-start | bytes 3932164
  103.2 4.6 %collective-permute-start.10 = (f32[256,1024]{1,0:T(8,128)S(1)}, f32[256,1024]{1,0:T(8,128)S(1)}, u32[]{:S(2)}, u32[]{:S(2)}) collective-permute-start(f32[256,1024]{1,0:T(8,128)S(1)} %get-tuple-element.51), channel_id=1, source_target_pairs={{0,1},{1,0},{2,3},{3,2},{4,5},{5,4},{6,7},{7,6},{8,9},{9,8},{10,11... | collective-permute-start | bytes 3145736 | tf_op jit(solution)/shard_map/ppermute | solution.py:68
  107.8 17.9 %collective-permute-start.11 = (f32[128,1024]{1,0:T(8,128)S(1)}, f32[128,1024]{1,0:T(8,128)S(1)}, u32[]{:S(2)}, u32[]{:S(2)}) collective-permute-start(f32[128,1024]{1,0:T(8,128)S(1)} %slice_add_fusion), channel_id=1, source_target_pairs={{0,2},{2,0},{1,3},{3,1},{4,6},{6,4},{5,7},{7,5},{8,10},{10,8},{9,1... | collective-permute-start | bytes 1572872 | tf_op jit(solution)/shard_map/ppermute | solution.py:68

commit v4 on v3

--- a/solution.py
+++ b/solution.py
@@ -129,7 +129,9 @@
 
 
 HELD = ((0,), (4,), (1,), (8, 12), (2, 3), (5, 9, 13), (6, 10, 14), (7, 11, 15))
-CALLS = ((0, 1, 12, 2, 3), (13, 14, 4, 8, 5, 9, 6, 10), (15, 7, 11))
+CALLS = ((0, 1, 12, 2, 3), (4, 8, 13, 14, 5, 9, 6, 10), (15, 7, 11))
+PLACED = ((0, 1, 12, 2, 3, 4, 8), (13, 14, 5, 9, 6, 10), (15, 7, 11))
+AHEAD = 2 * LANES
 NEAR = (0, 1, 12, 2, 3, 13, 14, 15)
 LATE = CALLS[1] + CALLS[2]
 FIRST_DEPTH, MIDDLE_DEPTH, LAST_DEPTH = (len(tiles) * LANES for tiles in CALLS)
@@ -184,7 +186,7 @@
 
 
 def right_copies(call, b_in, b_f, spots_s, sem_b, sem_s):
-    tiles = CALLS[call]
+    tiles = PLACED[call]
     copies, spots = [], []
     for source, held in zip(b_in, [held for held in HELD if set(held) & set(tiles)], strict=True):
         for k, tile in enumerate(held):
@@ -197,18 +199,18 @@
     return copies, spots
 
 
-def place_right(tiles, b_f, spots_s, b_hi, b_lo):
+def place_right(first, tiles, b_f, spots_s, b_hi, b_lo):
     def right_tile(tile, _):
         for k in range(INNER):
             rows = pl.ds(pl.multiple_of(tile * LANES + k * BLOCK, BLOCK), BLOCK)
             for c in range(COLS_B // 2):
 
                 def load(pair):
-                    return b_f[tile, pl.ds(pl.multiple_of(pair * BLOCK, BLOCK), BLOCK), :]
+                    return b_f[first + tile, pl.ds(pl.multiple_of(pair * BLOCK, BLOCK), BLOCK), :]
 
                 spot = k * COLS_B + 2 * c
-                left = spots_s[tile, spot].astype(jnp.int32)
-                right = spots_s[tile, spot + 1].astype(jnp.int32)
+                left = spots_s[first + tile, spot].astype(jnp.int32)
+                right = spots_s[first + tile, spot + 1].astype(jnp.int32)
                 lanes = slice(c * LANES, (c + 1) * LANES)
                 b_hi[rows, lanes], b_lo[rows, lanes] = halves(block_pair(load, left, right))
         return 0
@@ -236,13 +238,14 @@
 
 def early_kernel(n_right, *refs):
     b_in = refs[:n_right]
-    b_hi, b_lo, b_f, spots_b, sem_b, sem_s = refs[n_right:]
+    b_hi, b_lo, ahead_hi, ahead_lo, b_f, spots_b, sem_b, sem_s = refs[n_right:]
     copies, spots = right_copies(0, b_in, b_f, spots_b, sem_b, sem_s)
     for copy in spots + copies:
         copy.start()
     for copy in spots + copies:
         copy.wait()
-    place_right(len(CALLS[0]), b_f, spots_b, b_hi, b_lo)
+    place_right(0, len(CALLS[0]), b_f, spots_b, b_hi, b_lo)
+    place_right(len(CALLS[0]), 2, b_f, spots_b, ahead_hi, ahead_lo)
 
 
 def first_kernel(*refs):
@@ -266,14 +269,16 @@
 
 
 def middle_kernel(n_right, *refs):
-    me_ref, a_in, near, c_in, b_in = refs[0], refs[1], refs[2:4], refs[4], refs[5 : 5 + n_right]
-    late_hi, late_lo, c_out = refs[5 + n_right : 8 + n_right]
-    a_f, spots_a, sem_a, sem_sa, c_held, sem_c, b_f, b_hi, b_lo, spots_b, sem_b, sem_s = refs[8 + n_right :]
+    me_ref, a_in, near, c_in, ahead, b_in = refs[0], refs[1], refs[2:4], refs[4], refs[5:7], refs[7 : 7 + n_right]
+    late_hi, late_lo, c_out = refs[7 + n_right : 10 + n_right]
+    a_f, spots_a, sem_a, sem_sa, c_held, sem_c, b_f, b_hi, b_lo, spots_b, sem_b, sem_s = refs[10 + n_right :]
     copies_a, spots_of_a = left_copies((a_in,), a_f, spots_a, sem_a, sem_sa)
     copies, spots = right_copies(1, b_in, b_f, spots_b, sem_b, sem_s)
     held = [pltpu.make_async_copy(c_in, c_held, sem_c.at[0])]
+    for k, dense in enumerate((b_hi, b_lo)):
+        held.append(pltpu.make_async_copy(ahead[k], dense.at[pl.ds(0, AHEAD)], sem_c.at[5 + k]))
     for k, late in enumerate((late_hi, late_lo)):
-        for n, (first, at, lanes) in enumerate(((FIRST_DEPTH, 0, 256), (FIRST_DEPTH + 256, MIDDLE_DEPTH, 128))):
+        for n, (first, at, lanes) in enumerate(((FIRST_DEPTH, AHEAD, 256), (FIRST_DEPTH + 256, MIDDLE_DEPTH, 128))):
             source = near[k].at[:, pl.ds(first, lanes)]
             held.append(pltpu.make_async_copy(source, late.at[:, pl.ds(at, lanes)], sem_c.at[1 + 2 * k + n]))
     for copy in spots_of_a + copies_a + spots + copies + held:
@@ -283,7 +288,8 @@
     place_left(me_ref, 4, a_f, spots_a, late_hi, late_lo)
     for copy in spots + copies:
         copy.wait()
-    place_right(len(CALLS[1]), b_f, spots_b, b_hi, b_lo)
+    rest = pl.ds(AHEAD, MIDDLE_DEPTH - AHEAD)
+    place_right(0, len(PLACED[1]), b_f, spots_b, b_hi.at[rest], b_lo.at[rest])
     for copy in held:
         copy.wait()
 
@@ -302,7 +308,7 @@
         copy.start()
     for copy in spots + copies:
         copy.wait()
-    place_right(len(CALLS[2]), b_f, spots_b, b_hi, b_lo)
+    place_right(0, len(CALLS[2]), b_f, spots_b, b_hi, b_lo)
 
     def store(lanes, total):
         total += c_in[:, lanes]
@@ -314,11 +320,11 @@
 
 
 def right_scratch(call):
-    tiles = len(CALLS[call])
+    tiles, depth = len(PLACED[call]), len(CALLS[call]) * LANES
     return [
         pltpu.VMEM((tiles, B_ROWS, LANES), jnp.float32),
-        pltpu.VMEM((tiles * LANES, 1024), jnp.bfloat16),
-        pltpu.VMEM((tiles * LANES, 1024), jnp.bfloat16),
+        pltpu.VMEM((depth, 1024), jnp.bfloat16),
+        pltpu.VMEM((depth, 1024), jnp.bfloat16),
         pltpu.SMEM((tiles, LANES), jnp.float32),
         pltpu.SemaphoreType.DMA((tiles,)),
         pltpu.SemaphoreType.DMA((tiles,)),
@@ -326,7 +332,7 @@
 
 
 def used_by(call, b_all):
-    return [b_all[k] for k in range(len(HELD)) if set(HELD[k]) & set(CALLS[call])]
+    return [b_all[k] for k in range(len(HELD)) if set(HELD[k]) & set(PLACED[call])]
 
 
 def cost(call):
@@ -345,12 +351,13 @@
 def early_right(b_all):
     operands = used_by(0, b_all)
     dense = jax.ShapeDtypeStruct((FIRST_DEPTH, 1024), jnp.bfloat16)
+    ahead = jax.ShapeDtypeStruct((AHEAD, 1024), jnp.bfloat16)
     scratch = right_scratch(0)
     return pl.pallas_call(
         lambda *refs: early_kernel(len(operands), *refs),
-        out_shape=(dense, dense),
+        out_shape=(dense, dense, ahead, ahead),
         in_specs=[WHERE] * len(operands),
-        out_specs=(IN_VMEM,) * 2,
+        out_specs=(IN_VMEM,) * 4,
         scratch_shapes=scratch[:1] + scratch[3:],
         compiler_params=pltpu.CompilerParams(vmem_limit_bytes=FIRST),
         cost_estimate=pl.CostEstimate(flops=10**9, bytes_accessed=16 * 1024 * 1024, transcendentals=0),
@@ -370,23 +377,23 @@
     )(me, *a_near, *right)
 
 
-def middle_product(me, a_far, near_hi, near_lo, so_far, b_all):
+def middle_product(me, a_far, near_hi, near_lo, so_far, ahead, b_all):
     operands = used_by(1, b_all)
     late = jax.ShapeDtypeStruct((512, len(LATE) * LANES), jnp.bfloat16)
     return pl.pallas_call(
         lambda *refs: middle_kernel(len(operands), *refs),
         out_shape=(late, late, jax.ShapeDtypeStruct((512, 1024), jnp.float32)),
-        in_specs=[IN_SMEM] + [WHERE] * (4 + len(operands)),
+        in_specs=[IN_SMEM] + [WHERE] * (6 + len(operands)),
         out_specs=(IN_VMEM,) * 3,
         scratch_shapes=[
             *LEFT_SCRATCH,
             pltpu.VMEM((512, 1024), jnp.float32),
-            pltpu.SemaphoreType.DMA((5,)),
+            pltpu.SemaphoreType.DMA((7,)),
             *right_scratch(1),
         ],
         compiler_params=pltpu.CompilerParams(vmem_limit_bytes=MIDDLE),
         cost_estimate=cost(1),
-    )(me, a_far, near_hi, near_lo, so_far, *operands)
+    )(me, a_far, near_hi, near_lo, so_far, *ahead, *operands)
 
 
 def last_product(late_hi, late_lo, so_far, b_all):
@@ -435,9 +442,9 @@
     a_two, *right = hold((a_two, *right))
     a_four = exchange_col(jnp.concatenate([own_a, a_one, a_two], axis=0), 1)
     x_three, a_two = hold((x_three, a_two))
-    near_hi, near_lo, total = first_product(me, (own_a, a_one, a_two), right)
+    near_hi, near_lo, total = first_product(me, (own_a, a_one, a_two), right[:2])
     b_all += [x_three, x_four, exchange(x_three, "x", 1)]
-    late_hi, late_lo, total = middle_product(me, a_four, near_hi, near_lo, total, b_all)
+    late_hi, late_lo, total = middle_product(me, a_four, near_hi, near_lo, total, right[2:], b_all)
     other, send, keep = last_product(late_hi, late_lo, total, b_all)
 
     got = swap(other, "core")

time: 128 us -> 127 us (level)
  waiting for transfers between devices: 39.9 us -> 37.9 us
    ppermute x3, waiting for transfers between devices: 8.84 us -> 6.88 us  [exchange_col(): return lax.ppermute(array, ('col', 'core'), route)]
    unnamed x15 -> x23, local copies, waits for them, and re-layouts: 4.52 us -> 5.3 us
  transfers between devices with their start and end apart: 12 -> 12, of which waited for: 7 -> 7; matrix products, arithmetic and copies ran while one was open for 2% -> 2% of each run, Pallas kernels for 15% -> 16%
where the time goes in v4:
time: 127 us; the launch traced here: 126 us
  starting transfers between devices  52.1 us (41%)
  waiting for transfers between devices  37.9 us (30%)
  Pallas kernels  25.4 us (20%)
  local copies, waits for them, and re-layouts  6.34 us (5%)
  other arithmetic  3.22 us (3%)
    ppermute x7, starting transfers between devices, exchange(): return lax.ppermute(array, (axis, 'core'), route)  35.5 us
    ppermute x7, waiting for transfers between devices, exchange(): return lax.ppermute(array, (axis, 'core'), route)  16.2 us
    ppermute x2, waiting for transfers between devices, swap(): return lax.ppermute(array, axis, [(0, 1), (1, 0)])  14.8 us
    pallas_call x1, Pallas kernels, middle_product(): pl.pallas_call(lambda *refs: middle_kernel(len(operands), *refs), out_sha...  9.69 us
    ppermute x3, starting transfers between devices, exchange_col(): return lax.ppermute(array, ('col', 'core'), route)  9.09 us
    ppermute x2, starting transfers between devices, swap(): return lax.ppermute(array, axis, [(0, 1), (1, 0)])  7.5 us
    ppermute x3, waiting for transfers between devices, exchange_col(): return lax.ppermute(array, ('col', 'core'), route)  6.88 us
    pallas_call x1, Pallas kernels, first_product(): pl.pallas_call(first_kernel, out_shape=(near, near, jax.ShapeDtypeStruct(...  5.92 us
  transfers between devices with their start and end apart: 12, of which 7 were waited for; matrix products, arithmetic and copies ran while one was open for 2% of the time, Pallas kernels for 16%

profile of v4, /device:TPU:56, one launch (start us, length us, event | category | flops | bytes accessed | tf_op | source)
XLA Modules:
  0.0 125.8 jit_solution(4861576388545560981)
XLA Ops:
  0.7 2.2 %shard_map.73 = (f32[520,128]{1,0:T(8,128)}, f32[776,128]{1,0:T(8,128)}) custom-call(s32[2]{0:T(128)} %bitcast.18, s32[1,1,1]{2,1,0:T(1,128)S(6)} %copy.9.refs_1_, s32[2,2,8]{2,1,0:T(2,128)} %bitcast.16, s32[2,24]{1,0:T(2,128)} %bitcast.17, f32[24,64,64]{2,1,0:T(8,128)} %bitcast.14, f32[16,64,64]{2,1,0:T(8,128)} %bitcast.15), custom_call_target="tpu_custom_call" | custom-call | tf_op jit(solution)/shard_map/pallas_call | solution.py:110
  2.9 6.1 %collective-permute-start.1 = (f32[776,128]{1,0:T(8,128)}, f32[776,128]{1,0:T(8,128)S(1)}, u32[]{:S(2)}, u32[]{:S(2)}) collective-permute-start(f32[776,128]{1,0:T(8,128)} %get-tuple-element.33.refs_0_), channel_id=1, source_target_pairs={{0,32},{1,97},{32,0},{33,65},{64,96},{65,33},{96,64},{97,1},{2,34}... | collective-permute-start | bytes 1191944 | tf_op jit(solution)/shard_map/ppermute | solution.py:33
  9.0 3.4 %collective-permute-start = (f32[776,128]{1,0:T(8,128)}, f32[776,128]{1,0:T(8,128)S(1)}, u32[]{:S(2)}, u32[]{:S(2)}) collective-permute-start(f32[776,128]{1,0:T(8,128)} %get-tuple-element.33.refs_0_), channel_id=1, source_target_pairs={{0,128},{1,385},{128,0},{129,257},{256,384},{257,129},{384,256},{3... | collective-permute-start | bytes 1191944 | tf_op jit(solution)/shard_map/ppermute | solution.py:33
  12.4 6.9 %collective-permute-done.1.refs_1_ = f32[776,128]{1,0:T(8,128)S(1)} collective-permute-done((f32[776,128]{1,0:T(8,128)}, f32[776,128]{1,0:T(8,128)S(1)}, u32[]{:S(2)}, u32[]{:S(2)}) %collective-permute-start.1) | collective-permute-done | bytes 397344 | tf_op jit(solution)/shard_map/ppermute | solution.py:33
  19.3 0.0 collective-permute-done.refs_2_
  19.4 1.1 pad_maximum_fusion.1
  20.5 9.6 %collective-permute-start.4 = (f32[1552,128]{1,0:T(8,128)S(1)}, f32[1552,128]{1,0:T(8,128)S(1)}, u32[]{:S(2)}, u32[]{:S(2)}) collective-permute-start(f32[1552,128]{1,0:T(8,128)S(1)} %get-tuple-element.61), channel_id=1, source_target_pairs={{0,96},{1,33},{32,64},{33,1},{64,32},{65,97},{96,0},{97,65},{2,98}... | collective-permute-start | bytes 2383880 | tf_op jit(solution)/shard_map/ppermute | solution.py:33
  30.1 4.7 %collective-permute-start.3 = (f32[1552,128]{1,0:T(8,128)S(1)}, f32[1552,128]{1,0:T(8,128)S(1)}, u32[]{:S(2)}, u32[]{:S(2)}) collective-permute-start(f32[1552,128]{1,0:T(8,128)S(1)} %get-tuple-element.62), channel_id=1, source_target_pairs={{0,384},{1,129},{128,256},{129,1},{256,128},{257,385},{384,0},{385... | collective-permute-start | bytes 2383880 | tf_op jit(solution)/shard_map/ppermute | solution.py:33
  34.8 0.0 copy-done
  34.8 4.7 %collective-permute-start.2 = (f32[520,128]{1,0:T(8,128)S(1)}, f32[520,128]{1,0:T(8,128)S(1)}, u32[]{:S(2)}, u32[]{:S(2)}) collective-permute-start(f32[520,128]{1,0:T(8,128)S(1)} %copy-done), channel_id=1, source_target_pairs={{0,16},{1,17},{4,20},{5,21},{8,24},{9,25},{12,28},{13,29},{16,0},{... | collective-permute-start | bytes 798728 | tf_op jit(solution)/shard_map/ppermute | solution.py:47
  39.5 0.8 constant_dynamic-update-slice_fusion.1
  40.3 7.3 %collective-permute-done.4.refs_3_ = f32[1552,128]{1,0:T(8,128)S(1)} collective-permute-done((f32[1552,128]{1,0:T(8,128)S(1)}, f32[1552,128]{1,0:T(8,128)S(1)}, u32[]{:S(2)}, u32[]{:S(2)}) %collective-permute-start.4) | collective-permute-done | bytes 794656 | tf_op jit(solution)/shard_map/ppermute | solution.py:33
  47.6 0.0 collective-permute-done.3.refs_4_
  47.6 1.0 constant_dynamic-update-slice_fusion
  48.5 1.3 %collective-permute-done.2.refs_2_ = f32[520,128]{1,0:T(8,128)S(1)} collective-permute-done((f32[520,128]{1,0:T(8,128)S(1)}, f32[520,128]{1,0:T(8,128)S(1)}, u32[]{:S(2)}, u32[]{:S(2)}) %collective-permute-start.2) | collective-permute-done | bytes 266272 | tf_op jit(solution)/shard_map/ppermute | solution.py:47
  49.8 2.3 %collective-permute-start.7 = (f32[2328,128]{1,0:T(8,128)}, f32[2328,128]{1,0:T(8,128)S(1)}, u32[]{:S(2)}, u32[]{:S(2)}) collective-permute-start(f32[2328,128]{1,0:T(8,128)} %constant_dynamic-update-slice_fusion), channel_id=1, source_target_pairs={{0,128},{1,385},{128,0},{129,257},{256,384},{257,129},{384,256},{3... | collective-permute-start | bytes 3575816 | tf_op jit(solution)/shard_map/ppermute | solution.py:33
  52.2 2.5 %collective-permute-start.5 = (f32[1040,128]{1,0:T(8,128)S(1)}, f32[1040,128]{1,0:T(8,128)S(1)}, u32[]{:S(2)}, u32[]{:S(2)}) collective-permute-start(f32[1040,128]{1,0:T(8,128)S(1)} %pad_maximum_fusion.3), channel_id=1, source_target_pairs={{0,8},{1,25},{4,28},{5,13},{8,0},{9,17},{12,20},{13,5},{16,24},{17... | collective-permute-start | bytes 1597448 | tf_op jit(solution)/shard_map/ppermute | solution.py:47
  54.7 4.4 %collective-permute-start.8 = (f32[2328,128]{1,0:T(8,128)}, f32[2328,128]{1,0:T(8,128)}, u32[]{:S(2)}, u32[]{:S(2)}) collective-permute-start(f32[2328,128]{1,0:T(8,128)} %constant_dynamic-update-slice_fusion), channel_id=1, source_target_pairs={{0,384},{1,129},{128,256},{129,1},{256,128},{257,385},{384,0},{385... | collective-permute-start | bytes 3575816 | tf_op jit(solution)/shard_map/ppermute | solution.py:33
  59.1 0.0 copy-done.1
  59.1 4.0 %shard_map.74 = (bf16[640,1024]{1,0:T(8,128)(2,1)S(1)}, bf16[640,1024]{1,0:T(8,128)(2,1)S(1)}, bf16[256,1024]{1,0:T(8,128)(2,1)S(1)}, bf16[256,1024]{1,0:T(8,128)(2,1)S(1)}) custom-call(f32[776,128]{1,0:T(8,128)S(1)} %copy-done.1, f32[776,128]{1,0:T(8,128)S(1)} %collective-permute-done.1.refs_1_, f32[776,128]{1,0:T(8,128)S(1)} %collective-permute-done.refs_2_, ...), custom_call_target="tpu_custom_call" | custom-call | flops 1000000000 | bytes 16777216 | tf_op jit(solution)/shard_map/pallas_call | solution.py:356
  63.1 0.0 copy-start.4
  63.1 1.1 copy-done.4
  64.2 0.8 copy-done.8
  65.0 5.6 %collective-permute-done.5.refs_3_ = f32[1040,128]{1,0:T(8,128)S(1)} collective-permute-done((f32[1040,128]{1,0:T(8,128)S(1)}, f32[1040,128]{1,0:T(8,128)S(1)}, u32[]{:S(2)}, u32[]{:S(2)}) %collective-permute-start.5) | collective-permute-done | bytes 532512 | tf_op jit(solution)/shard_map/ppermute | solution.py:47
  70.6 1.1 pad_maximum_fusion
  71.6 1.9 %collective-permute-start.6 = (f32[2080,128]{1,0:T(8,128)}, f32[2080,128]{1,0:T(8,128)}, u32[]{:S(2)}, u32[]{:S(2)}) collective-permute-start(f32[2080,128]{1,0:T(8,128)} %pad_maximum_fusion), channel_id=1, source_target_pairs={{0,4},{1,29},{4,0},{5,9},{8,12},{9,5},{12,8},{13,17},{16,20},{17,1... | collective-permute-start | bytes 3194888 | tf_op jit(solution)/shard_map/ppermute | solution.py:47
  73.5 1.9 %collective-permute-done.7.refs_7_ = f32[2328,128]{1,0:T(8,128)S(1)} collective-permute-done((f32[2328,128]{1,0:T(8,128)}, f32[2328,128]{1,0:T(8,128)S(1)}, u32[]{:S(2)}, u32[]{:S(2)}) %collective-permute-start.7) | collective-permute-done | bytes 1191968 | tf_op jit(solution)/shard_map/ppermute | solution.py:33
  75.5 0.0 copy-done.2
  75.5 5.1 %collective-permute-start.9 = (f32[2328,128]{1,0:T(8,128)S(1)}, f32[2328,128]{1,0:T(8,128)S(1)}, u32[]{:S(2)}, u32[]{:S(2)}) collective-permute-start(f32[2328,128]{1,0:T(8,128)S(1)} %collective-permute-done.7.refs_7_), channel_id=1, source_target_pairs={{0,384},{1,129},{128,256},{129,1},{256,128},{257,385},{384,0},{385... | collective-permute-start | bytes 3575816 | tf_op jit(solution)/shard_map/ppermute | solution.py:33
  80.6 0.0 copy-done.6
  80.6 0.0 copy-done.10
  80.6 0.1 concatenate.18.refs_0_
  80.7 1.3 %copy-done.3 = bf16[640,1024]{1,0:T(8,128)(2,1)S(1)} copy-done((bf16[640,1024]{1,0:T(8,128)(2,1)S(1)}, bf16[640,1024]{1,0:T(8,128)(2,1)}, u32[]{:S(2)}) %copy-start.3) | copy-done | bytes 1310744
  82.0 1.3 %copy-done.5 = bf16[640,1024]{1,0:T(8,128)(2,1)S(1)} copy-done((bf16[640,1024]{1,0:T(8,128)(2,1)S(1)}, bf16[640,1024]{1,0:T(8,128)(2,1)}, u32[]{:S(2)}) %copy-start.5) | copy-done | bytes 1310744
  83.3 5.9 %shard_map.75 = (bf16[512,1024]{1,0:T(8,128)(2,1)S(1)}, bf16[512,1024]{1,0:T(8,128)(2,1)S(1)}, f32[512,1024]{1,0:T(8,128)S(1)}) custom-call(s32[149]{0:T(256)S(1)} %concatenate.18.refs_0_, f32[520,128]{1,0:T(8,128)S(1)} %copy-done, f32[520,128]{1,0:T(8,128)S(1)} %collective-permute-done.2.refs_2_, f32[1040,128]{1,0:T(8,128)S(1)} %collective-permute-done.5.refs_3_, ...), custom_call_target="tpu_custom_call" | custom-call | flops 2013265920 | bytes 16777216 | tf_op jit(solution)/shard_map/pallas_call | solution.py:369
  89.3 0.0 collective-permute-done.8.refs_8_
  89.3 0.0 collective-permute-done.6.refs_1_
  89.3 0.0 copy-done.7
  89.3 0.0 copy-done.9
  89.3 9.7 %shard_map.76 = (bf16[512,1408]{1,0:T(8,128)(2,1)S(1)}, bf16[512,1408]{1,0:T(8,128)(2,1)S(1)}, f32[512,1024]{1,0:T(8,128)S(1)}) custom-call(s32[149]{0:T(256)S(1)} %concatenate.18.refs_0_, f32[2080,128]{1,0:T(8,128)} %collective-permute-done.6.refs_1_, bf16[512,1024]{1,0:T(8,128)(2,1)S(1)} %get-tuple-element.49.refs_2_, ...), custom_call_target="tpu_custom_call" | custom-call | flops 3221225472 | bytes 16777216 | tf_op jit(solution)/shard_map/pallas_call | solution.py:383
  99.0 0.0 collective-permute-done.9.refs_3_
  99.0 3.5 %shard_map.77 = (f32[256,1024]{1,0:T(8,128)S(1)}, f32[128,1024]{1,0:T(8,128)S(1)}, f32[128,1024]{1,0:T(8,128)S(1)}) custom-call(bf16[512,1408]{1,0:T(8,128)(2,1)S(1)} %get-tuple-element.55.refs_0_, bf16[512,1408]{1,0:T(8,128)(2,1)S(1)} %get-tuple-element.56.refs_1_, f32[512,1024]{1,0:T(8,128)S(1)} %get-tuple-element.57.refs_2_, ...), custom_call_target="tpu_custom_call" | custom-call | flops 1207959552 | bytes 16777216 | tf_op jit(solution)/shard_map/pallas_call | solution.py:401
  102.5 1.9 %collective-permute-start.10 = (f32[256,1024]{1,0:T(8,128)S(1)}, f32[256,1024]{1,0:T(8,128)S(1)}, u32[]{:S(2)}, u32[]{:S(2)}) collective-permute-start(f32[256,1024]{1,0:T(8,128)S(1)} %get-tuple-element.59), channel_id=1, source_target_pairs={{0,1},{1,0},{2,3},{3,2},{4,5},{5,4},{6,7},{7,6},{8,9},{9,8},{10,11... | collective-permute-start | bytes 3145736 | tf_op jit(solution)/shard_map/ppermute | solution.py:68
  104.5 2.6 %collective-permute-done.10 = f32[256,1024]{1,0:T(8,128)S(1)} collective-permute-done((f32[256,1024]{1,0:T(8,128)S(1)}, f32[256,1024]{1,0:T(8,128)S(1)}, u32[]{:S(2)}, u32[]{:S(2)}) %collective-permute-start.10) | collective-permute-done | bytes 1048608 | tf_op jit(solution)/shard_map/ppermute | solution.py:68
  107.1 0.1 slice_add_fusion
  107.2 5.6 %collective-permute-start.11 = (f32[128,1024]{1,0:T(8,128)S(1)}, f32[128,1024]{1,0:T(8,128)S(1)}, u32[]{:S(2)}, u32[]{:S(2)}) collective-permute-start(f32[128,1024]{1,0:T(8,128)S(1)} %slice_add_fusion), channel_id=1, source_target_pairs={{0,2},{2,0},{1,3},{3,1},{4,6},{6,4},{5,7},{7,5},{8,10},{10,8},{9,1... | collective-permute-start | bytes 1572872 | tf_op jit(solution)/shard_map/ppermute | solution.py:68
  112.7 12.2 %collective-permute-done.11 = f32[128,1024]{1,0:T(8,128)S(1)} collective-permute-done((f32[128,1024]{1,0:T(8,128)S(1)}, f32[128,1024]{1,0:T(8,128)S(1)}, u32[]{:S(2)}, u32[]{:S(2)}) %collective-permute-start.11) | collective-permute-done | bytes 524320 | tf_op jit(solution)/shard_map/ppermute | solution.py:68
  125.0 0.9 fusion
  (11 shorter events, 0.1 us)
Async XLA Ops:
  2.9 16.4 %collective-permute-start.1 = (f32[776,128]{1,0:T(8,128)}, f32[776,128]{1,0:T(8,128)S(1)}, u32[]{:S(2)}, u32[]{:S(2)}) collective-permute-start(f32[776,128]{1,0:T(8,128)} %get-tuple-element.33.refs_0_), channel_id=1, source_target_pairs={{0,32},{1,97},{32,0},{33,65},{64,96},{65,33},{96,64},{97,1},{2,34}... | collective-permute-start | bytes 1191944 | tf_op jit(solution)/shard_map/ppermute | solution.py:33
  9.0 10.4 %collective-permute-start = (f32[776,128]{1,0:T(8,128)}, f32[776,128]{1,0:T(8,128)S(1)}, u32[]{:S(2)}, u32[]{:S(2)}) collective-permute-start(f32[776,128]{1,0:T(8,128)} %get-tuple-element.33.refs_0_), channel_id=1, source_target_pairs={{0,128},{1,385},{128,0},{129,257},{256,384},{257,129},{384,256},{3... | collective-permute-start | bytes 1191944 | tf_op jit(solution)/shard_map/ppermute | solution.py:33
  19.4 15.4 %copy-start = (f32[520,128]{1,0:T(8,128)S(1)}, f32[520,128]{1,0:T(8,128)}, u32[]{:S(2)}) copy-start(f32[520,128]{1,0:T(8,128)} %get-tuple-element.35.refs_1_) | copy-start | bytes 798724
  20.5 27.1 %collective-permute-start.4 = (f32[1552,128]{1,0:T(8,128)S(1)}, f32[1552,128]{1,0:T(8,128)S(1)}, u32[]{:S(2)}, u32[]{:S(2)}) collective-permute-start(f32[1552,128]{1,0:T(8,128)S(1)} %get-tuple-element.61), channel_id=1, source_target_pairs={{0,96},{1,33},{32,64},{33,1},{64,32},{65,97},{96,0},{97,65},{2,98}... | collective-permute-start | bytes 2383880 | tf_op jit(solution)/shard_map/ppermute | solution.py:33
  30.1 17.5 %collective-permute-start.3 = (f32[1552,128]{1,0:T(8,128)S(1)}, f32[1552,128]{1,0:T(8,128)S(1)}, u32[]{:S(2)}, u32[]{:S(2)}) collective-permute-start(f32[1552,128]{1,0:T(8,128)S(1)} %get-tuple-element.62), channel_id=1, source_target_pairs={{0,384},{1,129},{128,256},{129,1},{256,128},{257,385},{384,0},{385... | collective-permute-start | bytes 2383880 | tf_op jit(solution)/shard_map/ppermute | solution.py:33
  34.8 15.1 %collective-permute-start.2 = (f32[520,128]{1,0:T(8,128)S(1)}, f32[520,128]{1,0:T(8,128)S(1)}, u32[]{:S(2)}, u32[]{:S(2)}) collective-permute-start(f32[520,128]{1,0:T(8,128)S(1)} %copy-done), channel_id=1, source_target_pairs={{0,16},{1,17},{4,20},{5,21},{8,24},{9,25},{12,28},{13,29},{16,0},{... | collective-permute-start | bytes 798728 | tf_op jit(solution)/shard_map/ppermute | solution.py:47
  40.3 18.8 %copy-start.1 = (f32[776,128]{1,0:T(8,128)S(1)}, f32[776,128]{1,0:T(8,128)}, u32[]{:S(2)}) copy-start(f32[776,128]{1,0:T(8,128)} %get-tuple-element.33.refs_0_) | copy-start | bytes 1191940
  49.8 25.7 %collective-permute-start.7 = (f32[2328,128]{1,0:T(8,128)}, f32[2328,128]{1,0:T(8,128)S(1)}, u32[]{:S(2)}, u32[]{:S(2)}) collective-permute-start(f32[2328,128]{1,0:T(8,128)} %constant_dynamic-update-slice_fusion), channel_id=1, source_target_pairs={{0,128},{1,385},{128,0},{129,257},{256,384},{257,129},{384,256},{3... | collective-permute-start | bytes 3575816 | tf_op jit(solution)/shard_map/ppermute | solution.py:33
  52.2 18.4 %collective-permute-start.5 = (f32[1040,128]{1,0:T(8,128)S(1)}, f32[1040,128]{1,0:T(8,128)S(1)}, u32[]{:S(2)}, u32[]{:S(2)}) collective-permute-start(f32[1040,128]{1,0:T(8,128)S(1)} %pad_maximum_fusion.3), channel_id=1, source_target_pairs={{0,8},{1,25},{4,28},{5,13},{8,0},{9,17},{12,20},{13,5},{16,24},{17... | collective-permute-start | bytes 1597448 | tf_op jit(solution)/shard_map/ppermute | solution.py:47
  54.7 34.6 %collective-permute-start.8 = (f32[2328,128]{1,0:T(8,128)}, f32[2328,128]{1,0:T(8,128)}, u32[]{:S(2)}, u32[]{:S(2)}) collective-permute-start(f32[2328,128]{1,0:T(8,128)} %constant_dynamic-update-slice_fusion), channel_id=1, source_target_pairs={{0,384},{1,129},{128,256},{129,1},{256,128},{257,385},{384,0},{385... | collective-permute-start | bytes 3575816 | tf_op jit(solution)/shard_map/ppermute | solution.py:33
  63.1 1.1 copy-start.4
  64.2 0.8 copy-start.8
  65.0 10.5 %copy-start.2 = (bf16[640,1024]{1,0:T(8,128)(2,1)}, bf16[640,1024]{1,0:T(8,128)(2,1)S(1)}, u32[]{:S(2)}) copy-start(bf16[640,1024]{1,0:T(8,128)(2,1)S(1)} %get-tuple-element.47.refs_4_) | copy-start | bytes 3932164
  65.0 15.6 %copy-start.6 = (bf16[256,1024]{1,0:T(8,128)(2,1)}, bf16[256,1024]{1,0:T(8,128)(2,1)S(1)}, u32[]{:S(2)}) copy-start(bf16[256,1024]{1,0:T(8,128)(2,1)S(1)} %get-tuple-element.52.refs_5_) | copy-start | bytes 1572868
  65.0 15.6 %copy-start.10 = (s32[144]{0:T(256)S(1)}, s32[144]{0:T(256)}, u32[]{:S(2)}) copy-start(s32[144]{0:T(256)} %constant.22.clone) | copy-start | bytes 1732
  71.6 17.6 %collective-permute-start.6 = (f32[2080,128]{1,0:T(8,128)}, f32[2080,128]{1,0:T(8,128)}, u32[]{:S(2)}, u32[]{:S(2)}) collective-permute-start(f32[2080,128]{1,0:T(8,128)} %pad_maximum_fusion), channel_id=1, source_target_pairs={{0,4},{1,29},{4,0},{5,9},{8,12},{9,5},{12,8},{13,17},{16,20},{17,1... | collective-permute-start | bytes 3194888 | tf_op jit(solution)/shard_map/ppermute | solution.py:47
  75.5 23.5 %collective-permute-start.9 = (f32[2328,128]{1,0:T(8,128)S(1)}, f32[2328,128]{1,0:T(8,128)S(1)}, u32[]{:S(2)}, u32[]{:S(2)}) collective-permute-start(f32[2328,128]{1,0:T(8,128)S(1)} %collective-permute-done.7.refs_7_), channel_id=1, source_target_pairs={{0,384},{1,129},{128,256},{129,1},{256,128},{257,385},{384,0},{385... | collective-permute-start | bytes 3575816 | tf_op jit(solution)/shard_map/ppermute | solution.py:33
  80.7 1.3 %copy-start.3 = (bf16[640,1024]{1,0:T(8,128)(2,1)S(1)}, bf16[640,1024]{1,0:T(8,128)(2,1)}, u32[]{:S(2)}) copy-start(bf16[640,1024]{1,0:T(8,128)(2,1)} %copy-done.2) | copy-start | bytes 3932164
  82.0 1.3 %copy-start.5 = (bf16[640,1024]{1,0:T(8,128)(2,1)S(1)}, bf16[640,1024]{1,0:T(8,128)(2,1)}, u32[]{:S(2)}) copy-start(bf16[640,1024]{1,0:T(8,128)(2,1)} %copy-done.4) | copy-start | bytes 3932164
  83.3 6.0 %copy-start.7 = (bf16[256,1024]{1,0:T(8,128)(2,1)S(1)}, bf16[256,1024]{1,0:T(8,128)(2,1)}, u32[]{:S(2)}) copy-start(bf16[256,1024]{1,0:T(8,128)(2,1)} %copy-done.6) | copy-start | bytes 1572868
  83.3 6.0 %copy-start.9 = (bf16[256,1024]{1,0:T(8,128)(2,1)S(1)}, bf16[256,1024]{1,0:T(8,128)(2,1)}, u32[]{:S(2)}) copy-start(bf16[256,1024]{1,0:T(8,128)(2,1)} %copy-done.8) | copy-start | bytes 1572868
  102.5 4.6 %collective-permute-start.10 = (f32[256,1024]{1,0:T(8,128)S(1)}, f32[256,1024]{1,0:T(8,128)S(1)}, u32[]{:S(2)}, u32[]{:S(2)}) collective-permute-start(f32[256,1024]{1,0:T(8,128)S(1)} %get-tuple-element.59), channel_id=1, source_target_pairs={{0,1},{1,0},{2,3},{3,2},{4,5},{5,4},{6,7},{7,6},{8,9},{9,8},{10,11... | collective-permute-start | bytes 3145736 | tf_op jit(solution)/shard_map/ppermute | solution.py:68
  107.2 17.8 %collective-permute-start.11 = (f32[128,1024]{1,0:T(8,128)S(1)}, f32[128,1024]{1,0:T(8,128)S(1)}, u32[]{:S(2)}, u32[]{:S(2)}) collective-permute-start(f32[128,1024]{1,0:T(8,128)S(1)} %slice_add_fusion), channel_id=1, source_target_pairs={{0,2},{2,0},{1,3},{3,1},{4,6},{6,4},{5,7},{7,5},{8,10},{10,8},{9,1... | collective-permute-start | bytes 1572872 | tf_op jit(solution)/shard_map/ppermute | solution.py:68

commit v5 on v4

--- a/solution.py
+++ b/solution.py
@@ -141,8 +141,8 @@
     lane = lax.broadcasted_iota(jnp.int32, (BLOCK, LANES), 1)
     low = jnp.maximum(left, 0)
     high = jnp.maximum(right, 0)
-    one = pltpu.roll(load(low // 2), (low % 2) * BLOCK, 1)
-    two = pltpu.roll(load(high // 2), (1 - high % 2) * BLOCK, 1)
+    one = pltpu.roll(load(low >> 1), (low & 1) * BLOCK, 1)
+    two = pltpu.roll(load(high >> 1), (1 - (high & 1)) * BLOCK, 1)
     one = jnp.where((lane < BLOCK) & (left >= 0), one, 0.0)
     return jnp.where((lane >= BLOCK) & (right >= 0), two, one)
 
@@ -182,7 +182,7 @@
             a_hi[rows, lanes], a_lo[rows, lanes] = halves(block_pair(load, left, right))
         return 0
 
-    lax.fori_loop(0, 8, left_tile, 0)
+    lax.fori_loop(0, 8, left_tile, 0, unroll=2)
 
 
 def right_copies(call, b_in, b_f, spots_s, sem_b, sem_s):
@@ -215,7 +215,7 @@
                 b_hi[rows, lanes], b_lo[rows, lanes] = halves(block_pair(load, left, right))
         return 0
 
-    lax.fori_loop(0, tiles, right_tile, 0)
+    lax.fori_loop(0, tiles, right_tile, 0, unroll=3 if tiles == 3 else 2 - tiles % 2)
 
 
 def left_copies(parts, a_f, spots_s, sem_a, sem_s):
@@ -425,16 +425,16 @@
     )
     z_one = exchange(own, "zh", 0)
     x_one = exchange(own, "x", 0)
-    x_one, z_one, own_a = hold((x_one, z_one, own_a))
+    z_one, own_a = hold((z_one, own_a))
     a_one = exchange_col(own_a, 4)
 
-    z_two = exchange(jnp.concatenate([own, z_one], axis=0), "zh", 1)
+    z_two = exchange(jnp.concatenate([own, z_one, own[:8]], axis=0), "zh", 1)
     x_two = exchange(jnp.concatenate([own, x_one], axis=0), "x", 1)
     x_two, z_two = hold((x_two, z_two))
     a_one, _ = hold((a_one, z_two))
     a_two = exchange_col(jnp.concatenate([own_a, a_one], axis=0), 2)
 
-    column = jnp.concatenate([z_one, z_two], axis=0)
+    column = jnp.concatenate([z_one, z_two[: 2 * B_ROWS]], axis=0)
     x_three = exchange(column, "x", 0)
     x_four = exchange(column, "x", 1)
     b_all = [own, z_one, x_one, z_two, x_two]

time: 127 us -> 127 us (level)
  waiting for transfers between devices: 37.9 us -> 40.9 us
  Pallas kernels: 25.4 us -> 23.4 us
    ppermute x3, waiting for transfers between devices: 6.88 us -> 8.43 us  [exchange_col(): return lax.ppermute(array, ('col', 'core'), route)]
    ppermute x7, waiting for transfers between devices: 16.2 us -> 17.6 us  [exchange(): return lax.ppermute(array, (axis, 'core'), route)]
    unnamed x23 -> x22, local copies, waits for them, and re-layouts: 5.3 us -> 4.52 us
  transfers between devices with their start and end apart: 12 -> 12, of which waited for: 7 -> 8; matrix products, arithmetic and copies ran while one was open for 2% -> 2% of each run, Pallas kernels for 16% -> 15%
where the time goes in v5:
time: 127 us; the launch traced here: 126 us
  starting transfers between devices  51.4 us (40%)
  waiting for transfers between devices  40.9 us (32%)
  Pallas kernels  23.4 us (18%)
  local copies, waits for them, and re-layouts  5.36 us (4%)
  other arithmetic  4.27 us (3%)
    ppermute x7, starting transfers between devices, exchange(): return lax.ppermute(array, (axis, 'core'), route)  35.4 us
    ppermute x7, waiting for transfers between devices, exchange(): return lax.ppermute(array, (axis, 'core'), route)  17.6 us
    ppermute x2, waiting for transfers between devices, swap(): return lax.ppermute(array, axis, [(0, 1), (1, 0)])  14.8 us
    pallas_call x1, Pallas kernels, middle_product(): pl.pallas_call(lambda *refs: middle_kernel(len(operands), *refs), out_sha...  8.98 us
    ppermute x3, starting transfers between devices, exchange_col(): return lax.ppermute(array, ('col', 'core'), route)  8.82 us
    ppermute x3, waiting for transfers between devices, exchange_col(): return lax.ppermute(array, ('col', 'core'), route)  8.43 us
    ppermute x2, starting transfers between devices, swap(): return lax.ppermute(array, axis, [(0, 1), (1, 0)])  7.28 us
    pallas_call x1, Pallas kernels, first_product(): pl.pallas_call(first_kernel, out_shape=(near, near, jax.ShapeDtypeStruct(...  5.46 us
  transfers between devices with their start and end apart: 12, of which 8 were waited for; matrix products, arithmetic and copies ran while one was open for 2% of the time, Pallas kernels for 15%

profile of v5, /device:TPU:56, one launch (start us, length us, event | category | flops | bytes accessed | tf_op | source)
XLA Modules:
  0.0 126.4 jit_solution(6293940975361678331)
XLA Ops:
  0.7 2.2 %shard_map.73 = (f32[520,128]{1,0:T(8,128)}, f32[776,128]{1,0:T(8,128)}) custom-call(s32[2]{0:T(128)} %bitcast.18, s32[1,1,1]{2,1,0:T(1,128)S(6)} %copy.8.refs_1_, s32[2,2,8]{2,1,0:T(2,128)} %bitcast.16, s32[2,24]{1,0:T(2,128)} %bitcast.17, f32[24,64,64]{2,1,0:T(8,128)} %bitcast.14, f32[16,64,64]{2,1,0:T(8,128)} %bitcast.15), custom_call_target="tpu_custom_call" | custom-call | tf_op jit(solution)/shard_map/pallas_call | solution.py:110
  2.9 0.0 copy-start
  2.9 6.2 %collective-permute-start = (f32[776,128]{1,0:T(8,128)}, f32[776,128]{1,0:T(8,128)S(1)}, u32[]{:S(2)}, u32[]{:S(2)}) collective-permute-start(f32[776,128]{1,0:T(8,128)} %get-tuple-element.32.refs_0_), channel_id=1, source_target_pairs={{0,32},{1,97},{32,0},{33,65},{64,96},{65,33},{96,64},{97,1},{2,34}... | collective-permute-start | bytes 1191944 | tf_op jit(solution)/shard_map/ppermute | solution.py:33
  9.1 3.4 %collective-permute-start.2 = (f32[776,128]{1,0:T(8,128)}, f32[776,128]{1,0:T(8,128)S(1)}, u32[]{:S(2)}, u32[]{:S(2)}) collective-permute-start(f32[776,128]{1,0:T(8,128)} %get-tuple-element.32.refs_0_), channel_id=1, source_target_pairs={{0,128},{1,385},{128,0},{129,257},{256,384},{257,129},{384,256},{3... | collective-permute-start | bytes 1191944 | tf_op jit(solution)/shard_map/ppermute | solution.py:33
  12.5 0.7 slice.12
  13.2 6.2 %collective-permute-done.refs_1_ = f32[776,128]{1,0:T(8,128)S(1)} collective-permute-done((f32[776,128]{1,0:T(8,128)}, f32[776,128]{1,0:T(8,128)S(1)}, u32[]{:S(2)}, u32[]{:S(2)}) %collective-permute-start) | collective-permute-done | bytes 397344 | tf_op jit(solution)/shard_map/ppermute | solution.py:33
  19.5 1.1 pad_maximum_fusion.2
  20.5 0.0 copy-start.1
  20.5 9.7 %collective-permute-start.4 = (f32[1560,128]{1,0:T(8,128)S(1)}, f32[1560,128]{1,0:T(8,128)S(1)}, u32[]{:S(2)}, u32[]{:S(2)}) collective-permute-start(f32[1560,128]{1,0:T(8,128)S(1)} %pad_maximum_fusion.2), channel_id=1, source_target_pairs={{0,96},{1,33},{32,64},{33,1},{64,32},{65,97},{96,0},{97,65},{2,98}... | collective-permute-start | bytes 2396168 | tf_op jit(solution)/shard_map/ppermute | solution.py:33
  30.2 0.0 collective-permute-done.2.refs_2_
  30.3 0.0 copy-done
  30.3 0.1 pad_maximum_fusion.3
  30.3 4.7 %collective-permute-start.3 = (f32[1552,128]{1,0:T(8,128)S(1)}, f32[1552,128]{1,0:T(8,128)S(1)}, u32[]{:S(2)}, u32[]{:S(2)}) collective-permute-start(f32[1552,128]{1,0:T(8,128)S(1)} %pad_maximum_fusion.3), channel_id=1, source_target_pairs={{0,384},{1,129},{128,256},{129,1},{256,128},{257,385},{384,0},{385... | collective-permute-start | bytes 2383880 | tf_op jit(solution)/shard_map/ppermute | solution.py:33
  35.0 0.0 copy-done.1
  35.0 4.7 %collective-permute-start.1 = (f32[520,128]{1,0:T(8,128)S(1)}, f32[520,128]{1,0:T(8,128)S(1)}, u32[]{:S(2)}, u32[]{:S(2)}) collective-permute-start(f32[520,128]{1,0:T(8,128)S(1)} %copy-done.1), channel_id=1, source_target_pairs={{0,16},{1,17},{4,20},{5,21},{8,24},{9,25},{12,28},{13,29},{16,0},{... | collective-permute-start | bytes 798728 | tf_op jit(solution)/shard_map/ppermute | solution.py:47
  39.7 5.8 %collective-permute-done.3.refs_4_ = f32[1552,128]{1,0:T(8,128)S(1)} collective-permute-done((f32[1552,128]{1,0:T(8,128)S(1)}, f32[1552,128]{1,0:T(8,128)S(1)}, u32[]{:S(2)}, u32[]{:S(2)}) %collective-permute-start.3) | collective-permute-done | bytes 794656 | tf_op jit(solution)/shard_map/ppermute | solution.py:33
  45.5 2.2 %collective-permute-done.4.refs_3_ = f32[1560,128]{1,0:T(8,128)S(1)} collective-permute-done((f32[1560,128]{1,0:T(8,128)S(1)}, f32[1560,128]{1,0:T(8,128)S(1)}, u32[]{:S(2)}, u32[]{:S(2)}) %collective-permute-start.4) | collective-permute-done | bytes 798752 | tf_op jit(solution)/shard_map/ppermute | solution.py:33
  47.7 0.1 slice.13
  47.8 2.3 %collective-permute-done.1.refs_2_ = f32[520,128]{1,0:T(8,128)S(1)} collective-permute-done((f32[520,128]{1,0:T(8,128)S(1)}, f32[520,128]{1,0:T(8,128)S(1)}, u32[]{:S(2)}, u32[]{:S(2)}) %collective-permute-start.1) | collective-permute-done | bytes 266272 | tf_op jit(solution)/shard_map/ppermute | solution.py:47
  50.1 1.1 pad_maximum_fusion
  51.2 2.1 %collective-permute-start.7 = (f32[2328,128]{1,0:T(8,128)}, f32[2328,128]{1,0:T(8,128)S(1)}, u32[]{:S(2)}, u32[]{:S(2)}) collective-permute-start(f32[2328,128]{1,0:T(8,128)} %pad_maximum_fusion), channel_id=1, source_target_pairs={{0,128},{1,385},{128,0},{129,257},{256,384},{257,129},{384,256},{3... | collective-permute-start | bytes 3575816 | tf_op jit(solution)/shard_map/ppermute | solution.py:33
  53.3 2.2 %collective-permute-start.5 = (f32[1040,128]{1,0:T(8,128)S(1)}, f32[1040,128]{1,0:T(8,128)S(1)}, u32[]{:S(2)}, u32[]{:S(2)}) collective-permute-start(f32[1040,128]{1,0:T(8,128)S(1)} %pad_maximum_fusion.4), channel_id=1, source_target_pairs={{0,8},{1,25},{4,28},{5,13},{8,0},{9,17},{12,20},{13,5},{16,24},{17... | collective-permute-start | bytes 1597448 | tf_op jit(solution)/shard_map/ppermute | solution.py:47
  55.6 4.5 %collective-permute-start.8 = (f32[2328,128]{1,0:T(8,128)}, f32[2328,128]{1,0:T(8,128)}, u32[]{:S(2)}, u32[]{:S(2)}) collective-permute-start(f32[2328,128]{1,0:T(8,128)} %pad_maximum_fusion), channel_id=1, source_target_pairs={{0,384},{1,129},{128,256},{129,1},{256,128},{257,385},{384,0},{385... | collective-permute-start | bytes 3575816 | tf_op jit(solution)/shard_map/ppermute | solution.py:33
  60.1 3.9 %shard_map.74 = (bf16[640,1024]{1,0:T(8,128)(2,1)S(1)}, bf16[640,1024]{1,0:T(8,128)(2,1)S(1)}, bf16[256,1024]{1,0:T(8,128)(2,1)S(1)}, bf16[256,1024]{1,0:T(8,128)(2,1)S(1)}) custom-call(f32[776,128]{1,0:T(8,128)S(1)} %copy-done, f32[776,128]{1,0:T(8,128)S(1)} %collective-permute-done.refs_1_, f32[776,128]{1,0:T(8,128)S(1)} %collective-permute-done.2.refs_2_, ...), custom_call_target="tpu_custom_call" | custom-call | flops 1000000000 | bytes 16777216 | tf_op jit(solution)/shard_map/pallas_call | solution.py:356
  64.0 0.0 copy-start.4
  64.0 1.1 copy-done.4
  65.1 0.8 copy-done.8
  65.9 6.1 %collective-permute-done.5.refs_3_ = f32[1040,128]{1,0:T(8,128)S(1)} collective-permute-done((f32[1040,128]{1,0:T(8,128)S(1)}, f32[1040,128]{1,0:T(8,128)S(1)}, u32[]{:S(2)}, u32[]{:S(2)}) %collective-permute-start.5) | collective-permute-done | bytes 532512 | tf_op jit(solution)/shard_map/ppermute | solution.py:47
  72.0 1.1 pad_maximum_fusion.1
  73.1 1.9 %collective-permute-start.6 = (f32[2080,128]{1,0:T(8,128)}, f32[2080,128]{1,0:T(8,128)}, u32[]{:S(2)}, u32[]{:S(2)}) collective-permute-start(f32[2080,128]{1,0:T(8,128)} %pad_maximum_fusion.1), channel_id=1, source_target_pairs={{0,4},{1,29},{4,0},{5,9},{8,12},{9,5},{12,8},{13,17},{16,20},{17,1... | collective-permute-start | bytes 3194888 | tf_op jit(solution)/shard_map/ppermute | solution.py:47
  75.0 3.4 %collective-permute-done.7.refs_7_ = f32[2328,128]{1,0:T(8,128)S(1)} collective-permute-done((f32[2328,128]{1,0:T(8,128)}, f32[2328,128]{1,0:T(8,128)S(1)}, u32[]{:S(2)}, u32[]{:S(2)}) %collective-permute-start.7) | collective-permute-done | bytes 1191968 | tf_op jit(solution)/shard_map/ppermute | solution.py:33
  78.4 4.7 %collective-permute-start.9 = (f32[2328,128]{1,0:T(8,128)S(1)}, f32[2328,128]{1,0:T(8,128)S(1)}, u32[]{:S(2)}, u32[]{:S(2)}) collective-permute-start(f32[2328,128]{1,0:T(8,128)S(1)} %collective-permute-done.7.refs_7_), channel_id=1, source_target_pairs={{0,384},{1,129},{128,256},{129,1},{256,128},{257,385},{384,0},{385... | collective-permute-start | bytes 3575816 | tf_op jit(solution)/shard_map/ppermute | solution.py:33
  83.1 0.0 copy-done.10
  83.1 0.1 concatenate.18.refs_0_
  83.2 1.3 %copy-done.3 = bf16[640,1024]{1,0:T(8,128)(2,1)S(1)} copy-done((bf16[640,1024]{1,0:T(8,128)(2,1)S(1)}, bf16[640,1024]{1,0:T(8,128)(2,1)}, u32[]{:S(2)}) %copy-start.3) | copy-done | bytes 1310744
  84.5 1.3 %copy-done.5 = bf16[640,1024]{1,0:T(8,128)(2,1)S(1)} copy-done((bf16[640,1024]{1,0:T(8,128)(2,1)S(1)}, bf16[640,1024]{1,0:T(8,128)(2,1)}, u32[]{:S(2)}) %copy-start.5) | copy-done | bytes 1310744
  85.9 5.5 %shard_map.75 = (bf16[512,1024]{1,0:T(8,128)(2,1)S(1)}, bf16[512,1024]{1,0:T(8,128)(2,1)S(1)}, f32[512,1024]{1,0:T(8,128)S(1)}) custom-call(s32[149]{0:T(256)S(1)} %concatenate.18.refs_0_, f32[520,128]{1,0:T(8,128)S(1)} %copy-done.1, f32[520,128]{1,0:T(8,128)S(1)} %collective-permute-done.1.refs_2_, f32[1040,128]{1,0:T(8,128)S(1)} %collective-permute-done.5.refs_3_, ...), custom_call_target="tpu_custom_call" | custom-call | flops 2013265920 | bytes 16777216 | tf_op jit(solution)/shard_map/pallas_call | solution.py:369
  91.3 0.0 collective-permute-done.8.refs_8_
  91.3 0.0 collective-permute-done.6.refs_1_
  91.4 9.0 %shard_map.76 = (bf16[512,1408]{1,0:T(8,128)(2,1)S(1)}, bf16[512,1408]{1,0:T(8,128)(2,1)S(1)}, f32[512,1024]{1,0:T(8,128)S(1)}) custom-call(s32[149]{0:T(256)S(1)} %concatenate.18.refs_0_, f32[2080,128]{1,0:T(8,128)} %collective-permute-done.6.refs_1_, bf16[512,1024]{1,0:T(8,128)(2,1)S(1)} %get-tuple-element.47.refs_2_, ...), custom_call_target="tpu_custom_call" | custom-call | flops 3221225472 | bytes 16777216 | tf_op jit(solution)/shard_map/pallas_call | solution.py:383
  100.4 0.0 collective-permute-done.9.refs_3_
  100.4 2.9 %shard_map.77 = (f32[256,1024]{1,0:T(8,128)S(1)}, f32[128,1024]{1,0:T(8,128)S(1)}, f32[128,1024]{1,0:T(8,128)S(1)}) custom-call(bf16[512,1408]{1,0:T(8,128)(2,1)S(1)} %get-tuple-element.53.refs_0_, bf16[512,1408]{1,0:T(8,128)(2,1)S(1)} %get-tuple-element.54.refs_1_, f32[512,1024]{1,0:T(8,128)S(1)} %get-tuple-element.55.refs_2_, ...), custom_call_target="tpu_custom_call" | custom-call | flops 1207959552 | bytes 16777216 | tf_op jit(solution)/shard_map/pallas_call | solution.py:401
  103.3 1.9 %collective-permute-start.10 = (f32[256,1024]{1,0:T(8,128)S(1)}, f32[256,1024]{1,0:T(8,128)S(1)}, u32[]{:S(2)}, u32[]{:S(2)}) collective-permute-start(f32[256,1024]{1,0:T(8,128)S(1)} %get-tuple-element.57), channel_id=1, source_target_pairs={{0,1},{1,0},{2,3},{3,2},{4,5},{5,4},{6,7},{7,6},{8,9},{9,8},{10,11... | collective-permute-start | bytes 3145736 | tf_op jit(solution)/shard_map/ppermute | solution.py:68
  105.2 2.6 %collective-permute-done.10 = f32[256,1024]{1,0:T(8,128)S(1)} collective-permute-done((f32[256,1024]{1,0:T(8,128)S(1)}, f32[256,1024]{1,0:T(8,128)S(1)}, u32[]{:S(2)}, u32[]{:S(2)}) %collective-permute-start.10) | collective-permute-done | bytes 1048608 | tf_op jit(solution)/shard_map/ppermute | solution.py:68
  107.8 0.1 slice_add_fusion
  107.9 5.4 %collective-permute-start.11 = (f32[128,1024]{1,0:T(8,128)S(1)}, f32[128,1024]{1,0:T(8,128)S(1)}, u32[]{:S(2)}, u32[]{:S(2)}) collective-permute-start(f32[128,1024]{1,0:T(8,128)S(1)} %slice_add_fusion), channel_id=1, source_target_pairs={{0,2},{2,0},{1,3},{3,1},{4,6},{6,4},{5,7},{7,5},{8,10},{10,8},{9,1... | collective-permute-start | bytes 1572872 | tf_op jit(solution)/shard_map/ppermute | solution.py:68
  113.3 12.2 %collective-permute-done.11 = f32[128,1024]{1,0:T(8,128)S(1)} collective-permute-done((f32[128,1024]{1,0:T(8,128)S(1)}, f32[128,1024]{1,0:T(8,128)S(1)}, u32[]{:S(2)}, u32[]{:S(2)}) %collective-permute-start.11) | collective-permute-done | bytes 524320 | tf_op jit(solution)/shard_map/ppermute | solution.py:68
  125.5 0.9 fusion
  (13 shorter events, 0.1 us)
Async XLA Ops:
  2.9 27.4 %copy-start = (f32[776,128]{1,0:T(8,128)S(1)}, f32[776,128]{1,0:T(8,128)}, u32[]{:S(2)}) copy-start(f32[776,128]{1,0:T(8,128)} %get-tuple-element.32.refs_0_) | copy-start | bytes 1191940
  2.9 16.6 %collective-permute-start = (f32[776,128]{1,0:T(8,128)}, f32[776,128]{1,0:T(8,128)S(1)}, u32[]{:S(2)}, u32[]{:S(2)}) collective-permute-start(f32[776,128]{1,0:T(8,128)} %get-tuple-element.32.refs_0_), channel_id=1, source_target_pairs={{0,32},{1,97},{32,0},{33,65},{64,96},{65,33},{96,64},{97,1},{2,34}... | collective-permute-start | bytes 1191944 | tf_op jit(solution)/shard_map/ppermute | solution.py:33
  9.1 21.1 %collective-permute-start.2 = (f32[776,128]{1,0:T(8,128)}, f32[776,128]{1,0:T(8,128)S(1)}, u32[]{:S(2)}, u32[]{:S(2)}) collective-permute-start(f32[776,128]{1,0:T(8,128)} %get-tuple-element.32.refs_0_), channel_id=1, source_target_pairs={{0,128},{1,385},{128,0},{129,257},{256,384},{257,129},{384,256},{3... | collective-permute-start | bytes 1191944 | tf_op jit(solution)/shard_map/ppermute | solution.py:33
  20.5 14.5 %copy-start.1 = (f32[520,128]{1,0:T(8,128)S(1)}, f32[520,128]{1,0:T(8,128)}, u32[]{:S(2)}) copy-start(f32[520,128]{1,0:T(8,128)} %get-tuple-element.34.refs_1_) | copy-start | bytes 798724
  20.5 27.2 %collective-permute-start.4 = (f32[1560,128]{1,0:T(8,128)S(1)}, f32[1560,128]{1,0:T(8,128)S(1)}, u32[]{:S(2)}, u32[]{:S(2)}) collective-permute-start(f32[1560,128]{1,0:T(8,128)S(1)} %pad_maximum_fusion.2), channel_id=1, source_target_pairs={{0,96},{1,33},{32,64},{33,1},{64,32},{65,97},{96,0},{97,65},{2,98}... | collective-permute-start | bytes 2396168 | tf_op jit(solution)/shard_map/ppermute | solution.py:33
  30.3 15.2 %collective-permute-start.3 = (f32[1552,128]{1,0:T(8,128)S(1)}, f32[1552,128]{1,0:T(8,128)S(1)}, u32[]{:S(2)}, u32[]{:S(2)}) collective-permute-start(f32[1552,128]{1,0:T(8,128)S(1)} %pad_maximum_fusion.3), channel_id=1, source_target_pairs={{0,384},{1,129},{128,256},{129,1},{256,128},{257,385},{384,0},{385... | collective-permute-start | bytes 2383880 | tf_op jit(solution)/shard_map/ppermute | solution.py:33
  35.0 15.1 %collective-permute-start.1 = (f32[520,128]{1,0:T(8,128)S(1)}, f32[520,128]{1,0:T(8,128)S(1)}, u32[]{:S(2)}, u32[]{:S(2)}) collective-permute-start(f32[520,128]{1,0:T(8,128)S(1)} %copy-done.1), channel_id=1, source_target_pairs={{0,16},{1,17},{4,20},{5,21},{8,24},{9,25},{12,28},{13,29},{16,0},{... | collective-permute-start | bytes 798728 | tf_op jit(solution)/shard_map/ppermute | solution.py:47
  51.2 27.2 %collective-permute-start.7 = (f32[2328,128]{1,0:T(8,128)}, f32[2328,128]{1,0:T(8,128)S(1)}, u32[]{:S(2)}, u32[]{:S(2)}) collective-permute-start(f32[2328,128]{1,0:T(8,128)} %pad_maximum_fusion), channel_id=1, source_target_pairs={{0,128},{1,385},{128,0},{129,257},{256,384},{257,129},{384,256},{3... | collective-permute-start | bytes 3575816 | tf_op jit(solution)/shard_map/ppermute | solution.py:33
  53.3 18.7 %collective-permute-start.5 = (f32[1040,128]{1,0:T(8,128)S(1)}, f32[1040,128]{1,0:T(8,128)S(1)}, u32[]{:S(2)}, u32[]{:S(2)}) collective-permute-start(f32[1040,128]{1,0:T(8,128)S(1)} %pad_maximum_fusion.4), channel_id=1, source_target_pairs={{0,8},{1,25},{4,28},{5,13},{8,0},{9,17},{12,20},{13,5},{16,24},{17... | collective-permute-start | bytes 1597448 | tf_op jit(solution)/shard_map/ppermute | solution.py:47
  55.6 35.8 %collective-permute-start.8 = (f32[2328,128]{1,0:T(8,128)}, f32[2328,128]{1,0:T(8,128)}, u32[]{:S(2)}, u32[]{:S(2)}) collective-permute-start(f32[2328,128]{1,0:T(8,128)} %pad_maximum_fusion), channel_id=1, source_target_pairs={{0,384},{1,129},{128,256},{129,1},{256,128},{257,385},{384,0},{385... | collective-permute-start | bytes 3575816 | tf_op jit(solution)/shard_map/ppermute | solution.py:33
  64.0 1.1 copy-start.4
  65.1 0.8 copy-start.8
  65.9 12.5 %copy-start.2 = (bf16[640,1024]{1,0:T(8,128)(2,1)}, bf16[640,1024]{1,0:T(8,128)(2,1)S(1)}, u32[]{:S(2)}) copy-start(bf16[640,1024]{1,0:T(8,128)(2,1)S(1)} %get-tuple-element.45.refs_4_) | copy-start | bytes 3932164
  65.9 17.2 %copy-start.6 = (bf16[256,1024]{1,0:T(8,128)(2,1)}, bf16[256,1024]{1,0:T(8,128)(2,1)S(1)}, u32[]{:S(2)}) copy-start(bf16[256,1024]{1,0:T(8,128)(2,1)S(1)} %get-tuple-element.50.refs_5_) | copy-start | bytes 1572868
  65.9 17.2 %copy-start.10 = (s32[144]{0:T(256)S(1)}, s32[144]{0:T(256)}, u32[]{:S(2)}) copy-start(s32[144]{0:T(256)} %constant.22.clone) | copy-start | bytes 1732
  73.1 18.2 %collective-permute-start.6 = (f32[2080,128]{1,0:T(8,128)}, f32[2080,128]{1,0:T(8,128)}, u32[]{:S(2)}, u32[]{:S(2)}) collective-permute-start(f32[2080,128]{1,0:T(8,128)} %pad_maximum_fusion.1), channel_id=1, source_target_pairs={{0,4},{1,29},{4,0},{5,9},{8,12},{9,5},{12,8},{13,17},{16,20},{17,1... | collective-permute-start | bytes 3194888 | tf_op jit(solution)/shard_map/ppermute | solution.py:47
  78.4 22.0 %collective-permute-start.9 = (f32[2328,128]{1,0:T(8,128)S(1)}, f32[2328,128]{1,0:T(8,128)S(1)}, u32[]{:S(2)}, u32[]{:S(2)}) collective-permute-start(f32[2328,128]{1,0:T(8,128)S(1)} %collective-permute-done.7.refs_7_), channel_id=1, source_target_pairs={{0,384},{1,129},{128,256},{129,1},{256,128},{257,385},{384,0},{385... | collective-permute-start | bytes 3575816 | tf_op jit(solution)/shard_map/ppermute | solution.py:33
  83.2 1.3 %copy-start.3 = (bf16[640,1024]{1,0:T(8,128)(2,1)S(1)}, bf16[640,1024]{1,0:T(8,128)(2,1)}, u32[]{:S(2)}) copy-start(bf16[640,1024]{1,0:T(8,128)(2,1)} %copy-done.2) | copy-start | bytes 3932164
  84.5 1.3 %copy-start.5 = (bf16[640,1024]{1,0:T(8,128)(2,1)S(1)}, bf16[640,1024]{1,0:T(8,128)(2,1)}, u32[]{:S(2)}) copy-start(bf16[640,1024]{1,0:T(8,128)(2,1)} %copy-done.4) | copy-start | bytes 3932164
  85.9 5.5 %copy-start.7 = (bf16[256,1024]{1,0:T(8,128)(2,1)S(1)}, bf16[256,1024]{1,0:T(8,128)(2,1)}, u32[]{:S(2)}) copy-start(bf16[256,1024]{1,0:T(8,128)(2,1)} %copy-done.6) | copy-start | bytes 1572868
  85.9 5.5 %copy-start.9 = (bf16[256,1024]{1,0:T(8,128)(2,1)S(1)}, bf16[256,1024]{1,0:T(8,128)(2,1)}, u32[]{:S(2)}) copy-start(bf16[256,1024]{1,0:T(8,128)(2,1)} %copy-done.8) | copy-start | bytes 1572868
  103.3 4.6 %collective-permute-start.10 = (f32[256,1024]{1,0:T(8,128)S(1)}, f32[256,1024]{1,0:T(8,128)S(1)}, u32[]{:S(2)}, u32[]{:S(2)}) collective-permute-start(f32[256,1024]{1,0:T(8,128)S(1)} %get-tuple-element.57), channel_id=1, source_target_pairs={{0,1},{1,0},{2,3},{3,2},{4,5},{5,4},{6,7},{7,6},{8,9},{9,8},{10,11... | collective-permute-start | bytes 3145736 | tf_op jit(solution)/shard_map/ppermute | solution.py:68
  107.9 17.6 %collective-permute-start.11 = (f32[128,1024]{1,0:T(8,128)S(1)}, f32[128,1024]{1,0:T(8,128)S(1)}, u32[]{:S(2)}, u32[]{:S(2)}) collective-permute-start(f32[128,1024]{1,0:T(8,128)S(1)} %slice_add_fusion), channel_id=1, source_target_pairs={{0,2},{2,0},{1,3},{3,1},{4,6},{6,4},{5,7},{7,5},{8,10},{10,8},{9,1... | collective-permute-start | bytes 1572872 | tf_op jit(solution)/shard_map/ppermute | solution.py:68

commit v6 on v5

--- a/solution.py
+++ b/solution.py
@@ -409,6 +409,30 @@
     )(late_hi, late_lo, so_far, *operands)
 
 
+def join_kernel(*refs):
+    parts, out, sems = refs[:-2], refs[-2], refs[-1]
+    copies, row = [], 0
+    for k, part in enumerate(parts):
+        copies.append(pltpu.make_async_copy(part, out.at[pl.ds(row, part.shape[0])], sems.at[k]))
+        row += part.shape[0]
+    for copy in copies:
+        copy.start()
+    for copy in copies:
+        copy.wait()
+
+
+def join(parts):
+    rows = sum(part.shape[0] for part in parts)
+    return pl.pallas_call(
+        join_kernel,
+        out_shape=jax.ShapeDtypeStruct((rows, LANES), jnp.float32),
+        in_specs=[WHERE] * len(parts),
+        out_specs=IN_VMEM,
+        scratch_shapes=[pltpu.SemaphoreType.DMA((len(parts),))],
+        compiler_params=pltpu.CompilerParams(vmem_limit_bytes=4 * 1024 * 1024),
+    )(*parts)
+
+
 def body(a_values, a_places, a_counts, b_values, b_places, b_counts):
     hold = lax.optimization_barrier
     by_place = [holder for place in range(8) for core in range(2) for holder in holders(place, core)]
@@ -425,7 +449,7 @@
     )
     z_one = exchange(own, "zh", 0)
     x_one = exchange(own, "x", 0)
-    z_one, own_a = hold((z_one, own_a))
+    z_one, own_a, me = hold((z_one, own_a, me))
     a_one = exchange_col(own_a, 4)
 
     z_two = exchange(jnp.concatenate([own, z_one, own[:8]], axis=0), "zh", 1)
@@ -440,7 +464,7 @@
     b_all = [own, z_one, x_one, z_two, x_two]
     right = early_right(b_all)
     a_two, *right = hold((a_two, *right))
-    a_four = exchange_col(jnp.concatenate([own_a, a_one, a_two], axis=0), 1)
+    a_four = exchange_col(join([own_a, a_one, a_two]), 1)
     x_three, a_two = hold((x_three, a_two))
     near_hi, near_lo, total = first_product(me, (own_a, a_one, a_two), right[:2])
     b_all += [x_three, x_four, exchange(x_three, "x", 1)]

time: 127 us -> 124 us (0.976)
  the two profiles are of different devices: /device:TPU:56 before, /device:TPU:1 now
where the time goes in v6:
time: 124 us
  starting transfers between devices  63.9 us (52%)
  waiting for transfers between devices  31.7 us (26%)
  Pallas kernels  24 us (19%)
  other arithmetic  2.18 us (2%)
    ppermute x7, starting transfers between devices, exchange(): return lax.ppermute(array, (axis, 'core'), route)  36.1 us
    ppermute x3, starting transfers between devices, exchange_col(): return lax.ppermute(array, ('col', 'core'), route)  18.9 us
    ppermute x2, waiting for transfers between devices, swap(): return lax.ppermute(array, axis, [(0, 1), (1, 0)])  14.2 us
    ppermute x3, waiting for transfers between devices, exchange_col(): return lax.ppermute(array, ('col', 'core'), route)  9.97 us
    pallas_call x1, Pallas kernels, middle_product(): pl.pallas_call(lambda *refs: middle_kernel(len(operands), *refs), out_sha...  9.44 us
    ppermute x2, starting transfers between devices, swap(): return lax.ppermute(array, axis, [(0, 1), (1, 0)])  8.84 us
    ppermute x7, waiting for transfers between devices, exchange(): return lax.ppermute(array, (axis, 'core'), route)  7.46 us
    pallas_call x1, Pallas kernels, first_product(): pl.pallas_call(first_kernel, out_shape=(near, near, jax.ShapeDtypeStruct(...  5.47 us
  transfers between devices with their start and end apart: 12, of which 7 were waited for; matrix products, arithmetic and copies ran while one was open for 2% of the time, Pallas kernels for 15%

profile of v6, /device:TPU:1, one launch (start us, length us, event | category | flops | bytes accessed | tf_op | source)
XLA Modules:
  0.0 123.6 jit_solution(10781317187968604689)
XLA Ops:
  0.0 0.0 copy-start.2
  0.7 2.2 %shard_map.73 = (f32[520,128]{1,0:T(8,128)}, f32[776,128]{1,0:T(8,128)}) custom-call(s32[2]{0:T(128)} %bitcast.18, s32[1,1,1]{2,1,0:T(1,128)S(6)} %copy.8.refs_1_, s32[2,2,8]{2,1,0:T(2,128)} %bitcast.16, s32[2,24]{1,0:T(2,128)} %bitcast.17, f32[24,64,64]{2,1,0:T(8,128)} %bitcast.14, f32[16,64,64]{2,1,0:T(8,128)} %bitcast.15), custom_call_target="tpu_custom_call" | custom-call | tf_op jit(solution)/shard_map/pallas_call | solution.py:110
  2.9 0.0 copy-start
  2.9 11.6 %collective-permute-start = (f32[776,128]{1,0:T(8,128)}, f32[776,128]{1,0:T(8,128)S(1)}, u32[]{:S(2)}, u32[]{:S(2)}) collective-permute-start(f32[776,128]{1,0:T(8,128)} %get-tuple-element.33.refs_0_), channel_id=1, source_target_pairs={{0,32},{1,97},{32,0},{33,65},{64,96},{65,33},{96,64},{97,1},{2,34}... | collective-permute-start | bytes 1191944 | tf_op jit(solution)/shard_map/ppermute | solution.py:33
  14.5 4.4 %collective-permute-start.2 = (f32[776,128]{1,0:T(8,128)}, f32[776,128]{1,0:T(8,128)S(1)}, u32[]{:S(2)}, u32[]{:S(2)}) collective-permute-start(f32[776,128]{1,0:T(8,128)} %get-tuple-element.33.refs_0_), channel_id=1, source_target_pairs={{0,128},{1,385},{128,0},{129,257},{256,384},{257,129},{384,256},{3... | collective-permute-start | bytes 1191944 | tf_op jit(solution)/shard_map/ppermute | solution.py:33
  18.9 0.7 slice.12
  19.6 0.0 copy-done.2
  19.6 0.1 concatenate.15.refs_0_
  19.7 2.0 %collective-permute-done.refs_1_ = f32[776,128]{1,0:T(8,128)S(1)} collective-permute-done((f32[776,128]{1,0:T(8,128)}, f32[776,128]{1,0:T(8,128)S(1)}, u32[]{:S(2)}, u32[]{:S(2)}) %collective-permute-start) | collective-permute-done | bytes 397344 | tf_op jit(solution)/shard_map/ppermute | solution.py:33
  21.7 1.0 pad_maximum_fusion.1
  22.8 0.0 copy-start.1
  22.8 4.8 %collective-permute-start.4 = (f32[1560,128]{1,0:T(8,128)S(1)}, f32[1560,128]{1,0:T(8,128)S(1)}, u32[]{:S(2)}, u32[]{:S(2)}) collective-permute-start(f32[1560,128]{1,0:T(8,128)S(1)} %pad_maximum_fusion.1), channel_id=1, source_target_pairs={{0,96},{1,33},{32,64},{33,1},{64,32},{65,97},{96,0},{97,65},{2,98}... | collective-permute-start | bytes 2396168 | tf_op jit(solution)/shard_map/ppermute | solution.py:33
  27.6 0.0 collective-permute-done.2.refs_2_
  27.6 0.0 copy-done
  27.6 0.1 pad_maximum_fusion.2
  27.7 3.1 %collective-permute-start.3 = (f32[1552,128]{1,0:T(8,128)S(1)}, f32[1552,128]{1,0:T(8,128)S(1)}, u32[]{:S(2)}, u32[]{:S(2)}) collective-permute-start(f32[1552,128]{1,0:T(8,128)S(1)} %pad_maximum_fusion.2), channel_id=1, source_target_pairs={{0,384},{1,129},{128,256},{129,1},{256,128},{257,385},{384,0},{385... | collective-permute-start | bytes 2383880 | tf_op jit(solution)/shard_map/ppermute | solution.py:33
  30.8 0.0 copy-done.1
  30.8 7.5 %collective-permute-start.1 = (f32[520,128]{1,0:T(8,128)S(1)}, f32[520,128]{1,0:T(8,128)S(1)}, u32[]{:S(2)}, u32[]{:S(2)}) collective-permute-start(f32[520,128]{1,0:T(8,128)S(1)} %copy-done.1), channel_id=1, source_target_pairs={{0,16},{1,17},{4,20},{5,21},{8,24},{9,25},{12,28},{13,29},{16,0},{... | collective-permute-start | bytes 798728 | tf_op jit(solution)/shard_map/ppermute | solution.py:47
  38.3 2.5 %collective-permute-done.3.refs_4_ = f32[1552,128]{1,0:T(8,128)S(1)} collective-permute-done((f32[1552,128]{1,0:T(8,128)S(1)}, f32[1552,128]{1,0:T(8,128)S(1)}, u32[]{:S(2)}, u32[]{:S(2)}) %collective-permute-start.3) | collective-permute-done | bytes 794656 | tf_op jit(solution)/shard_map/ppermute | solution.py:33
  40.8 2.9 %collective-permute-done.4.refs_3_ = f32[1560,128]{1,0:T(8,128)S(1)} collective-permute-done((f32[1560,128]{1,0:T(8,128)S(1)}, f32[1560,128]{1,0:T(8,128)S(1)}, u32[]{:S(2)}, u32[]{:S(2)}) %collective-permute-start.4) | collective-permute-done | bytes 798752 | tf_op jit(solution)/shard_map/ppermute | solution.py:33
  43.7 0.1 slice.13
  43.7 0.1 pad_maximum_fusion
  43.8 8.4 %collective-permute-start.7 = (f32[2328,128]{1,0:T(8,128)S(1)}, f32[2328,128]{1,0:T(8,128)S(1)}, u32[]{:S(2)}, u32[]{:S(2)}) collective-permute-start(f32[2328,128]{1,0:T(8,128)S(1)} %pad_maximum_fusion), channel_id=1, source_target_pairs={{0,128},{1,385},{128,0},{129,257},{256,384},{257,129},{384,256},{3... | collective-permute-start | bytes 3575816 | tf_op jit(solution)/shard_map/ppermute | solution.py:33
  52.2 0.0 collective-permute-done.1.refs_1_.refs_2_
  52.3 5.9 %collective-permute-start.5 = (f32[1040,128]{1,0:T(8,128)S(1)}, f32[1040,128]{1,0:T(8,128)S(1)}, u32[]{:S(2)}, u32[]{:S(2)}) collective-permute-start(f32[1040,128]{1,0:T(8,128)S(1)} %pad_maximum_fusion.3), channel_id=1, source_target_pairs={{0,8},{1,25},{4,28},{5,13},{8,0},{9,17},{12,20},{13,5},{16,24},{17... | collective-permute-start | bytes 1597448 | tf_op jit(solution)/shard_map/ppermute | solution.py:47
  58.2 1.9 %collective-permute-start.8 = (f32[2328,128]{1,0:T(8,128)S(1)}, f32[2328,128]{1,0:T(8,128)S(1)}, u32[]{:S(2)}, u32[]{:S(2)}) collective-permute-start(f32[2328,128]{1,0:T(8,128)S(1)} %pad_maximum_fusion), channel_id=1, source_target_pairs={{0,384},{1,129},{128,256},{129,1},{256,128},{257,385},{384,0},{385... | collective-permute-start | bytes 3575816 | tf_op jit(solution)/shard_map/ppermute | solution.py:33
  60.1 3.9 %shard_map.74 = (bf16[640,1024]{1,0:T(8,128)(2,1)S(1)}, bf16[640,1024]{1,0:T(8,128)(2,1)S(1)}, bf16[256,1024]{1,0:T(8,128)(2,1)S(1)}, bf16[256,1024]{1,0:T(8,128)(2,1)S(1)}) custom-call(f32[776,128]{1,0:T(8,128)S(1)} %copy-done, f32[776,128]{1,0:T(8,128)S(1)} %collective-permute-done.refs_1_, f32[776,128]{1,0:T(8,128)S(1)} %collective-permute-done.2.refs_2_, ...), custom_call_target="tpu_custom_call" | custom-call | flops 1000000000 | bytes 16777216 | tf_op jit(solution)/shard_map/pallas_call | solution.py:356
  64.0 4.8 %collective-permute-done.5.refs_2_.refs_3_ = f32[1040,128]{1,0:T(8,128)S(1)} collective-permute-done((f32[1040,128]{1,0:T(8,128)S(1)}, f32[1040,128]{1,0:T(8,128)S(1)}, u32[]{:S(2)}, u32[]{:S(2)}) %collective-permute-start.5) | collective-permute-done | bytes 532512 | tf_op jit(solution)/shard_map/ppermute | solution.py:47
  68.8 0.1 shard_map.75
  68.9 5.6 %collective-permute-start.6 = (f32[2080,128]{1,0:T(8,128)S(1)}, f32[2080,128]{1,0:T(8,128)S(1)}, u32[]{:S(2)}, u32[]{:S(2)}) collective-permute-start(f32[2080,128]{1,0:T(8,128)S(1)} %shard_map.75), channel_id=1, source_target_pairs={{0,4},{1,29},{4,0},{5,9},{8,12},{9,5},{12,8},{13,17},{16,20},{17,1... | collective-permute-start | bytes 3194888 | tf_op jit(solution)/shard_map/ppermute | solution.py:47
  74.5 0.0 collective-permute-done.7.refs_7_
  74.5 1.9 %collective-permute-start.9 = (f32[2328,128]{1,0:T(8,128)S(1)}, f32[2328,128]{1,0:T(8,128)S(1)}, u32[]{:S(2)}, u32[]{:S(2)}) collective-permute-start(f32[2328,128]{1,0:T(8,128)S(1)} %collective-permute-done.7.refs_7_), channel_id=1, source_target_pairs={{0,384},{1,129},{128,256},{129,1},{256,128},{257,385},{384,0},{385... | collective-permute-start | bytes 3575816 | tf_op jit(solution)/shard_map/ppermute | solution.py:33
  76.4 5.5 %shard_map.76 = (bf16[512,1024]{1,0:T(8,128)(2,1)S(1)}, bf16[512,1024]{1,0:T(8,128)(2,1)S(1)}, f32[512,1024]{1,0:T(8,128)S(1)}) custom-call(s32[149]{0:T(256)S(1)} %concatenate.15.refs_0_, f32[520,128]{1,0:T(8,128)S(1)} %copy-done.1, f32[520,128]{1,0:T(8,128)S(1)} %collective-permute-done.1.refs_1_.refs_2_, ...), custom_call_target="tpu_custom_call" | custom-call | flops 2013265920 | bytes 16777216 | tf_op jit(solution)/shard_map/pallas_call | solution.py:369
  81.9 0.0 collective-permute-done.8.refs_8_
  81.9 5.2 %collective-permute-done.6.refs_1_ = f32[2080,128]{1,0:T(8,128)S(1)} collective-permute-done((f32[2080,128]{1,0:T(8,128)S(1)}, f32[2080,128]{1,0:T(8,128)S(1)}, u32[]{:S(2)}, u32[]{:S(2)}) %collective-permute-start.6) | collective-permute-done | bytes 1064992 | tf_op jit(solution)/shard_map/ppermute | solution.py:47
  87.1 9.4 %shard_map.77 = (bf16[512,1408]{1,0:T(8,128)(2,1)S(1)}, bf16[512,1408]{1,0:T(8,128)(2,1)S(1)}, f32[512,1024]{1,0:T(8,128)S(1)}) custom-call(s32[149]{0:T(256)S(1)} %concatenate.15.refs_0_, f32[2080,128]{1,0:T(8,128)S(1)} %collective-permute-done.6.refs_1_, bf16[512,1024]{1,0:T(8,128)(2,1)S(1)} %get-tuple-element.49.refs_2_, ...), custom_call_target="tpu_custom_call" | custom-call | flops 3221225472 | bytes 16777216 | tf_op jit(solution)/shard_map/pallas_call | solution.py:383
  96.6 0.0 collective-permute-done.9.refs_3_
  96.6 2.9 %shard_map.78 = (f32[256,1024]{1,0:T(8,128)S(1)}, f32[128,1024]{1,0:T(8,128)S(1)}, f32[128,1024]{1,0:T(8,128)S(1)}) custom-call(bf16[512,1408]{1,0:T(8,128)(2,1)S(1)} %get-tuple-element.55.refs_0_, bf16[512,1408]{1,0:T(8,128)(2,1)S(1)} %get-tuple-element.56.refs_1_, f32[512,1024]{1,0:T(8,128)S(1)} %get-tuple-element.57.refs_2_, ...), custom_call_target="tpu_custom_call" | custom-call | flops 1207959552 | bytes 16777216 | tf_op jit(solution)/shard_map/pallas_call | solution.py:401
  99.5 2.4 %collective-permute-start.10 = (f32[256,1024]{1,0:T(8,128)S(1)}, f32[256,1024]{1,0:T(8,128)S(1)}, u32[]{:S(2)}, u32[]{:S(2)}) collective-permute-start(f32[256,1024]{1,0:T(8,128)S(1)} %get-tuple-element.59), channel_id=1, source_target_pairs={{0,1},{1,0},{2,3},{3,2},{4,5},{5,4},{6,7},{7,6},{8,9},{9,8},{10,11... | collective-permute-start | bytes 3145736 | tf_op jit(solution)/shard_map/ppermute | solution.py:68
  102.0 2.3 %collective-permute-done.10 = f32[256,1024]{1,0:T(8,128)S(1)} collective-permute-done((f32[256,1024]{1,0:T(8,128)S(1)}, f32[256,1024]{1,0:T(8,128)S(1)}, u32[]{:S(2)}, u32[]{:S(2)}) %collective-permute-start.10) | collective-permute-done | bytes 1048608 | tf_op jit(solution)/shard_map/ppermute | solution.py:68
  104.2 0.1 slice_add_fusion
  104.3 6.4 %collective-permute-start.11 = (f32[128,1024]{1,0:T(8,128)S(1)}, f32[128,1024]{1,0:T(8,128)S(1)}, u32[]{:S(2)}, u32[]{:S(2)}) collective-permute-start(f32[128,1024]{1,0:T(8,128)S(1)} %slice_add_fusion), channel_id=1, source_target_pairs={{0,2},{2,0},{1,3},{3,1},{4,6},{6,4},{5,7},{7,5},{8,10},{10,8},{9,1... | collective-permute-start | bytes 1572872 | tf_op jit(solution)/shard_map/ppermute | solution.py:68
  110.7 12.0 %collective-permute-done.11 = f32[128,1024]{1,0:T(8,128)S(1)} collective-permute-done((f32[128,1024]{1,0:T(8,128)S(1)}, f32[128,1024]{1,0:T(8,128)S(1)}, u32[]{:S(2)}, u32[]{:S(2)}) %collective-permute-start.11) | collective-permute-done | bytes 524320 | tf_op jit(solution)/shard_map/ppermute | solution.py:68
  122.7 0.9 fusion
  (1 shorter events, 0.0 us)
Async XLA Ops:
  0.0 19.6 %copy-start.2 = (s32[144]{0:T(256)S(1)}, s32[144]{0:T(256)}, u32[]{:S(2)}) copy-start(s32[144]{0:T(256)} %constant.22.clone) | copy-start | bytes 1732
  2.9 24.7 %copy-start = (f32[776,128]{1,0:T(8,128)S(1)}, f32[776,128]{1,0:T(8,128)}, u32[]{:S(2)}) copy-start(f32[776,128]{1,0:T(8,128)} %get-tuple-element.33.refs_0_) | copy-start | bytes 1191940
  2.9 18.8 %collective-permute-start = (f32[776,128]{1,0:T(8,128)}, f32[776,128]{1,0:T(8,128)S(1)}, u32[]{:S(2)}, u32[]{:S(2)}) collective-permute-start(f32[776,128]{1,0:T(8,128)} %get-tuple-element.33.refs_0_), channel_id=1, source_target_pairs={{0,32},{1,97},{32,0},{33,65},{64,96},{65,33},{96,64},{97,1},{2,34}... | collective-permute-start | bytes 1191944 | tf_op jit(solution)/shard_map/ppermute | solution.py:33
  14.5 13.0 %collective-permute-start.2 = (f32[776,128]{1,0:T(8,128)}, f32[776,128]{1,0:T(8,128)S(1)}, u32[]{:S(2)}, u32[]{:S(2)}) collective-permute-start(f32[776,128]{1,0:T(8,128)} %get-tuple-element.33.refs_0_), channel_id=1, source_target_pairs={{0,128},{1,385},{128,0},{129,257},{256,384},{257,129},{384,256},{3... | collective-permute-start | bytes 1191944 | tf_op jit(solution)/shard_map/ppermute | solution.py:33
  22.8 8.0 %copy-start.1 = (f32[520,128]{1,0:T(8,128)S(1)}, f32[520,128]{1,0:T(8,128)}, u32[]{:S(2)}) copy-start(f32[520,128]{1,0:T(8,128)} %get-tuple-element.36.refs_0_.refs_1_) | copy-start | bytes 798724
  22.8 20.9 %collective-permute-start.4 = (f32[1560,128]{1,0:T(8,128)S(1)}, f32[1560,128]{1,0:T(8,128)S(1)}, u32[]{:S(2)}, u32[]{:S(2)}) collective-permute-start(f32[1560,128]{1,0:T(8,128)S(1)} %pad_maximum_fusion.1), channel_id=1, source_target_pairs={{0,96},{1,33},{32,64},{33,1},{64,32},{65,97},{96,0},{97,65},{2,98}... | collective-permute-start | bytes 2396168 | tf_op jit(solution)/shard_map/ppermute | solution.py:33
  27.7 13.1 %collective-permute-start.3 = (f32[1552,128]{1,0:T(8,128)S(1)}, f32[1552,128]{1,0:T(8,128)S(1)}, u32[]{:S(2)}, u32[]{:S(2)}) collective-permute-start(f32[1552,128]{1,0:T(8,128)S(1)} %pad_maximum_fusion.2), channel_id=1, source_target_pairs={{0,384},{1,129},{128,256},{129,1},{256,128},{257,385},{384,0},{385... | collective-permute-start | bytes 2383880 | tf_op jit(solution)/shard_map/ppermute | solution.py:33
  30.8 21.5 %collective-permute-start.1 = (f32[520,128]{1,0:T(8,128)S(1)}, f32[520,128]{1,0:T(8,128)S(1)}, u32[]{:S(2)}, u32[]{:S(2)}) collective-permute-start(f32[520,128]{1,0:T(8,128)S(1)} %copy-done.1), channel_id=1, source_target_pairs={{0,16},{1,17},{4,20},{5,21},{8,24},{9,25},{12,28},{13,29},{16,0},{... | collective-permute-start | bytes 798728 | tf_op jit(solution)/shard_map/ppermute | solution.py:47
  43.8 30.7 %collective-permute-start.7 = (f32[2328,128]{1,0:T(8,128)S(1)}, f32[2328,128]{1,0:T(8,128)S(1)}, u32[]{:S(2)}, u32[]{:S(2)}) collective-permute-start(f32[2328,128]{1,0:T(8,128)S(1)} %pad_maximum_fusion), channel_id=1, source_target_pairs={{0,128},{1,385},{128,0},{129,257},{256,384},{257,129},{384,256},{3... | collective-permute-start | bytes 3575816 | tf_op jit(solution)/shard_map/ppermute | solution.py:33
  52.3 16.5 %collective-permute-start.5 = (f32[1040,128]{1,0:T(8,128)S(1)}, f32[1040,128]{1,0:T(8,128)S(1)}, u32[]{:S(2)}, u32[]{:S(2)}) collective-permute-start(f32[1040,128]{1,0:T(8,128)S(1)} %pad_maximum_fusion.3), channel_id=1, source_target_pairs={{0,8},{1,25},{4,28},{5,13},{8,0},{9,17},{12,20},{13,5},{16,24},{17... | collective-permute-start | bytes 1597448 | tf_op jit(solution)/shard_map/ppermute | solution.py:47
  58.2 23.7 %collective-permute-start.8 = (f32[2328,128]{1,0:T(8,128)S(1)}, f32[2328,128]{1,0:T(8,128)S(1)}, u32[]{:S(2)}, u32[]{:S(2)}) collective-permute-start(f32[2328,128]{1,0:T(8,128)S(1)} %pad_maximum_fusion), channel_id=1, source_target_pairs={{0,384},{1,129},{128,256},{129,1},{256,128},{257,385},{384,0},{385... | collective-permute-start | bytes 3575816 | tf_op jit(solution)/shard_map/ppermute | solution.py:33
  68.9 18.2 %collective-permute-start.6 = (f32[2080,128]{1,0:T(8,128)S(1)}, f32[2080,128]{1,0:T(8,128)S(1)}, u32[]{:S(2)}, u32[]{:S(2)}) collective-permute-start(f32[2080,128]{1,0:T(8,128)S(1)} %shard_map.75), channel_id=1, source_target_pairs={{0,4},{1,29},{4,0},{5,9},{8,12},{9,5},{12,8},{13,17},{16,20},{17,1... | collective-permute-start | bytes 3194888 | tf_op jit(solution)/shard_map/ppermute | solution.py:47
  74.5 22.1 %collective-permute-start.9 = (f32[2328,128]{1,0:T(8,128)S(1)}, f32[2328,128]{1,0:T(8,128)S(1)}, u32[]{:S(2)}, u32[]{:S(2)}) collective-permute-start(f32[2328,128]{1,0:T(8,128)S(1)} %collective-permute-done.7.refs_7_), channel_id=1, source_target_pairs={{0,384},{1,129},{128,256},{129,1},{256,128},{257,385},{384,0},{385... | collective-permute-start | bytes 3575816 | tf_op jit(solution)/shard_map/ppermute | solution.py:33
  99.5 4.7 %collective-permute-start.10 = (f32[256,1024]{1,0:T(8,128)S(1)}, f32[256,1024]{1,0:T(8,128)S(1)}, u32[]{:S(2)}, u32[]{:S(2)}) collective-permute-start(f32[256,1024]{1,0:T(8,128)S(1)} %get-tuple-element.59), channel_id=1, source_target_pairs={{0,1},{1,0},{2,3},{3,2},{4,5},{5,4},{6,7},{7,6},{8,9},{9,8},{10,11... | collective-permute-start | bytes 3145736 | tf_op jit(solution)/shard_map/ppermute | solution.py:68
  104.3 18.4 %collective-permute-start.11 = (f32[128,1024]{1,0:T(8,128)S(1)}, f32[128,1024]{1,0:T(8,128)S(1)}, u32[]{:S(2)}, u32[]{:S(2)}) collective-permute-start(f32[128,1024]{1,0:T(8,128)S(1)} %slice_add_fusion), channel_id=1, source_target_pairs={{0,2},{2,0},{1,3},{3,1},{4,6},{6,4},{5,7},{7,5},{8,10},{10,8},{9,1... | collective-permute-start | bytes 1572872 | tf_op jit(solution)/shard_map/ppermute | solution.py:68

commit v7 on v6

--- a/solution.py
+++ b/solution.py
@@ -182,7 +182,7 @@
             a_hi[rows, lanes], a_lo[rows, lanes] = halves(block_pair(load, left, right))
         return 0
 
-    lax.fori_loop(0, 8, left_tile, 0, unroll=2)
+    lax.fori_loop(0, 8, left_tile, 0, unroll=4)
 
 
 def right_copies(call, b_in, b_f, spots_s, sem_b, sem_s):
@@ -215,7 +215,7 @@
                 b_hi[rows, lanes], b_lo[rows, lanes] = halves(block_pair(load, left, right))
         return 0
 
-    lax.fori_loop(0, tiles, right_tile, 0, unroll=3 if tiles == 3 else 2 - tiles % 2)
+    lax.fori_loop(0, tiles, right_tile, 0, unroll=3 if tiles % 3 == 0 else 2 - tiles % 2)
 
 
 def left_copies(parts, a_f, spots_s, sem_a, sem_s):

time: 124 us -> 124 us (level)
  no operation moved by 1% of the time
where the time goes in v7:
time: 124 us
  starting transfers between devices  64.2 us (52%)
  waiting for transfers between devices  31.9 us (26%)
  Pallas kernels  23.5 us (19%)
  other arithmetic  2.18 us (2%)
    ppermute x7, starting transfers between devices, exchange(): return lax.ppermute(array, (axis, 'core'), route)  36.1 us
    ppermute x3, starting transfers between devices, exchange_col(): return lax.ppermute(array, ('col', 'core'), route)  18.9 us
    ppermute x2, waiting for transfers between devices, swap(): return lax.ppermute(array, axis, [(0, 1), (1, 0)])  14.2 us
    ppermute x3, waiting for transfers between devices, exchange_col(): return lax.ppermute(array, ('col', 'core'), route)  10.2 us
    pallas_call x1, Pallas kernels, middle_product(): pl.pallas_call(lambda *refs: middle_kernel(len(operands), *refs), out_sha...  9.16 us
    ppermute x2, starting transfers between devices, swap(): return lax.ppermute(array, axis, [(0, 1), (1, 0)])  9.12 us
    ppermute x7, waiting for transfers between devices, exchange(): return lax.ppermute(array, (axis, 'core'), route)  7.46 us
    pallas_call x1, Pallas kernels, first_product(): pl.pallas_call(first_kernel, out_shape=(near, near, jax.ShapeDtypeStruct(...  5.25 us
  transfers between devices with their start and end apart: 12, of which 7 were waited for; matrix products, arithmetic and copies ran while one was open for 2% of the time, Pallas kernels for 15%

profile of v7, /device:TPU:1, one launch (start us, length us, event | category | flops | bytes accessed | tf_op | source)
XLA Modules:
  0.0 123.6 jit_solution(9061076395539651598)
XLA Ops:
  0.0 0.0 copy-start.2
  0.7 2.2 %shard_map.73 = (f32[520,128]{1,0:T(8,128)}, f32[776,128]{1,0:T(8,128)}) custom-call(s32[2]{0:T(128)} %bitcast.18, s32[1,1,1]{2,1,0:T(1,128)S(6)} %copy.8.refs_1_, s32[2,2,8]{2,1,0:T(2,128)} %bitcast.16, s32[2,24]{1,0:T(2,128)} %bitcast.17, f32[24,64,64]{2,1,0:T(8,128)} %bitcast.14, f32[16,64,64]{2,1,0:T(8,128)} %bitcast.15), custom_call_target="tpu_custom_call" | custom-call | tf_op jit(solution)/shard_map/pallas_call | solution.py:110
  2.9 0.0 copy-start
  2.9 11.6 %collective-permute-start = (f32[776,128]{1,0:T(8,128)}, f32[776,128]{1,0:T(8,128)S(1)}, u32[]{:S(2)}, u32[]{:S(2)}) collective-permute-start(f32[776,128]{1,0:T(8,128)} %get-tuple-element.33.refs_0_), channel_id=1, source_target_pairs={{0,32},{1,97},{32,0},{33,65},{64,96},{65,33},{96,64},{97,1},{2,34}... | collective-permute-start | bytes 1191944 | tf_op jit(solution)/shard_map/ppermute | solution.py:33
  14.5 4.4 %collective-permute-start.2 = (f32[776,128]{1,0:T(8,128)}, f32[776,128]{1,0:T(8,128)S(1)}, u32[]{:S(2)}, u32[]{:S(2)}) collective-permute-start(f32[776,128]{1,0:T(8,128)} %get-tuple-element.33.refs_0_), channel_id=1, source_target_pairs={{0,128},{1,385},{128,0},{129,257},{256,384},{257,129},{384,256},{3... | collective-permute-start | bytes 1191944 | tf_op jit(solution)/shard_map/ppermute | solution.py:33
  18.9 0.7 slice.12
  19.6 0.0 copy-done.2
  19.6 0.1 concatenate.15.refs_0_
  19.7 2.0 %collective-permute-done.refs_1_ = f32[776,128]{1,0:T(8,128)S(1)} collective-permute-done((f32[776,128]{1,0:T(8,128)}, f32[776,128]{1,0:T(8,128)S(1)}, u32[]{:S(2)}, u32[]{:S(2)}) %collective-permute-start) | collective-permute-done | bytes 397344 | tf_op jit(solution)/shard_map/ppermute | solution.py:33
  21.7 1.0 pad_maximum_fusion.1
  22.8 0.0 copy-start.1
  22.8 4.8 %collective-permute-start.4 = (f32[1560,128]{1,0:T(8,128)S(1)}, f32[1560,128]{1,0:T(8,128)S(1)}, u32[]{:S(2)}, u32[]{:S(2)}) collective-permute-start(f32[1560,128]{1,0:T(8,128)S(1)} %pad_maximum_fusion.1), channel_id=1, source_target_pairs={{0,96},{1,33},{32,64},{33,1},{64,32},{65,97},{96,0},{97,65},{2,98}... | collective-permute-start | bytes 2396168 | tf_op jit(solution)/shard_map/ppermute | solution.py:33
  27.6 0.0 collective-permute-done.2.refs_2_
  27.6 0.0 copy-done
  27.6 0.1 pad_maximum_fusion.2
  27.7 3.1 %collective-permute-start.3 = (f32[1552,128]{1,0:T(8,128)S(1)}, f32[1552,128]{1,0:T(8,128)S(1)}, u32[]{:S(2)}, u32[]{:S(2)}) collective-permute-start(f32[1552,128]{1,0:T(8,128)S(1)} %pad_maximum_fusion.2), channel_id=1, source_target_pairs={{0,384},{1,129},{128,256},{129,1},{256,128},{257,385},{384,0},{385... | collective-permute-start | bytes 2383880 | tf_op jit(solution)/shard_map/ppermute | solution.py:33
  30.8 0.0 copy-done.1
  30.8 7.5 %collective-permute-start.1 = (f32[520,128]{1,0:T(8,128)S(1)}, f32[520,128]{1,0:T(8,128)S(1)}, u32[]{:S(2)}, u32[]{:S(2)}) collective-permute-start(f32[520,128]{1,0:T(8,128)S(1)} %copy-done.1), channel_id=1, source_target_pairs={{0,16},{1,17},{4,20},{5,21},{8,24},{9,25},{12,28},{13,29},{16,0},{... | collective-permute-start | bytes 798728 | tf_op jit(solution)/shard_map/ppermute | solution.py:47
  38.3 2.5 %collective-permute-done.3.refs_4_ = f32[1552,128]{1,0:T(8,128)S(1)} collective-permute-done((f32[1552,128]{1,0:T(8,128)S(1)}, f32[1552,128]{1,0:T(8,128)S(1)}, u32[]{:S(2)}, u32[]{:S(2)}) %collective-permute-start.3) | collective-permute-done | bytes 794656 | tf_op jit(solution)/shard_map/ppermute | solution.py:33
  40.8 2.9 %collective-permute-done.4.refs_3_ = f32[1560,128]{1,0:T(8,128)S(1)} collective-permute-done((f32[1560,128]{1,0:T(8,128)S(1)}, f32[1560,128]{1,0:T(8,128)S(1)}, u32[]{:S(2)}, u32[]{:S(2)}) %collective-permute-start.4) | collective-permute-done | bytes 798752 | tf_op jit(solution)/shard_map/ppermute | solution.py:33
  43.7 0.1 slice.13
  43.7 0.1 pad_maximum_fusion
  43.8 8.4 %collective-permute-start.7 = (f32[2328,128]{1,0:T(8,128)S(1)}, f32[2328,128]{1,0:T(8,128)S(1)}, u32[]{:S(2)}, u32[]{:S(2)}) collective-permute-start(f32[2328,128]{1,0:T(8,128)S(1)} %pad_maximum_fusion), channel_id=1, source_target_pairs={{0,128},{1,385},{128,0},{129,257},{256,384},{257,129},{384,256},{3... | collective-permute-start | bytes 3575816 | tf_op jit(solution)/shard_map/ppermute | solution.py:33
  52.2 0.0 collective-permute-done.1.refs_1_.refs_2_
  52.3 5.9 %collective-permute-start.5 = (f32[1040,128]{1,0:T(8,128)S(1)}, f32[1040,128]{1,0:T(8,128)S(1)}, u32[]{:S(2)}, u32[]{:S(2)}) collective-permute-start(f32[1040,128]{1,0:T(8,128)S(1)} %pad_maximum_fusion.3), channel_id=1, source_target_pairs={{0,8},{1,25},{4,28},{5,13},{8,0},{9,17},{12,20},{13,5},{16,24},{17... | collective-permute-start | bytes 1597448 | tf_op jit(solution)/shard_map/ppermute | solution.py:47
  58.2 1.9 %collective-permute-start.8 = (f32[2328,128]{1,0:T(8,128)S(1)}, f32[2328,128]{1,0:T(8,128)S(1)}, u32[]{:S(2)}, u32[]{:S(2)}) collective-permute-start(f32[2328,128]{1,0:T(8,128)S(1)} %pad_maximum_fusion), channel_id=1, source_target_pairs={{0,384},{1,129},{128,256},{129,1},{256,128},{257,385},{384,0},{385... | collective-permute-start | bytes 3575816 | tf_op jit(solution)/shard_map/ppermute | solution.py:33
  60.1 3.9 %shard_map.74 = (bf16[640,1024]{1,0:T(8,128)(2,1)S(1)}, bf16[640,1024]{1,0:T(8,128)(2,1)S(1)}, bf16[256,1024]{1,0:T(8,128)(2,1)S(1)}, bf16[256,1024]{1,0:T(8,128)(2,1)S(1)}) custom-call(f32[776,128]{1,0:T(8,128)S(1)} %copy-done, f32[776,128]{1,0:T(8,128)S(1)} %collective-permute-done.refs_1_, f32[776,128]{1,0:T(8,128)S(1)} %collective-permute-done.2.refs_2_, ...), custom_call_target="tpu_custom_call" | custom-call | flops 1000000000 | bytes 16777216 | tf_op jit(solution)/shard_map/pallas_call | solution.py:356
  64.0 4.8 %collective-permute-done.5.refs_2_.refs_3_ = f32[1040,128]{1,0:T(8,128)S(1)} collective-permute-done((f32[1040,128]{1,0:T(8,128)S(1)}, f32[1040,128]{1,0:T(8,128)S(1)}, u32[]{:S(2)}, u32[]{:S(2)}) %collective-permute-start.5) | collective-permute-done | bytes 532512 | tf_op jit(solution)/shard_map/ppermute | solution.py:47
  68.8 0.1 shard_map.75
  68.9 5.6 %collective-permute-start.6 = (f32[2080,128]{1,0:T(8,128)S(1)}, f32[2080,128]{1,0:T(8,128)S(1)}, u32[]{:S(2)}, u32[]{:S(2)}) collective-permute-start(f32[2080,128]{1,0:T(8,128)S(1)} %shard_map.75), channel_id=1, source_target_pairs={{0,4},{1,29},{4,0},{5,9},{8,12},{9,5},{12,8},{13,17},{16,20},{17,1... | collective-permute-start | bytes 3194888 | tf_op jit(solution)/shard_map/ppermute | solution.py:47
  74.5 0.0 collective-permute-done.7.refs_7_
  74.5 1.9 %collective-permute-start.9 = (f32[2328,128]{1,0:T(8,128)S(1)}, f32[2328,128]{1,0:T(8,128)S(1)}, u32[]{:S(2)}, u32[]{:S(2)}) collective-permute-start(f32[2328,128]{1,0:T(8,128)S(1)} %collective-permute-done.7.refs_7_), channel_id=1, source_target_pairs={{0,384},{1,129},{128,256},{129,1},{256,128},{257,385},{384,0},{385... | collective-permute-start | bytes 3575816 | tf_op jit(solution)/shard_map/ppermute | solution.py:33
  76.4 5.2 %shard_map.76 = (bf16[512,1024]{1,0:T(8,128)(2,1)S(1)}, bf16[512,1024]{1,0:T(8,128)(2,1)S(1)}, f32[512,1024]{1,0:T(8,128)S(1)}) custom-call(s32[149]{0:T(256)S(1)} %concatenate.15.refs_0_, f32[520,128]{1,0:T(8,128)S(1)} %copy-done.1, f32[520,128]{1,0:T(8,128)S(1)} %collective-permute-done.1.refs_1_.refs_2_, ...), custom_call_target="tpu_custom_call" | custom-call | flops 2013265920 | bytes 16777216 | tf_op jit(solution)/shard_map/pallas_call | solution.py:369
  81.7 0.0 collective-permute-done.8.refs_8_
  81.7 5.4 %collective-permute-done.6.refs_1_ = f32[2080,128]{1,0:T(8,128)S(1)} collective-permute-done((f32[2080,128]{1,0:T(8,128)S(1)}, f32[2080,128]{1,0:T(8,128)S(1)}, u32[]{:S(2)}, u32[]{:S(2)}) %collective-permute-start.6) | collective-permute-done | bytes 1064992 | tf_op jit(solution)/shard_map/ppermute | solution.py:47
  87.1 9.2 %shard_map.77 = (bf16[512,1408]{1,0:T(8,128)(2,1)S(1)}, bf16[512,1408]{1,0:T(8,128)(2,1)S(1)}, f32[512,1024]{1,0:T(8,128)S(1)}) custom-call(s32[149]{0:T(256)S(1)} %concatenate.15.refs_0_, f32[2080,128]{1,0:T(8,128)S(1)} %collective-permute-done.6.refs_1_, bf16[512,1024]{1,0:T(8,128)(2,1)S(1)} %get-tuple-element.49.refs_2_, ...), custom_call_target="tpu_custom_call" | custom-call | flops 3221225472 | bytes 16777216 | tf_op jit(solution)/shard_map/pallas_call | solution.py:383
  96.3 0.0 collective-permute-done.9.refs_3_
  96.3 2.9 %shard_map.78 = (f32[256,1024]{1,0:T(8,128)S(1)}, f32[128,1024]{1,0:T(8,128)S(1)}, f32[128,1024]{1,0:T(8,128)S(1)}) custom-call(bf16[512,1408]{1,0:T(8,128)(2,1)S(1)} %get-tuple-element.55.refs_0_, bf16[512,1408]{1,0:T(8,128)(2,1)S(1)} %get-tuple-element.56.refs_1_, f32[512,1024]{1,0:T(8,128)S(1)} %get-tuple-element.57.refs_2_, ...), custom_call_target="tpu_custom_call" | custom-call | flops 1207959552 | bytes 16777216 | tf_op jit(solution)/shard_map/pallas_call | solution.py:401
  99.2 2.4 %collective-permute-start.10 = (f32[256,1024]{1,0:T(8,128)S(1)}, f32[256,1024]{1,0:T(8,128)S(1)}, u32[]{:S(2)}, u32[]{:S(2)}) collective-permute-start(f32[256,1024]{1,0:T(8,128)S(1)} %get-tuple-element.59), channel_id=1, source_target_pairs={{0,1},{1,0},{2,3},{3,2},{4,5},{5,4},{6,7},{7,6},{8,9},{9,8},{10,11... | collective-permute-start | bytes 3145736 | tf_op jit(solution)/shard_map/ppermute | solution.py:68
  101.7 2.3 %collective-permute-done.10 = f32[256,1024]{1,0:T(8,128)S(1)} collective-permute-done((f32[256,1024]{1,0:T(8,128)S(1)}, f32[256,1024]{1,0:T(8,128)S(1)}, u32[]{:S(2)}, u32[]{:S(2)}) %collective-permute-start.10) | collective-permute-done | bytes 1048608 | tf_op jit(solution)/shard_map/ppermute | solution.py:68
  103.9 0.1 slice_add_fusion
  104.0 6.7 %collective-permute-start.11 = (f32[128,1024]{1,0:T(8,128)S(1)}, f32[128,1024]{1,0:T(8,128)S(1)}, u32[]{:S(2)}, u32[]{:S(2)}) collective-permute-start(f32[128,1024]{1,0:T(8,128)S(1)} %slice_add_fusion), channel_id=1, source_target_pairs={{0,2},{2,0},{1,3},{3,1},{4,6},{6,4},{5,7},{7,5},{8,10},{10,8},{9,1... | collective-permute-start | bytes 1572872 | tf_op jit(solution)/shard_map/ppermute | solution.py:68
  110.7 12.0 %collective-permute-done.11 = f32[128,1024]{1,0:T(8,128)S(1)} collective-permute-done((f32[128,1024]{1,0:T(8,128)S(1)}, f32[128,1024]{1,0:T(8,128)S(1)}, u32[]{:S(2)}, u32[]{:S(2)}) %collective-permute-start.11) | collective-permute-done | bytes 524320 | tf_op jit(solution)/shard_map/ppermute | solution.py:68
  122.7 0.9 fusion
  (1 shorter events, 0.0 us)
Async XLA Ops:
  0.0 19.6 %copy-start.2 = (s32[144]{0:T(256)S(1)}, s32[144]{0:T(256)}, u32[]{:S(2)}) copy-start(s32[144]{0:T(256)} %constant.22.clone) | copy-start | bytes 1732
  2.9 24.7 %copy-start = (f32[776,128]{1,0:T(8,128)S(1)}, f32[776,128]{1,0:T(8,128)}, u32[]{:S(2)}) copy-start(f32[776,128]{1,0:T(8,128)} %get-tuple-element.33.refs_0_) | copy-start | bytes 1191940
  2.9 18.8 %collective-permute-start = (f32[776,128]{1,0:T(8,128)}, f32[776,128]{1,0:T(8,128)S(1)}, u32[]{:S(2)}, u32[]{:S(2)}) collective-permute-start(f32[776,128]{1,0:T(8,128)} %get-tuple-element.33.refs_0_), channel_id=1, source_target_pairs={{0,32},{1,97},{32,0},{33,65},{64,96},{65,33},{96,64},{97,1},{2,34}... | collective-permute-start | bytes 1191944 | tf_op jit(solution)/shard_map/ppermute | solution.py:33
  14.5 13.0 %collective-permute-start.2 = (f32[776,128]{1,0:T(8,128)}, f32[776,128]{1,0:T(8,128)S(1)}, u32[]{:S(2)}, u32[]{:S(2)}) collective-permute-start(f32[776,128]{1,0:T(8,128)} %get-tuple-element.33.refs_0_), channel_id=1, source_target_pairs={{0,128},{1,385},{128,0},{129,257},{256,384},{257,129},{384,256},{3... | collective-permute-start | bytes 1191944 | tf_op jit(solution)/shard_map/ppermute | solution.py:33
  22.8 8.0 %copy-start.1 = (f32[520,128]{1,0:T(8,128)S(1)}, f32[520,128]{1,0:T(8,128)}, u32[]{:S(2)}) copy-start(f32[520,128]{1,0:T(8,128)} %get-tuple-element.36.refs_0_.refs_1_) | copy-start | bytes 798724
  22.8 20.9 %collective-permute-start.4 = (f32[1560,128]{1,0:T(8,128)S(1)}, f32[1560,128]{1,0:T(8,128)S(1)}, u32[]{:S(2)}, u32[]{:S(2)}) collective-permute-start(f32[1560,128]{1,0:T(8,128)S(1)} %pad_maximum_fusion.1), channel_id=1, source_target_pairs={{0,96},{1,33},{32,64},{33,1},{64,32},{65,97},{96,0},{97,65},{2,98}... | collective-permute-start | bytes 2396168 | tf_op jit(solution)/shard_map/ppermute | solution.py:33
  27.7 13.1 %collective-permute-start.3 = (f32[1552,128]{1,0:T(8,128)S(1)}, f32[1552,128]{1,0:T(8,128)S(1)}, u32[]{:S(2)}, u32[]{:S(2)}) collective-permute-start(f32[1552,128]{1,0:T(8,128)S(1)} %pad_maximum_fusion.2), channel_id=1, source_target_pairs={{0,384},{1,129},{128,256},{129,1},{256,128},{257,385},{384,0},{385... | collective-permute-start | bytes 2383880 | tf_op jit(solution)/shard_map/ppermute | solution.py:33
  30.8 21.5 %collective-permute-start.1 = (f32[520,128]{1,0:T(8,128)S(1)}, f32[520,128]{1,0:T(8,128)S(1)}, u32[]{:S(2)}, u32[]{:S(2)}) collective-permute-start(f32[520,128]{1,0:T(8,128)S(1)} %copy-done.1), channel_id=1, source_target_pairs={{0,16},{1,17},{4,20},{5,21},{8,24},{9,25},{12,28},{13,29},{16,0},{... | collective-permute-start | bytes 798728 | tf_op jit(solution)/shard_map/ppermute | solution.py:47
  43.8 30.7 %collective-permute-start.7 = (f32[2328,128]{1,0:T(8,128)S(1)}, f32[2328,128]{1,0:T(8,128)S(1)}, u32[]{:S(2)}, u32[]{:S(2)}) collective-permute-start(f32[2328,128]{1,0:T(8,128)S(1)} %pad_maximum_fusion), channel_id=1, source_target_pairs={{0,128},{1,385},{128,0},{129,257},{256,384},{257,129},{384,256},{3... | collective-permute-start | bytes 3575816 | tf_op jit(solution)/shard_map/ppermute | solution.py:33
  52.3 16.5 %collective-permute-start.5 = (f32[1040,128]{1,0:T(8,128)S(1)}, f32[1040,128]{1,0:T(8,128)S(1)}, u32[]{:S(2)}, u32[]{:S(2)}) collective-permute-start(f32[1040,128]{1,0:T(8,128)S(1)} %pad_maximum_fusion.3), channel_id=1, source_target_pairs={{0,8},{1,25},{4,28},{5,13},{8,0},{9,17},{12,20},{13,5},{16,24},{17... | collective-permute-start | bytes 1597448 | tf_op jit(solution)/shard_map/ppermute | solution.py:47
  58.2 23.5 %collective-permute-start.8 = (f32[2328,128]{1,0:T(8,128)S(1)}, f32[2328,128]{1,0:T(8,128)S(1)}, u32[]{:S(2)}, u32[]{:S(2)}) collective-permute-start(f32[2328,128]{1,0:T(8,128)S(1)} %pad_maximum_fusion), channel_id=1, source_target_pairs={{0,384},{1,129},{128,256},{129,1},{256,128},{257,385},{384,0},{385... | collective-permute-start | bytes 3575816 | tf_op jit(solution)/shard_map/ppermute | solution.py:33
  68.9 18.2 %collective-permute-start.6 = (f32[2080,128]{1,0:T(8,128)S(1)}, f32[2080,128]{1,0:T(8,128)S(1)}, u32[]{:S(2)}, u32[]{:S(2)}) collective-permute-start(f32[2080,128]{1,0:T(8,128)S(1)} %shard_map.75), channel_id=1, source_target_pairs={{0,4},{1,29},{4,0},{5,9},{8,12},{9,5},{12,8},{13,17},{16,20},{17,1... | collective-permute-start | bytes 3194888 | tf_op jit(solution)/shard_map/ppermute | solution.py:47
  74.5 21.8 %collective-permute-start.9 = (f32[2328,128]{1,0:T(8,128)S(1)}, f32[2328,128]{1,0:T(8,128)S(1)}, u32[]{:S(2)}, u32[]{:S(2)}) collective-permute-start(f32[2328,128]{1,0:T(8,128)S(1)} %collective-permute-done.7.refs_7_), channel_id=1, source_target_pairs={{0,384},{1,129},{128,256},{129,1},{256,128},{257,385},{384,0},{385... | collective-permute-start | bytes 3575816 | tf_op jit(solution)/shard_map/ppermute | solution.py:33
  99.2 4.7 %collective-permute-start.10 = (f32[256,1024]{1,0:T(8,128)S(1)}, f32[256,1024]{1,0:T(8,128)S(1)}, u32[]{:S(2)}, u32[]{:S(2)}) collective-permute-start(f32[256,1024]{1,0:T(8,128)S(1)} %get-tuple-element.59), channel_id=1, source_target_pairs={{0,1},{1,0},{2,3},{3,2},{4,5},{5,4},{6,7},{7,6},{8,9},{9,8},{10,11... | collective-permute-start | bytes 3145736 | tf_op jit(solution)/shard_map/ppermute | solution.py:68
  104.0 18.7 %collective-permute-start.11 = (f32[128,1024]{1,0:T(8,128)S(1)}, f32[128,1024]{1,0:T(8,128)S(1)}, u32[]{:S(2)}, u32[]{:S(2)}) collective-permute-start(f32[128,1024]{1,0:T(8,128)S(1)} %slice_add_fusion), channel_id=1, source_target_pairs={{0,2},{2,0},{1,3},{3,1},{4,6},{6,4},{5,7},{7,5},{8,10},{10,8},{9,1... | collective-permute-start | bytes 1572872 | tf_op jit(solution)/shard_map/ppermute | solution.py:68
